TPU v7x, 32 devices: a whole 2x2x4 slice. The times are simulated.
32 devices in a mesh: wide: 16 (over z, y, x), freq: 2 (over core).
Axes of the slice: x: 2, y: 2, z: 4, core: 2. Of those that a mesh axis runs over, the one named last changes fastest.
Arguments:
- wave: bfloat16 [2, 2, 1024, 1024], P(None, 'freq', 'wide'), may hold values from -6 to 6
- filters: bfloat16 [2, 2, 2, 3, 81], P(None, None, 'freq'), may hold values from -0.6640625 to 0.6640625
- vel_bins: int32 [2, 2, 3, 1024], replicated, may hold values from 0 to 2
- blend_levels: int32 [2, 2, 3, 1024], replicated, may hold values from 1 to 16
- aperture: int32 [2, 64, 64], replicated, may hold values 0 or 1
Outputs:
- image_shallow: float32 [1024, 1024], P('wide', 'freq')
- image_deep: float32 [1024, 1024], P('wide', 'freq')
All inputs are finite; a program needn't handle non-finite values.
Results may differ from a plain program's by a relative error of at most 0.017.
Values may be sent and summed in bfloat16 or wider, within the bound.
No kernel may reach another device: no remote copies, remote signals or barrier semaphores. Data moves between devices by JAX's collectives and lax.ppermute only.
A program may use at most 64 MiB of HBM per device.

v0:
```python
import jax
import jax.numpy as jnp
from jax import lax
from jax.sharding import PartitionSpec as P

SIDE = 32
TAPS = 9
VBINS = 3
BLK = 16


def blend_table(bin_ids, levels):
    weights = levels.astype(jnp.float32)
    onehot = (bin_ids[:, None, :] == jnp.arange(VBINS, dtype=jnp.int32)[None, :, None]).astype(
        jnp.float32
    )
    return jnp.sum(onehot * weights[:, None, :], axis=0) / jnp.sum(weights, axis=0)[None, :]


def banded_bins(field_item, filt_real, filt_imag, table):
    rows_tile = max(1, 128 // SIDE)
    window = rows_tile + TAPS - 1
    tile_count = SIDE // rows_tile
    half_taps = TAPS // 2
    tap_range = jnp.arange(TAPS)[None, None, :]
    row_pick = (
        jnp.arange(window)[:, None, None] - jnp.arange(rows_tile)[None, :, None] == tap_range
    ).astype(jnp.float32)
    col_pick = (
        jnp.arange(SIDE)[:, None, None] - jnp.arange(SIDE)[None, :, None] + half_taps == tap_range
    ).astype(jnp.float32)

    def spread(filt_part):
        taps_grid = filt_part.reshape(VBINS, TAPS, TAPS).astype(jnp.float32)
        banded = jnp.einsum("iya,jxb,kab->kijyx", row_pick, col_pick, taps_grid)
        return banded.reshape(VBINS, window * SIDE, rows_tile * SIDE)

    band_real = spread(filt_real)
    band_imag = spread(filt_imag)
    upper_half = jnp.stack([band_real, band_imag], 1)
    lower_half = jnp.stack([-band_imag, band_real], 1)
    matrix = jnp.stack([upper_half, lower_half], 0)
    matrix = (
        jnp.transpose(matrix, (0, 3, 1, 2, 4))
        .reshape(2 * window * SIDE, VBINS * 2 * rows_tile * SIDE)
        .astype(jnp.bfloat16)
    )
    batch_rows = field_item.shape[1]
    grid_field = field_item.reshape(2, batch_rows, SIDE, SIDE)
    padded = jnp.pad(grid_field, ((0, 0), (0, 0), (half_taps, half_taps), (0, 0)))
    pieces = jnp.stack(
        [
            padded[:, :, tile_index * rows_tile : tile_index * rows_tile + window, :]
            for tile_index in range(tile_count)
        ],
        2,
    )
    pieces = jnp.transpose(pieces, (1, 2, 0, 3, 4)).reshape(
        batch_rows, tile_count, 2 * window * SIDE
    )
    product = jnp.dot(pieces, matrix, preferred_element_type=jnp.float32)
    product = product.reshape(batch_rows, tile_count, VBINS, 2, rows_tile * SIDE)
    weights = table.reshape(VBINS, tile_count, rows_tile * SIDE)
    return jnp.einsum("bnkct,knt->cbnt", product, weights).reshape(2, batch_rows, SIDE * SIDE)


def extrapolate(field, filters_now, table):
    blended = banded_bins(field[:, 0], filters_now[0, 0], filters_now[1, 0], table)
    members = [blended.astype(jnp.bfloat16)]
    return jnp.stack(members, 1)


def local_aperture(blocks, offset, row_count):
    picked = lax.dynamic_slice_in_dim(blocks, offset // BLK, row_count // BLK, 0)
    return jnp.repeat(jnp.repeat(picked, BLK, axis=0), BLK, axis=1)


def body(wave, filters, vel_bins, blend_levels, aperture):
    source_rows = wave.shape[2]
    offset = lax.axis_index("wide") * source_rows
    first = extrapolate(wave, filters[0], blend_table(vel_bins[0, 0], blend_levels[0, 0]))
    moved = lax.all_to_all(first, "wide", split_axis=3, concat_axis=2, tiled=True)
    second = extrapolate(
        jnp.swapaxes(moved, 2, 3), filters[0], blend_table(vel_bins[0, 1], blend_levels[0, 1])
    )
    keep_mask = local_aperture(aperture[0].T, offset, source_rows)
    shallow_field = jnp.where(keep_mask[None, None] > 0, second, jnp.zeros_like(second))
    shallow_part = jnp.sum(shallow_field[0].astype(jnp.float32), axis=0)
    image_shallow = lax.psum_scatter(
        shallow_part.astype(jnp.bfloat16), "freq", scatter_dimension=1, tiled=True
    ).astype(jnp.float32)
    third = extrapolate(shallow_field, filters[1], blend_table(vel_bins[1, 1], blend_levels[1, 1]))
    returned = lax.all_to_all(third, "wide", split_axis=3, concat_axis=2, tiled=True)
    fourth = extrapolate(
        jnp.swapaxes(returned, 2, 3), filters[1], blend_table(vel_bins[1, 0], blend_levels[1, 0])
    )
    keep_mask = local_aperture(aperture[1], offset, source_rows)
    deep_field = jnp.where(keep_mask[None, None] > 0, fourth, jnp.zeros_like(fourth))
    deep_part = jnp.sum(deep_field[0].astype(jnp.float32), axis=0)
    image_deep = lax.psum_scatter(
        deep_part.astype(jnp.bfloat16), "freq", scatter_dimension=1, tiled=True
    ).astype(jnp.float32)
    return (image_shallow, image_deep)


def solution(mesh):
    return jax.shard_map(
        body,
        mesh=mesh,
        in_specs=(P(None, "freq", "wide", None), P(None, None, "freq", None, None), P(), P(), P()),
        out_specs=(P("wide", "freq"), P("wide", "freq")),
        check_vma=False,
    )
```

profile of v0, /device:TPU:0, one launch (start us, length us, event | category | flops | bytes accessed | tf_op | source)
XLA Modules:
  0.0 107.2 jit_solution(17525005623977842383)
XLA Ops:
  7.2 1.5 %slice_convert_fusion.1 = (f32[1,1,3,1024]{3,1,2,0:T(1,128)S(1)}, f32[1,1,3,1024]{3,1,2,0:T(1,128)S(1)}, f32[1,1,3,1024]{3,1,2,0:T(1,128)S(1)}, f32[1,1,3,1024]{3,1,2,0:T(1,128)}) fusion(s32[2,2,3,1024]{3,1,2,0:T(2,128)} %param.8), kind=kLoop, calls=%fused_computation.150 | loop fusion | flops 12288 | bytes 98304 | tf_op jit(solution)/shard_map/convert_element_type | solution.py:13
  8.7 1.5 %fusion.90 = (f32[1024]{0:T(1024)S(1)}, f32[1024]{0:T(1024)}, f32[1024]{0:T(1024)}, f32[1024]{0:T(1024)}) fusion(s32[2,2,3,1024]{3,1,2,0:T(2,128)} %param.8), kind=kLoop, calls=%fused_computation.162 | loop fusion | flops 20480 | bytes 65536 | tf_op jit(solution)/shard_map/reduce_sum | solution.py:17
  10.1 1.2 %copy.76 = bf16[2,1,64,1024]{2,3,0,1:T(8,128)(2,1)S(1)} copy(bf16[2,1,64,1024]{3,2,1,0:T(8,128)(2,1)} %param.5) | data formatting | bytes 524288 | tf_op args[0]
  14.1 1.9 %copy.78 = bf16[3,12,32,4,32]{4,3,2,1,0:T(4,128)(2,1)} copy(bf16[3,12,32,4,32]{4,1,2,3,0:T(8,128)(2,1)S(1)} %get-tuple-element.12) | data formatting | bytes 589824 | tf_op jit(solution)/shard_map/convert.15
  16.0 2.0 %reshape.270 = bf16[3,1,384,128]{3,2,0,1:T(8,128)(2,1)S(1)} reshape(bf16[3,12,32,4,32]{4,3,2,1,0:T(4,128)(2,1)} %copy.78) | data formatting | bytes 589824 | tf_op jit(solution)/shard_map/convert.15
  18.9 1.9 %copy.77 = bf16[3,12,32,4,32]{4,3,2,1,0:T(4,128)(2,1)} copy(bf16[3,12,32,4,32]{4,1,2,3,0:T(8,128)(2,1)S(1)} %fusion.2) | data formatting | bytes 589824 | tf_op jit(solution)/shard_map/convert.14
  20.8 2.0 %reshape.269 = bf16[3,1,384,128]{3,2,0,1:T(8,128)(2,1)S(1)} reshape(bf16[3,12,32,4,32]{4,3,2,1,0:T(4,128)(2,1)} %copy.77) | data formatting | bytes 589824 | tf_op jit(solution)/shard_map/convert.14
  22.8 0.9 copy.79
  24.6 1.2 %copy.80 = bf16[2,384,3,2,128]{4,3,2,1,0:T(2,128)(2,1)S(1)} copy(bf16[2,384,3,2,128]{4,1,2,3,0:T(8,128)(2,1)S(1)} %maximum_bitcast_fusion) | data formatting | bytes 2359296 | tf_op jit(solution)/shard_map/convert_element_type | solution.py:46
  28.0 2.8 %multiply_reduce_fusion.3 = bf16[8,128,64,2]{1,2,3,0:T(8,128)(2,1)S(1)} fusion(bf16[64,8,768,1,1]{0,2,4,3,1:T(8,128)(2,1)} %bitcast.440, bf16[3,2,128,768,1]{3,2,1,0,4:T(8,128)(2,1)S(1)} %bitcast.426, f32[8,128,3]{1,2,0:T(4,128)S(1)} %copy.166), kind=kOutput, calls=%fused_computation.9 | convolution fusion | flops 604635136 | bytes 2240512 | tf_op jit(solution)/shard_map/dot_general | solution.py:61
  31.3 1.1 %reshape.309 = bf16[16,2,4096]{2,1,0:T(2,128)(2,1)} reshape(bf16[1024,1,2,64]{3,2,1,0:T(2,128)(2,1)S(1)} %bitcast.416) | data formatting | bytes 524288
  32.4 8.4 %all-to-all-start = ((bf16[16,2,4096]{2,1,0:T(2,128)(2,1)}), bf16[16,2,4096]{2,1,0:T(2,128)(2,1)}, u32[]{:S(2)}, u32[]{:S(2)}) async-start(bf16[16,2,4096]{2,1,0:T(2,128)(2,1)} %reshape.309), calls=%async_computation | async-start | bytes 524288 | tf_op jit(solution)/shard_map/all_to_all | solution.py:82
  42.3 1.9 %copy.91 = bf16[3,12,32,4,32]{4,3,2,1,0:T(4,128)(2,1)} copy(bf16[3,12,32,4,32]{4,1,2,3,0:T(8,128)(2,1)S(1)} %get-tuple-element.10) | data formatting | bytes 589824 | tf_op jit(solution)/shard_map/convert.7
  44.2 2.0 %reshape.273 = bf16[3,1,384,128]{3,2,0,1:T(8,128)(2,1)S(1)} reshape(bf16[3,12,32,4,32]{4,3,2,1,0:T(4,128)(2,1)} %copy.91) | data formatting | bytes 589824 | tf_op jit(solution)/shard_map/convert.7
  47.7 1.9 %copy.90 = bf16[3,12,32,4,32]{4,3,2,1,0:T(4,128)(2,1)} copy(bf16[3,12,32,4,32]{4,1,2,3,0:T(8,128)(2,1)S(1)} %fusion.3) | data formatting | bytes 589824 | tf_op jit(solution)/shard_map/convert.6
  49.6 2.0 %reshape.272 = bf16[3,1,384,128]{3,2,0,1:T(8,128)(2,1)S(1)} reshape(bf16[3,12,32,4,32]{4,3,2,1,0:T(4,128)(2,1)} %copy.90) | data formatting | bytes 589824 | tf_op jit(solution)/shard_map/convert.6
  51.7 0.9 copy.92
  54.4 1.2 %copy.93 = bf16[2,384,3,2,128]{4,3,2,1,0:T(2,128)(2,1)S(1)} copy(bf16[2,384,3,2,128]{4,1,2,3,0:T(8,128)(2,1)S(1)} %maximum_bitcast_fusion.1) | data formatting | bytes 2359296 | tf_op jit(solution)/shard_map/convert_element_type | solution.py:46
  56.2 1.4 %copy.94 = bf16[768,768]{1,0:T(8,128)(2,1)} copy(bf16[768,768]{0,1:T(8,128)(2,1)S(1)} %bitcast.413) | data formatting | bytes 2359296 | tf_op jit(solution)/shard_map/dot_general | solution.py:61
  57.8 1.3 %reshape.310 = bf16[1024,1,2,64]{3,2,1,0:T(2,128)(2,1)S(1)} reshape(bf16[16,2,4096]{2,1,0:T(2,128)(2,1)} %all-to-all-done) | data formatting | bytes 524288
  60.4 1.6 %copy.114 = bf16[64,8,768,1,1]{2,1,4,3,0:T(8,128)(2,1)} copy(bf16[64,8,768,1,1]{0,2,1,4,3:T(8,128)(2,1)S(1)} %bitcast.422) | data formatting | bytes 1572864 | tf_op jit(solution)/shard_map/reshape | solution.py:58
  62.0 2.0 %multiply_reduce_fusion.2 = bf16[8,128,64,2]{1,0,3,2:T(8,128)(2,1)S(1)} fusion(bf16[64,8,768,1,1]{2,1,4,3,0:T(8,128)(2,1)} %copy.114, bf16[3,2,128,768,1]{3,2,1,0,4:T(8,128)(2,1)S(1)} %bitcast.427, f32[8,128,3]{1,0,2:T(8,128)S(1)} %fusion.78), kind=kOutput, calls=%fused_computation.8 | convolution fusion | flops 604635136 | bytes 2240512 | tf_op jit(solution)/shard_map/dot_general | solution.py:61
  64.7 1.0 copy-done.2
  65.7 1.4 %multiply_reduce_fusion.1 = bf16[8,128,64,2]{1,2,3,0:T(8,128)(2,1)S(1)} fusion(bf16[64,8,768,1,1]{0,2,4,3,1:T(8,128)(2,1)S(1)} %bitcast.441, bf16[3,2,128,768,1]{3,2,1,0,4:T(8,128)(2,1)S(1)} %bitcast.428, f32[8,128,3]{1,2,0:T(4,128)S(1)} %copy.168), kind=kOutput, calls=%fused_computation.7 | convolution fusion | flops 604635136 | bytes 2240512 | tf_op jit(solution)/shard_map/dot_general | solution.py:61
  67.6 1.1 %reshape.311 = bf16[16,2,4096]{2,1,0:T(2,128)(2,1)} reshape(bf16[1024,1,2,64]{3,2,1,0:T(2,128)(2,1)S(1)} %bitcast.417) | data formatting | bytes 524288
  68.7 6.8 %all-to-all-start.1 = ((bf16[16,2,4096]{2,1,0:T(2,128)(2,1)}), bf16[16,2,4096]{2,1,0:T(2,128)(2,1)S(1)}, u32[]{:S(2)}, u32[]{:S(2)}) async-start(bf16[16,2,4096]{2,1,0:T(2,128)(2,1)} %reshape.311), calls=%async_computation.2 | async-start | bytes 524288 | tf_op jit(solution)/shard_map/all_to_all | solution.py:93
  77.8 7.0 %all-to-all-done.1 = bf16[16,2,4096]{2,1,0:T(2,128)(2,1)S(1)} async-done(((bf16[16,2,4096]{2,1,0:T(2,128)(2,1)}), bf16[16,2,4096]{2,1,0:T(2,128)(2,1)S(1)}, u32[]{:S(2)}, u32[]{:S(2)}) %all-to-all-start.1) | async-done | bytes 262176 | tf_op jit(solution)/shard_map/all_to_all | solution.py:93
  86.4 1.6 %copy.136 = bf16[64,8,768,1,1]{2,1,4,3,0:T(8,128)(2,1)} copy(bf16[64,8,768,1,1]{0,2,1,4,3:T(8,128)(2,1)S(1)} %bitcast.423) | data formatting | bytes 1572864 | tf_op jit(solution)/shard_map/reshape | solution.py:58
  88.1 2.0 %multiply_reduce_fusion = bf16[8,128,64,2]{1,0,3,2:T(8,128)(2,1)S(1)} fusion(bf16[64,8,768,1,1]{2,1,4,3,0:T(8,128)(2,1)} %copy.136, bf16[3,2,128,768,1]{3,2,1,0,4:T(8,128)(2,1)S(1)} %bitcast.429, f32[8,128,3]{1,0,2:T(8,128)S(1)} %fusion.76), kind=kOutput, calls=%fused_computation.6 | convolution fusion | flops 604635136 | bytes 2240512 | tf_op jit(solution)/shard_map/dot_general | solution.py:61
  90.9 1.5 %convert_element_type.178 = f32[64,512]{1,0:T(8,128)} convert(bf16[64,512]{1,0:T(8,128)(2,1)} %reduce-scatter.3.cloned.1.call-done) | non-fusion elementwise | flops 32768 | bytes 196608 | tf_op jit(solution)/shard_map/convert_element_type | solution.py:91
  92.4 6.5 %reduce-scatter.5.cloned.1.call-done = bf16[64,512]{1,0:T(8,128)(2,1)} async-done(((bf16[64,1024]{1,0:T(8,128)(2,1)}), bf16[64,512]{1,0:T(8,128)(2,1)}) %reduce-scatter.5.cloned.1.call-update) | async-done | bytes 65552 | tf_op jit(solution)/shard_map/reduce_scatter | solution.py:100
  98.9 1.5 %convert_element_type.192 = f32[64,512]{1,0:T(8,128)} convert(bf16[64,512]{1,0:T(8,128)(2,1)} %reduce-scatter.5.cloned.1.call-done) | non-fusion elementwise | flops 32768 | bytes 196608 | tf_op jit(solution)/shard_map/convert_element_type | solution.py:102
  (129 shorter events, 18.9 us)
Async XLA Ops:
  11.4 0.7 copy-start.12
  12.1 1.2 %copy-start.8 = (bf16[2,64,8,12,32]{1,4,3,0,2:T(8,128)(2,1)}, bf16[2,64,8,12,32]{1,4,3,0,2:T(8,128)(2,1)S(1)}, u32[]{:S(2)}) copy-start(bf16[2,64,8,12,32]{1,4,3,0,2:T(8,128)(2,1)S(1)} %fusion.15) | copy-start | bytes 2359300
  26.4 0.8 copy-start.7
  26.4 1.6 %copy-start.11 = (f32[1024]{0:T(1024)S(1)}, f32[1024]{0:T(1024)}, u32[]{:S(2)}) copy-start(f32[1024]{0:T(1024)} %get-tuple-element.4) | copy-start | bytes 12292
  27.2 3.7 %copy-start = (bf16[768,768]{1,0:T(8,128)(2,1)}, bf16[768,768]{1,0:T(8,128)(2,1)S(1)}, u32[]{:S(2)}) copy-start(bf16[768,768]{1,0:T(8,128)(2,1)S(1)} %copy.81) | copy-start | bytes 3538948
  30.9 9.9 %copy-start.3 = (s32[2,64,64]{2,1,0:T(8,128)S(1)}, s32[2,64,64]{2,1,0:T(8,128)}, u32[]{:S(2)}) copy-start(s32[2,64,64]{2,1,0:T(8,128)} %param.9) | copy-start | bytes 98308
  30.9 10.6 %copy-start.13 = (bf16[3,81]{1,0:T(4,128)(2,1)S(1)}, bf16[3,81]{1,0:T(4,128)(2,1)}, u32[]{:S(2)}) copy-start(bf16[3,81]{1,0:T(4,128)(2,1)} %get-tuple-element.6) | copy-start | bytes 1462
  32.4 25.4 %all-to-all-start = ((bf16[16,2,4096]{2,1,0:T(2,128)(2,1)}), bf16[16,2,4096]{2,1,0:T(2,128)(2,1)}, u32[]{:S(2)}, u32[]{:S(2)}) async-start(bf16[16,2,4096]{2,1,0:T(2,128)(2,1)} %reshape.309), calls=%async_computation | async-start | bytes 524288 | tf_op jit(solution)/shard_map/all_to_all | solution.py:82
  53.3 0.7 copy-start.4
  53.3 0.7 copy-start.5
  53.3 0.7 copy-start.6
  53.3 0.8 copy-start.10
  56.2 1.5 %copy-start.9 = (f32[1024]{0:T(1024)S(1)}, f32[1024]{0:T(1024)}, u32[]{:S(2)}) copy-start(f32[1024]{0:T(1024)} %get-tuple-element.5) | copy-start | bytes 12292
  60.3 1.6 %copy-start.1 = (bf16[768,768]{1,0:T(8,128)(2,1)S(1)}, bf16[768,768]{1,0:T(8,128)(2,1)}, u32[]{:S(2)}) copy-start(bf16[768,768]{1,0:T(8,128)(2,1)} %copy-done) | copy-start | bytes 3538948
  64.5 1.3 %copy-start.2 = (bf16[768,768]{1,0:T(8,128)(2,1)S(1)}, bf16[768,768]{1,0:T(8,128)(2,1)}, u32[]{:S(2)}) copy-start(bf16[768,768]{1,0:T(8,128)(2,1)} %copy.94) | copy-start | bytes 3538948
  68.7 16.1 %all-to-all-start.1 = ((bf16[16,2,4096]{2,1,0:T(2,128)(2,1)}), bf16[16,2,4096]{2,1,0:T(2,128)(2,1)S(1)}, u32[]{:S(2)}, u32[]{:S(2)}) async-start(bf16[16,2,4096]{2,1,0:T(2,128)(2,1)} %reshape.311), calls=%async_computation.2 | async-start | bytes 524288 | tf_op jit(solution)/shard_map/all_to_all | solution.py:93
  75.5 15.4 %reduce-scatter.3.cloned.1.call-start = ((), (), s32[]{:S(2)}) async-start(), calls=%async_computation.4 | async-start | bytes 196608 | tf_op jit(solution)/shard_map/reduce_scatter | solution.py:89
  77.7 21.1 %reduce-scatter.5.cloned.1.call-start = ((), (), s32[]{:S(2)}) async-start(), calls=%async_computation.5 | async-start | bytes 196608 | tf_op jit(solution)/shard_map/reduce_scatter | solution.py:100
Sparse Core Ops, SparseCore 0:
  79.1 8.7 reduce-scatter.2
  91.0 7.8 reduce-scatter.4
where the time goes:
time: 108 us; the launch traced here: 107 us
  local copies, waits for them, and re-layouts  43.6 us (40%)
  starting transfers between devices  15.3 us (14%)
  between operations  14.9 us (14%)
  waiting for transfers between devices  13.6 us (13%)
  matrix products  11.1 us (10%)
  other arithmetic  8.71 us (8%)
    another operation x12, local copies, waits for them, and re-layouts  18.8 us
    unnamed x70, local copies, waits for them, and re-layouts  9.53 us
    all_to_all x1, starting transfers between devices, body(): lax.all_to_all(first, 'wide', split_axis=3, concat_axis=2, tiled=True)  8.38 us
    dot_general x4, matrix products, banded_bins(): product = jnp.dot(pieces, matrix, preferred_element_type=jnp.float32)  8.18 us
    all_to_all x1, waiting for transfers between devices, body(): lax.all_to_all(third, 'wide', split_axis=3, concat_axis=2, tiled=True)  7.05 us
    all_to_all x1, starting transfers between devices, body(): lax.all_to_all(third, 'wide', split_axis=3, concat_axis=2, tiled=True)  6.82 us
    reduce_scatter x1, waiting for transfers between devices, body(): lax.psum_scatter(deep_part.astype(jnp.bfloat16), 'freq', scatter_dimensio...  6.46 us
    convert_element_type x4, local copies, waits for them, and re-layouts, banded_bins(): matrix = jnp.transpose(matrix, (0, 3, 1, 2, 4)).reshape(2 * window * SIDE...  3.61 us
  transfers between devices with their start and end apart: 4, of which 2 were waited for; matrix products, arithmetic and copies ran while one was open for 24% of the time, Pallas kernels for 0%

commit v1 on v0

v1 whole, which is shorter than its diff:
```python
import functools
import math

import jax
import jax.numpy as jnp
from jax import lax
from jax.experimental import pallas as pl
from jax.experimental.pallas import tpu as pltpu
from jax.sharding import PartitionSpec as P

LANES = 128
VMEM_LIMIT = 24 * 1024 * 1024


class Sizes:
    def __init__(self, mesh, wave_shape, filters_shape, aperture_shape):
        self.wide = mesh.shape["wide"]
        self.freq = mesh.shape["freq"]
        self.pos = wave_shape[-1]
        self.rows = wave_shape[-2]
        self.side = math.isqrt(self.pos)
        self.bins = filters_shape[-2]
        self.tap_count = filters_shape[-1]
        self.taps = math.isqrt(self.tap_count)
        self.half = self.taps // 2
        self.tile_rows = LANES // self.side
        self.tiles = self.pos // LANES
        self.halo = -(-self.half // self.tile_rows)
        self.window = (1 + 2 * self.halo) * LANES
        self.blocks = aperture_shape[-1]
        self.blk = self.pos // self.blocks


def fill_taps(z, filt_ref, step, rows_ref):
    rows_ref[...] = jnp.zeros_like(rows_ref)
    for part in range(2):
        rows_ref[part * z.bins : (part + 1) * z.bins, : z.tap_count] = filt_ref[step, part, 0].astype(
            jnp.float32
        )


def fill_table(z, bins_ref, levels_ref, step, side, table_ref):
    ids = bins_ref[step, side]
    weights = levels_ref[step, side].astype(jnp.float32)
    total = jnp.sum(weights, axis=0, keepdims=True)
    table_ref[...] = jnp.zeros_like(table_ref)
    for k in range(z.bins):
        hit = jnp.sum(jnp.where(ids == k, weights, 0.0), axis=0, keepdims=True)
        table_ref[k : k + 1, :] = hit / total


def tap_index(z, in_y, in_x, out_y, out_x):
    a = in_y - out_y + (z.half - z.halo * z.tile_rows)
    b = in_x - out_x + z.half
    valid = (a >= 0) & (a < z.taps) & (b >= 0) & (b < z.taps)
    return jnp.where(valid, a * z.taps + b, LANES - 1)


def spread(rows_ref, row, index):
    source = jnp.broadcast_to(rows_ref[row : row + 1, :], index.shape)
    return jnp.take_along_axis(source, index, axis=1, mode="promise_in_bounds")


def chunk_order(z, column):
    chunk, inside = column // (2 * z.rows), column % (2 * z.rows)
    return inside // z.rows, chunk * z.rows + inside % z.rows


def first_kernel(z, wave_ref, filt_ref, bins_ref, levels_ref, out_ref, taps_ref, table_ref, band_ref, lhs_ref):
    fill_taps(z, filt_ref, 0, taps_ref)
    fill_table(z, bins_ref, levels_ref, 0, 0, table_ref)
    lane = lax.broadcasted_iota(jnp.int32, (z.window, LANES), 1)
    row = lax.broadcasted_iota(jnp.int32, (z.window, LANES), 0)
    for v in range(2):
        part, point = chunk_order(z, lane + v * LANES)
        index = tap_index(z, row // z.side, row % z.side, point // z.side, point % z.side)
        for k in range(z.bins):
            real, imag = spread(taps_ref, k, index), spread(taps_ref, z.bins + k, index)
            columns = slice((2 * k + v) * LANES, (2 * k + v + 1) * LANES)
            band_ref[: z.window, columns] = jnp.where(part == 0, real, imag).astype(jnp.bfloat16)
            band_ref[z.window :, columns] = jnp.where(part == 0, -imag, real).astype(jnp.bfloat16)
    spans = 1 + 2 * z.halo
    for part in range(2):
        for tile in range(z.tiles):
            for span in range(spans):
                source = tile + span - z.halo
                place = (part * spans + span) * LANES
                if 0 <= source < z.tiles:
                    piece = wave_ref[part, :, source * LANES : (source + 1) * LANES]
                else:
                    piece = jnp.zeros((z.rows, LANES), jnp.bfloat16)
                lhs_ref[tile * z.rows : (tile + 1) * z.rows, place : place + LANES] = piece
    lane = lax.broadcasted_iota(jnp.int32, (8, LANES), 1)
    points = [chunk_order(z, lane + v * LANES)[1] for v in range(2)]
    products = [
        jnp.dot(
            lhs_ref[...],
            band_ref[:, 2 * k * LANES : 2 * (k + 1) * LANES],
            preferred_element_type=jnp.float32,
        )
        for k in range(z.bins)
    ]
    for tile in range(z.tiles):
        weights = table_ref[:, tile * LANES : (tile + 1) * LANES]
        weights = jnp.concatenate(
            [jnp.take_along_axis(weights, p, axis=1, mode="promise_in_bounds") for p in points], axis=1
        )
        total = 0.0
        for k in range(z.bins):
            total = total + products[k][tile * z.rows : (tile + 1) * z.rows] * weights[k : k + 1]
        total = total.astype(jnp.bfloat16)
        chunks = LANES // z.rows
        for c in range(chunks):
            out_ref[tile * chunks + c] = total[:, 2 * z.rows * c : 2 * z.rows * (c + 1)]


def fill_columns(z, rows_ref, band_ref):
    lane = lax.broadcasted_iota(jnp.int32, (LANES, LANES), 1)
    row = lax.broadcasted_iota(jnp.int32, (LANES, LANES), 0)
    for span in range(1 + 2 * z.halo):
        inner = lane + span * LANES
        index = tap_index(z, inner // z.side, inner % z.side, row // z.side, row % z.side)
        for k in range(z.bins):
            for part in range(2):
                place = part * z.window + span * LANES
                band_ref[k * LANES : (k + 1) * LANES, place : place + LANES] = spread(
                    rows_ref, part * z.bins + k, index
                ).astype(jnp.bfloat16)


def turned(z, block):
    return jnp.concatenate([-block[:, z.rows :], block[:, : z.rows]], axis=1)


def over_sources(z, band_ref, columns, straight_ref, turned_ref, tile):
    start = tile * LANES
    rhs = jnp.concatenate(
        [straight_ref[start : start + z.window, :], turned_ref[start : start + z.window, :]], axis=0
    )
    product = jnp.dot(band_ref[...], rhs, preferred_element_type=jnp.float32)
    total = 0.0
    for k in range(z.bins):
        total = total + product[k * LANES : (k + 1) * LANES] * columns[start : start + LANES, k : k + 1]
    return total.astype(jnp.bfloat16)


def split_sum(z, real_ref, send_ref, own_ref):
    me = lax.axis_index("freq")
    width = z.pos // z.freq

    def part(shift):
        start = lax.rem(me + shift, z.freq) * width
        return real_ref[:, pl.ds(pl.multiple_of(start, width), width)]

    own_ref[...] = part(0).astype(jnp.float32)
    for shift in range(1, z.freq):
        send_ref[shift - 1] = part(shift)


def middle_kernel(
    z,
    moved_ref,
    filt_ref,
    bins_ref,
    levels_ref,
    aperture_ref,
    out_ref,
    send_ref,
    own_ref,
    taps_ref,
    table_ref,
    band_ref,
    straight_ref,
    turned_ref,
    real_ref,
):
    pad = z.halo * LANES
    width = 2 * z.rows
    for ref in (straight_ref, turned_ref):
        ref[:pad, :] = jnp.zeros((pad, width), jnp.bfloat16)
        ref[pad + z.pos :, :] = jnp.zeros((pad, width), jnp.bfloat16)
    field = moved_ref[...].reshape(z.pos, width)
    straight_ref[pad : pad + z.pos, :] = field
    turned_ref[pad : pad + z.pos, :] = turned(z, field)
    offset = lax.axis_index("wide") * z.rows
    receiver = lax.broadcasted_iota(jnp.int32, (z.blocks, width), 1) % z.rows + offset
    pick = (receiver // z.blk == lax.broadcasted_iota(jnp.int32, (z.blocks, width), 0)).astype(jnp.float32)
    keep = jnp.dot(aperture_ref[0].astype(jnp.float32), pick, preferred_element_type=jnp.float32)

    fill_taps(z, filt_ref, 0, taps_ref)
    fill_columns(z, taps_ref, band_ref)
    fill_table(z, bins_ref, levels_ref, 0, 1, table_ref)
    columns = jnp.transpose(table_ref[...])
    shallow = []
    per_tile = LANES // z.blk
    for tile in range(z.tiles):
        second = over_sources(z, band_ref, columns, straight_ref, turned_ref, tile)
        mask = keep[tile * per_tile : (tile + 1) * per_tile]
        mask = jnp.broadcast_to(mask[:, None, :], (per_tile, z.blk, width)).reshape(LANES, width)
        shallow.append(jnp.where(mask > 0.5, second, jnp.zeros_like(second)))
    for tile in range(z.tiles):
        place = pad + tile * LANES
        straight_ref[place : place + LANES, :] = shallow[tile]
        turned_ref[place : place + LANES, :] = turned(z, shallow[tile])
        flipped = jnp.transpose(shallow[tile].astype(jnp.float32))
        real_ref[:, tile * LANES : (tile + 1) * LANES] = flipped[: z.rows].astype(jnp.bfloat16)
    split_sum(z, real_ref, send_ref, own_ref)

    fill_taps(z, filt_ref, 1, taps_ref)
    fill_columns(z, taps_ref, band_ref)
    fill_table(z, bins_ref, levels_ref, 1, 1, table_ref)
    columns = jnp.transpose(table_ref[...])
    chunks = LANES // z.rows
    for tile in range(z.tiles):
        third = over_sources(z, band_ref, columns, straight_ref, turned_ref, tile)
        out_ref[tile * chunks : (tile + 1) * chunks] = third.reshape(chunks, z.rows, width)


def last_kernel(
    z,
    field_ref,
    filt_ref,
    bins_ref,
    levels_ref,
    aperture_ref,
    send_ref,
    own_ref,
    taps_ref,
    table_ref,
    band_ref,
    lhs_ref,
    real_ref,
):
    fill_taps(z, filt_ref, 1, taps_ref)
    fill_table(z, bins_ref, levels_ref, 1, 0, table_ref)
    lane = lax.broadcasted_iota(jnp.int32, (z.rows, LANES), 1)
    row = lax.broadcasted_iota(jnp.int32, (z.rows, LANES), 0)
    for block in range(2 * z.window // z.rows):
        part, start = block % 2, block // 2 * z.rows
        inner = row + start
        index = tap_index(z, inner // z.side, inner % z.side, lane // z.side, lane % z.side)
        for k in range(z.bins):
            taps = spread(taps_ref, part * z.bins + k, index)
            taps = taps if part == 0 else -taps
            band_ref[block * z.rows : (block + 1) * z.rows, k * LANES : (k + 1) * LANES] = taps.astype(
                jnp.bfloat16
            )
    per_tile = LANES // z.rows
    width = 2 * z.rows
    for tile in range(z.tiles):
        for place in range((1 + 2 * z.halo) * per_tile):
            source = (tile - z.halo) * per_tile + place
            if 0 <= source < z.wide:
                piece = field_ref[source]
            else:
                piece = jnp.zeros((z.rows, width), jnp.bfloat16)
            lhs_ref[tile * z.rows : (tile + 1) * z.rows, place * width : (place + 1) * width] = piece
    offset = lax.axis_index("wide") * z.rows
    source = lax.broadcasted_iota(jnp.int32, (z.rows, z.blocks), 0) + offset
    pick = (source // z.blk == lax.broadcasted_iota(jnp.int32, (z.rows, z.blocks), 1)).astype(jnp.float32)
    mine = jnp.dot(pick, aperture_ref[1].astype(jnp.float32), preferred_element_type=jnp.float32)
    receiver = lax.broadcasted_iota(jnp.int32, (z.blocks, z.pos), 1)
    stretch = (receiver // z.blk == lax.broadcasted_iota(jnp.int32, (z.blocks, z.pos), 0)).astype(jnp.float32)
    keep = jnp.dot(mine, stretch, preferred_element_type=jnp.float32)
    product = jnp.dot(lhs_ref[...], band_ref[...], preferred_element_type=jnp.float32)
    for tile in range(z.tiles):
        columns = slice(tile * LANES, (tile + 1) * LANES)
        total = 0.0
        for k in range(z.bins):
            part = product[tile * z.rows : (tile + 1) * z.rows, k * LANES : (k + 1) * LANES]
            total = total + part * table_ref[k : k + 1, columns]
        real_ref[:, columns] = jnp.where(keep[:, columns] > 0.5, total, 0.0).astype(jnp.bfloat16)
    split_sum(z, real_ref, send_ref, own_ref)


def call(kernel, operands, outs, scratch, flops, name):
    spec = pl.BlockSpec(memory_space=pltpu.VMEM)
    return pl.pallas_call(
        kernel,
        out_shape=outs,
        in_specs=[spec] * len(operands),
        out_specs=jax.tree.map(lambda _: spec, outs),
        scratch_shapes=[pltpu.VMEM(shape, dtype) for shape, dtype in scratch],
        compiler_params=pltpu.CompilerParams(vmem_limit_bytes=VMEM_LIMIT),
        cost_estimate=pl.CostEstimate(flops=flops, bytes_accessed=1 << 20, transcendentals=0),
        name=name,
    )(*operands)


def freq_sum(z, send, own):
    total = own
    for shift in range(1, z.freq):
        pairs = [(source, (source + shift) % z.freq) for source in range(z.freq)]
        total = total + lax.ppermute(send[shift - 1], "freq", pairs).astype(jnp.float32)
    return total


def body(mesh, wave, filters, vel_bins, blend_levels, aperture):
    z = Sizes(mesh, wave.shape, filters.shape, aperture.shape)
    bf16, f32 = jnp.bfloat16, jnp.float32
    chunks = jax.ShapeDtypeStruct((z.wide, z.rows, 2 * z.rows), bf16)
    width = z.pos // z.freq
    parts = [
        jax.ShapeDtypeStruct((z.freq - 1, z.rows, width), bf16),
        jax.ShapeDtypeStruct((z.rows, width), f32),
    ]
    small = [((8, LANES), f32), ((8, z.pos), f32)]
    dense = 2 * 2 * z.window * z.bins * z.pos * z.rows
    first = call(
        functools.partial(first_kernel, z),
        (wave[:, 0], filters, vel_bins, blend_levels),
        chunks,
        small
        + [
            ((2 * z.window, 2 * z.bins * LANES), bf16),
            ((z.tiles * z.rows, 2 * z.window), bf16),
        ],
        2 * dense,
        "first",
    )
    moved = lax.all_to_all(first, "wide", 0, 0, tiled=True)
    padded = z.pos + 2 * z.halo * LANES
    third, send, own = call(
        functools.partial(middle_kernel, z),
        (moved, filters, vel_bins, blend_levels, aperture),
        [chunks] + parts,
        small
        + [
            ((z.bins * LANES, 2 * z.window), bf16),
            ((padded, 2 * z.rows), bf16),
            ((padded, 2 * z.rows), bf16),
            ((z.rows, z.pos), bf16),
        ],
        4 * dense,
        "middle",
    )
    returned = lax.all_to_all(third, "wide", 0, 0, tiled=True)
    image_shallow = freq_sum(z, send, own)
    send, own = call(
        functools.partial(last_kernel, z),
        (returned, filters, vel_bins, blend_levels, aperture),
        parts,
        small
        + [
            ((2 * z.window, z.bins * LANES), bf16),
            ((z.tiles * z.rows, 2 * z.window), bf16),
            ((z.rows, z.pos), bf16),
        ],
        dense,
        "last",
    )
    image_deep = freq_sum(z, send, own)
    return image_shallow, image_deep


def solution(mesh):
    return jax.shard_map(
        functools.partial(body, mesh),
        mesh=mesh,
        in_specs=(P(None, "freq", "wide", None), P(None, None, "freq", None, None), P(), P(), P()),
        out_specs=(P("wide", "freq"), P("wide", "freq")),
        check_vma=False,
    )
```

time: 108 us -> 43.6 us (0.40)
  local copies, waits for them, and re-layouts: 43.6 us -> 2.51 us
  blocking collectives: 0 us -> 18.1 us
  between operations: 14.9 us -> 0.71 us
  starting transfers between devices: 15.3 us -> 3.69 us
  matrix products: 11.1 us -> 0 us
  other arithmetic: 8.71 us -> 1.35 us
  Pallas kernels: 0 us -> 7.2 us
  waiting for transfers between devices: 13.6 us -> 9.69 us
    another operation x20 -> x0, local copies, waits for them, and re-layouts: 20 us -> none
    all_to_all x0 -> x1, blocking collectives: none -> 18.1 us  [body(): moved = lax.all_to_all(first, 'wide', 0, 0, tiled=True)]
    all_to_all x2 -> x1, starting transfers between devices: 15.2 us -> 3.55 us  [body(): returned = lax.all_to_all(third, 'wide', 0, 0, tiled=True)]
    dot_general x8 -> x0, matrix products: 11.1 us -> none  [the longest x4 8.18 us: banded_bins(): product = jnp.dot(pieces, matrix, preferred_element_type=jnp.float32)]
    pallas_call x0 -> x3, Pallas kernels: none -> 7.2 us  [call(): pl.pallas_call(kernel, out_shape=outs, in_specs=[spec] * len(operands), o...]
    unnamed x70 -> x9, local copies, waits for them, and re-layouts: 9.53 us -> 2.51 us
    reduce_scatter x2 -> x0, waiting for transfers between devices: 6.48 us -> none  [the longest x1 6.46 us: body(): lax.psum_scatter(deep_part.astype(jnp.bfloat16), 'freq', scatter_dimensio...]
    convert_element_type x5 -> x0, other arithmetic: 4.69 us -> none  [the longest x1 1.5 us: body(): image_shallow = lax.psum_scatter(shallow_part.astype(jnp.bfloat16), 'freq...]
  transfers between devices with their start and end apart: 4 -> 3, of which waited for: 2 -> 2; matrix products, arithmetic and copies ran while one was open for 24% -> 2% of each run, Pallas kernels for 0% -> 3%
where the time goes in v1:
time: 43.6 us; the launch traced here: 43.3 us
  blocking collectives  18.1 us (42%)
  waiting for transfers between devices  9.69 us (22%)
  Pallas kernels  7.2 us (17%)
  starting transfers between devices  3.69 us (8%)
  local copies, waits for them, and re-layouts  2.51 us (6%)
  other arithmetic  1.35 us (3%)
  between operations  0.71 us (2%)
    all_to_all x1, blocking collectives, body(): moved = lax.all_to_all(first, 'wide', 0, 0, tiled=True)  18.1 us
    all_to_all x1, waiting for transfers between devices, body(): returned = lax.all_to_all(third, 'wide', 0, 0, tiled=True)  9.13 us
    pallas_call x3, Pallas kernels, call(): pl.pallas_call(kernel, out_shape=outs, in_specs=[spec] * len(operands), o...  7.2 us
    all_to_all x1, starting transfers between devices, body(): returned = lax.all_to_all(third, 'wide', 0, 0, tiled=True)  3.55 us
    unnamed x9, local copies, waits for them, and re-layouts  2.51 us
    add x2, other arithmetic, freq_sum(): total + lax.ppermute(send[shift - 1], 'freq', pairs).astype(jnp.float32)  1.35 us
  transfers between devices with their start and end apart: 3, of which 2 were waited for; matrix products, arithmetic and copies ran while one was open for 2% of the time, Pallas kernels for 3%

profile of v1, /device:TPU:0, one launch (start us, length us, event | category | flops | bytes accessed | tf_op | source)
XLA Modules:
  0.0 43.3 jit_solution(10130273443832284599)
XLA Ops:
  0.6 0.7 %copy.7.filt_ref = bf16[2,2,1,3,81]{4,3,2,1,0:T(4,128)(2,1)S(1)} copy(bf16[2,2,1,3,81]{4,1,3,2,0:T(2,128)(2,1)} %param.6) | data formatting | bytes 3888 | tf_op args[1]
  1.3 0.0 copy-start.2
  1.3 0.8 %copy.8.bins_ref = s32[2,2,3,1024]{3,2,1,0:T(4,128)S(1)} copy(s32[2,2,3,1024]{3,1,2,0:T(2,128)} %param.7) | data formatting | bytes 98304 | tf_op args[2]
  2.2 0.0 copy-done.2
  2.2 0.0 copy-start
  2.2 0.9 %copy-done = bf16[2,1,64,1024]{3,2,1,0:T(8,128)(2,1)S(1)} copy-done((bf16[2,1,64,1024]{3,2,1,0:T(8,128)(2,1)S(1)}, bf16[2,1,64,1024]{3,2,1,0:T(8,128)(2,1)}, u32[]{:S(2)}) %copy-start) | copy-done | bytes 262168
  3.2 1.9 %first.1 = bf16[16,64,128]{2,1,0:T(8,128)(2,1)S(1)} custom-call(bf16[2,64,1024]{2,1,0:T(8,128)(2,1)S(1)} %bitcast.3, bf16[2,2,1,3,81]{4,3,2,1,0:T(4,128)(2,1)S(1)} %copy.7.filt_ref, s32[2,2,3,1024]{3,2,1,0:T(4,128)S(1)} %copy.8.bins_ref, s32[2,2,3,1024]{3,2,1,0:T(4,128)S(1)} %copy.9.levels_ref), custom_call_target="tpu_custom_call" | custom-call | flops 603979776 | bytes 1048576 | tf_op jit(solution)/shard_map/first/pallas_call | solution.py:278
  5.1 0.0 copy-start.1
  5.1 18.1 %all_to_all.10.moved_ref = bf16[16,64,128]{2,1,0:T(8,128)(2,1)S(1)} all-to-all(bf16[16,64,128]{2,1,0:T(8,128)(2,1)S(1)} %first.1), channel_id=1, replica_groups=mesh['wide'=16,'freq'=2] {'wide'}, dimensions={0} | all-to-all | bytes 524288 | tf_op jit(solution)/shard_map/all_to_all | solution.py:321
  23.2 0.0 copy-done.1
  23.2 4.1 %middle.1 = (bf16[16,64,128]{2,1,0:T(8,128)(2,1)}, bf16[1,64,512]{2,1,0:T(8,128)(2,1)S(1)}, f32[64,512]{1,0:T(8,128)S(1)}) custom-call(bf16[16,64,128]{2,1,0:T(8,128)(2,1)S(1)} %all_to_all.10.moved_ref, bf16[2,2,1,3,81]{4,3,2,1,0:T(4,128)(2,1)S(1)} %copy.7.filt_ref, s32[2,2,3,1024]{3,2,1,0:T(4,128)S(1)} %copy.8.bins_ref, ...), custom_call_target="tpu_custom_call" | custom-call | flops 1207959552 | bytes 1048576 | tf_op jit(solution)/shard_map/middle/pallas_call | solution.py:278
  27.3 3.5 %all-to-all-start.1 = ((bf16[16,64,128]{2,1,0:T(8,128)(2,1)}), bf16[16,64,128]{2,1,0:T(8,128)(2,1)S(1)}, u32[]{:S(2)}, u32[]{:S(2)}) async-start(bf16[16,64,128]{2,1,0:T(8,128)(2,1)} %get-tuple-element.9), calls=%async_computation.1 | async-start | bytes 524288 | tf_op jit(solution)/shard_map/all_to_all | solution.py:337
  30.8 0.1 collective-permute-start
  30.9 9.1 %all-to-all-done.1.field_ref = bf16[16,64,128]{2,1,0:T(8,128)(2,1)S(1)} async-done(((bf16[16,64,128]{2,1,0:T(8,128)(2,1)}), bf16[16,64,128]{2,1,0:T(8,128)(2,1)S(1)}, u32[]{:S(2)}, u32[]{:S(2)}) %all-to-all-start.1) | async-done | bytes 262176 | tf_op jit(solution)/shard_map/all_to_all | solution.py:337
  40.0 1.2 %last.1 = (bf16[1,64,512]{2,1,0:T(8,128)(2,1)S(1)}, f32[64,512]{1,0:T(8,128)S(1)}) custom-call(bf16[16,64,128]{2,1,0:T(8,128)(2,1)S(1)} %all-to-all-done.1.field_ref, bf16[2,2,1,3,81]{4,3,2,1,0:T(4,128)(2,1)S(1)} %copy.7.filt_ref, s32[2,2,3,1024]{3,2,1,0:T(4,128)S(1)} %copy.8.bins_ref, s32[2,2,3,1024]{3,2,1,0:T(4,128)S(1)} %copy.9.levels_ref, ...), custom_call_target="tpu_custom_call" | custom-call | flops 301989888 | bytes 1048576 | tf_op jit(solution)/shard_map/last/pallas_call | solution.py:278
  41.3 0.1 collective-permute-start.1
  41.3 0.0 collective-permute-done
  41.3 0.7 %convert_add_fusion.1 = f32[64,512]{1,0:T(8,128)} fusion(f32[64,512]{1,0:T(8,128)S(1)} %get-tuple-element.7, bf16[64,512]{1,0:T(8,128)(2,1)S(1)} %collective-permute-done), kind=kLoop, calls=%fused_computation.1 | loop fusion | flops 65536 | bytes 327680 | tf_op jit(solution)/shard_map/add | solution.py:294
  42.0 0.6 %collective-permute-done.1 = bf16[64,512]{1,0:T(8,128)(2,1)S(1)} collective-permute-done((bf16[64,512]{1,0:T(8,128)(2,1)S(1)}, bf16[64,512]{1,0:T(8,128)(2,1)S(1)}, u32[]{:S(2)}, u32[]{:S(2)}) %collective-permute-start.1) | collective-permute-done | bytes 65568 | tf_op jit(solution)/shard_map/ppermute | solution.py:294
  42.6 0.7 %convert_add_fusion = f32[64,512]{1,0:T(8,128)} fusion(f32[64,512]{1,0:T(8,128)S(1)} %get-tuple-element.10, bf16[64,512]{1,0:T(8,128)(2,1)S(1)} %collective-permute-done.1), kind=kLoop, calls=%fused_computation | loop fusion | flops 65536 | bytes 327680 | tf_op jit(solution)/shard_map/add | solution.py:294
  (1 shorter events, 0.0 us)
Async XLA Ops:
  1.3 0.8 %copy-start.2 = (s32[2,2,3,1024]{3,1,2,0:T(2,128)S(1)}, s32[2,2,3,1024]{3,1,2,0:T(2,128)}, u32[]{:S(2)}) copy-start(s32[2,2,3,1024]{3,1,2,0:T(2,128)} %param.8) | copy-start | bytes 147460
  2.2 1.0 %copy-start = (bf16[2,1,64,1024]{3,2,1,0:T(8,128)(2,1)S(1)}, bf16[2,1,64,1024]{3,2,1,0:T(8,128)(2,1)}, u32[]{:S(2)}) copy-start(bf16[2,1,64,1024]{3,2,1,0:T(8,128)(2,1)} %param.5) | copy-start | bytes 786436
  5.1 18.1 %copy-start.1 = (s32[2,64,64]{2,1,0:T(8,128)S(1)}, s32[2,64,64]{2,1,0:T(8,128)}, u32[]{:S(2)}) copy-start(s32[2,64,64]{2,1,0:T(8,128)} %aperture_ref.3) | copy-start | bytes 98308
  27.3 12.8 %all-to-all-start.1 = ((bf16[16,64,128]{2,1,0:T(8,128)(2,1)}), bf16[16,64,128]{2,1,0:T(8,128)(2,1)S(1)}, u32[]{:S(2)}, u32[]{:S(2)}) async-start(bf16[16,64,128]{2,1,0:T(8,128)(2,1)} %get-tuple-element.9), calls=%async_computation.1 | async-start | bytes 524288 | tf_op jit(solution)/shard_map/all_to_all | solution.py:337
  30.8 10.5 %collective-permute-start = (bf16[64,512]{1,0:T(8,128)(2,1)S(1)}, bf16[64,512]{1,0:T(8,128)(2,1)S(1)}, u32[]{:S(2)}, u32[]{:S(2)}) collective-permute-start(bf16[64,512]{1,0:T(8,128)(2,1)S(1)} %bitcast.4), channel_id=1, source_target_pairs={{0,1},{1,0},{2,3},{3,2},{4,5},{5,4},{6,7},{7,6},{8,9},{9,8},{10,11... | collective-permute-start | bytes 196616 | tf_op jit(solution)/shard_map/ppermute | solution.py:294
  41.3 1.3 %collective-permute-start.1 = (bf16[64,512]{1,0:T(8,128)(2,1)S(1)}, bf16[64,512]{1,0:T(8,128)(2,1)S(1)}, u32[]{:S(2)}, u32[]{:S(2)}) collective-permute-start(bf16[64,512]{1,0:T(8,128)(2,1)S(1)} %bitcast.5), channel_id=1, source_target_pairs={{0,1},{1,0},{2,3},{3,2},{4,5},{5,4},{6,7},{7,6},{8,9},{9,8},{10,11... | collective-permute-start | bytes 196616 | tf_op jit(solution)/shard_map/ppermute | solution.py:294

commit v2 on v1

v2 whole, which is shorter than its diff:
```python
import functools
import math

import jax
import jax.numpy as jnp
from jax import lax
from jax.experimental import pallas as pl
from jax.experimental.pallas import tpu as pltpu
from jax.sharding import PartitionSpec as P

LANES = 128
VMEM_LIMIT = 24 * 1024 * 1024


class Sizes:
    def __init__(self, mesh, wave_shape, filters_shape, aperture_shape):
        self.wide = mesh.shape["wide"]
        self.freq = mesh.shape["freq"]
        self.pos = wave_shape[-1]
        self.rows = wave_shape[-2]
        self.side = math.isqrt(self.pos)
        self.bins = filters_shape[-2]
        self.tap_count = filters_shape[-1]
        self.taps = math.isqrt(self.tap_count)
        self.half = self.taps // 2
        self.tile_rows = LANES // self.side
        self.tiles = self.pos // LANES
        self.halo = -(-self.half // self.tile_rows)
        self.window = (1 + 2 * self.halo) * LANES
        self.blocks = aperture_shape[-1]
        self.blk = self.pos // self.blocks


def fill_taps(z, filt_ref, step, rows_ref):
    rows_ref[...] = jnp.zeros_like(rows_ref)
    for k in range(z.bins):
        pair = filt_ref[step, 0, k].astype(jnp.float32)
        for part in range(2):
            row = part * z.bins + k
            rows_ref[row : row + 1, : z.tap_count] = pair[part : part + 1]


def fill_table(z, bins_ref, levels_ref, step, side, table_ref):
    blend = bins_ref.shape[1]
    ids = [bins_ref[step, j, side : side + 1] for j in range(blend)]
    weights = [levels_ref[step, j, side : side + 1].astype(jnp.float32) for j in range(blend)]
    total = sum(weights[1:], weights[0])
    table_ref[...] = jnp.zeros_like(table_ref)
    for k in range(z.bins):
        hits = [jnp.where(i == k, w, 0.0) for i, w in zip(ids, weights)]
        table_ref[k : k + 1, :] = sum(hits[1:], hits[0]) / total


def tap_index(z, in_y, in_x, out_y, out_x):
    a = in_y - out_y + (z.half - z.halo * z.tile_rows)
    b = in_x - out_x + z.half
    valid = (a >= 0) & (a < z.taps) & (b >= 0) & (b < z.taps)
    return jnp.where(valid, a * z.taps + b, LANES - 1)


def spread(rows_ref, row, index):
    source = jnp.broadcast_to(rows_ref[row : row + 1, :], index.shape)
    return jnp.take_along_axis(source, index, axis=1, mode="promise_in_bounds")


def chunk_order(z, column):
    chunk, inside = column // (2 * z.rows), column % (2 * z.rows)
    return inside // z.rows, chunk * z.rows + inside % z.rows


def fetch(pairs, sems):
    copies = [pltpu.make_async_copy(source, target, sems.at[i]) for i, (source, target) in enumerate(pairs)]
    for copy in copies:
        copy.start()
    return copies


def sent(z, out_ref, out_hbm, sems, tile):
    chunks = LANES // z.rows
    place = pl.ds(tile * chunks, chunks)
    return pltpu.make_async_copy(out_ref.at[place], out_hbm.at[place], sems.at[tile])


def send_out(z, out_ref, out_hbm, sems, tile):
    sent(z, out_ref, out_hbm, sems, tile).start()


def first_kernel(
    z,
    wave_hbm,
    filt_hbm,
    bins_hbm,
    levels_hbm,
    out_hbm,
    wave_ref,
    filt_ref,
    bins_ref,
    levels_ref,
    taps_ref,
    table_ref,
    band_ref,
    lhs_ref,
    out_ref,
    out_sems,
    sems,
):
    copies = fetch(
        [(filt_hbm, filt_ref), (bins_hbm, bins_ref), (levels_hbm, levels_ref), (wave_hbm, wave_ref)], sems
    )
    copies[0].wait()
    fill_taps(z, filt_ref, 0, taps_ref)
    lane = lax.broadcasted_iota(jnp.int32, (z.window, LANES), 1)
    row = lax.broadcasted_iota(jnp.int32, (z.window, LANES), 0)
    for v in range(2):
        part, point = chunk_order(z, lane + v * LANES)
        index = tap_index(z, row // z.side, row % z.side, point // z.side, point % z.side)
        for k in range(z.bins):
            real, imag = spread(taps_ref, k, index), spread(taps_ref, z.bins + k, index)
            columns = slice((2 * k + v) * LANES, (2 * k + v + 1) * LANES)
            band_ref[: z.window, columns] = jnp.where(part == 0, real, imag).astype(jnp.bfloat16)
            band_ref[z.window :, columns] = jnp.where(part == 0, -imag, real).astype(jnp.bfloat16)
    copies[1].wait()
    copies[2].wait()
    fill_table(z, bins_ref, levels_ref, 0, 0, table_ref)
    copies[3].wait()
    spans = 1 + 2 * z.halo
    for part in range(2):
        for tile in range(z.tiles):
            for span in range(spans):
                source = tile + span - z.halo
                place = (part * spans + span) * LANES
                if 0 <= source < z.tiles:
                    piece = wave_ref[part, :, source * LANES : (source + 1) * LANES]
                else:
                    piece = jnp.zeros((z.rows, LANES), jnp.bfloat16)
                lhs_ref[tile * z.rows : (tile + 1) * z.rows, place : place + LANES] = piece
    lane = lax.broadcasted_iota(jnp.int32, (8, LANES), 1)
    points = [chunk_order(z, lane + v * LANES)[1] for v in range(2)]
    products = [
        jnp.dot(
            lhs_ref[...],
            band_ref[:, 2 * k * LANES : 2 * (k + 1) * LANES],
            preferred_element_type=jnp.float32,
        )
        for k in range(z.bins)
    ]
    for tile in range(z.tiles):
        weights = table_ref[:, tile * LANES : (tile + 1) * LANES]
        weights = jnp.concatenate(
            [jnp.take_along_axis(weights, p, axis=1, mode="promise_in_bounds") for p in points], axis=1
        )
        total = 0.0
        for k in range(z.bins):
            total = total + products[k][tile * z.rows : (tile + 1) * z.rows] * weights[k : k + 1]
        total = total.astype(jnp.bfloat16)
        chunks = LANES // z.rows
        for c in range(chunks):
            out_ref[tile * chunks + c] = total[:, 2 * z.rows * c : 2 * z.rows * (c + 1)]
        send_out(z, out_ref, out_hbm, out_sems, tile)
    for tile in range(z.tiles):
        sent(z, out_ref, out_hbm, out_sems, tile).wait()


def prepare_middle_kernel(
    z,
    filt_hbm,
    bins_hbm,
    levels_hbm,
    aperture_hbm,
    second_ref,
    third_ref,
    keep_ref,
    filt_ref,
    bins_ref,
    levels_ref,
    aperture_ref,
    taps_ref,
    table_ref,
    columns_ref,
    sems,
):
    copies = fetch(
        [(filt_hbm, filt_ref), (bins_hbm, bins_ref), (levels_hbm, levels_ref), (aperture_hbm, aperture_ref)],
        sems,
    )
    for copy in copies:
        copy.wait()
    lane = lax.broadcasted_iota(jnp.int32, (LANES, LANES), 1)
    row = lax.broadcasted_iota(jnp.int32, (LANES, LANES), 0)
    for step, band_ref in ((0, second_ref), (1, third_ref)):
        fill_taps(z, filt_ref, step, taps_ref)
        fill_table(z, bins_ref, levels_ref, step, 1, table_ref)
        columns = jnp.transpose(table_ref[...])
        for k in range(z.bins):
            columns_ref[k] = jnp.broadcast_to(columns[:, k : k + 1], (z.pos, LANES))

        @pl.loop(0, 1 + 2 * z.halo)
        def _(span, band_ref=band_ref):
            inner = lane + span * LANES
            index = tap_index(z, inner // z.side, inner % z.side, row // z.side, row % z.side)
            for part in range(2):
                taps = [spread(taps_ref, part * z.bins + k, index) for k in range(z.bins)]
                place = pl.multiple_of(part * z.window + span * LANES, LANES)
                for tile in range(z.tiles):
                    total = 0.0
                    for k in range(z.bins):
                        total = total + taps[k] * columns_ref[k, tile * LANES : (tile + 1) * LANES, :]
                    band_ref[tile, :, pl.ds(place, LANES)] = total.astype(jnp.bfloat16)

    width = 2 * z.rows
    offset = lax.axis_index("wide") * z.rows
    receiver = lax.broadcasted_iota(jnp.int32, (z.blocks, width), 1) % z.rows + offset
    pick = (receiver // z.blk == lax.broadcasted_iota(jnp.int32, (z.blocks, width), 0)).astype(jnp.float32)
    keep_ref[...] = jnp.dot(aperture_ref[0].astype(jnp.float32), pick, preferred_element_type=jnp.float32)


def prepare_last_kernel(
    z,
    filt_hbm,
    bins_hbm,
    levels_hbm,
    aperture_hbm,
    fourth_ref,
    keep_ref,
    filt_ref,
    bins_ref,
    levels_ref,
    aperture_ref,
    taps_ref,
    table_ref,
    sems,
):
    copies = fetch(
        [(filt_hbm, filt_ref), (bins_hbm, bins_ref), (levels_hbm, levels_ref), (aperture_hbm, aperture_ref)],
        sems,
    )
    for copy in copies:
        copy.wait()
    fill_taps(z, filt_ref, 1, taps_ref)
    fill_table(z, bins_ref, levels_ref, 1, 0, table_ref)
    lane = lax.broadcasted_iota(jnp.int32, (z.rows, LANES), 1)
    row = lax.broadcasted_iota(jnp.int32, (z.rows, LANES), 0)

    @pl.loop(0, z.window // z.rows)
    def _(block):
        inner = row + block * z.rows
        index = tap_index(z, inner // z.side, inner % z.side, lane // z.side, lane % z.side)
        for part in range(2):
            taps = [spread(taps_ref, part * z.bins + k, index) for k in range(z.bins)]
            place = pl.multiple_of((2 * block + part) * z.rows, z.rows)
            for tile in range(z.tiles):
                total = 0.0
                for k in range(z.bins):
                    total = total + taps[k] * table_ref[k : k + 1, tile * LANES : (tile + 1) * LANES]
                total = total if part == 0 else -total
                fourth_ref[tile, pl.ds(place, z.rows), :] = total.astype(jnp.bfloat16)

    offset = lax.axis_index("wide") * z.rows
    source = lax.broadcasted_iota(jnp.int32, (z.rows, z.blocks), 0) + offset
    pick = (source // z.blk == lax.broadcasted_iota(jnp.int32, (z.rows, z.blocks), 1)).astype(jnp.float32)
    mine = jnp.dot(pick, aperture_ref[1].astype(jnp.float32), preferred_element_type=jnp.float32)
    receiver = lax.broadcasted_iota(jnp.int32, (z.blocks, z.pos), 1)
    stretch = (receiver // z.blk == lax.broadcasted_iota(jnp.int32, (z.blocks, z.pos), 0)).astype(jnp.float32)
    keep_ref[...] = jnp.dot(mine, stretch, preferred_element_type=jnp.float32)


def turned(z, block):
    return jnp.concatenate([-block[:, z.rows :], block[:, : z.rows]], axis=1)


def over_sources(z, band_ref, straight_ref, turned_ref, tile):
    start = tile * LANES
    rhs = jnp.concatenate(
        [straight_ref[start : start + z.window, :], turned_ref[start : start + z.window, :]], axis=0
    )
    return jnp.dot(band_ref[tile], rhs, preferred_element_type=jnp.float32)


def middle_kernel(
    z,
    moved_ref,
    second_ref,
    third_ref,
    keep_ref,
    out_hbm,
    shallow_hbm,
    straight_ref,
    turned_ref,
    straight2_ref,
    turned2_ref,
    out_ref,
    out_sems,
    shallow_sem,
):
    pad = z.halo * LANES
    width = 2 * z.rows
    for ref in (straight_ref, turned_ref, straight2_ref, turned2_ref):
        ref[:pad, :] = jnp.zeros((pad, width), jnp.bfloat16)
        ref[pad + z.pos :, :] = jnp.zeros((pad, width), jnp.bfloat16)
    field = moved_ref[...].reshape(z.pos, width)
    straight_ref[pad : pad + z.pos, :] = field
    turned_ref[pad : pad + z.pos, :] = turned(z, field)
    per_tile = LANES // z.blk
    for tile in range(z.tiles):
        place = slice(pad + tile * LANES, pad + (tile + 1) * LANES)
        mask = keep_ref[tile * per_tile : (tile + 1) * per_tile, :]
        mask = jnp.broadcast_to(mask[:, None, :], (per_tile, z.blk, width)).reshape(LANES, width)
        shallow = over_sources(z, second_ref, straight_ref, turned_ref, tile) * mask
        shallow = shallow.astype(jnp.bfloat16)
        straight2_ref[place, :] = shallow
        turned2_ref[place, :] = turned(z, shallow)
    shallow_copy = pltpu.make_async_copy(
        straight2_ref.at[pl.ds(pad, z.pos)], shallow_hbm, shallow_sem.at[0]
    )
    shallow_copy.start()
    chunks = LANES // z.rows
    for tile in range(z.tiles):
        third = over_sources(z, third_ref, straight2_ref, turned2_ref, tile).astype(jnp.bfloat16)
        out_ref[tile * chunks : (tile + 1) * chunks] = third.reshape(chunks, z.rows, width)
        send_out(z, out_ref, out_hbm, out_sems, tile)
    for tile in range(z.tiles):
        sent(z, out_ref, out_hbm, out_sems, tile).wait()
    shallow_copy.wait()


def split_sum(z, real_ref, send_ref, own_ref):
    me = lax.axis_index("freq")
    width = z.pos // z.freq

    def part(shift):
        start = lax.rem(me + shift, z.freq) * width
        return real_ref[:, pl.ds(pl.multiple_of(start, width), width)]

    own_ref[...] = part(0).astype(jnp.float32)
    for shift in range(1, z.freq):
        send_ref[shift - 1] = part(shift)


def turn_kernel(z, shallow_hbm, send_ref, own_ref, shallow_ref, real_ref, sems):
    for copy in fetch([(shallow_hbm, shallow_ref)], sems):
        copy.wait()
    for tile in range(z.tiles):
        columns = slice(tile * LANES, (tile + 1) * LANES)
        flipped = jnp.transpose(shallow_ref[columns, :].astype(jnp.float32))
        real_ref[:, columns] = flipped[: z.rows].astype(jnp.bfloat16)
    split_sum(z, real_ref, send_ref, own_ref)


def last_kernel(z, field_ref, fourth_ref, keep_ref, send_ref, own_ref, lhs_ref, real_ref):
    pad = 2 * z.halo * LANES
    width = 2 * z.rows
    lhs_ref[:, :pad] = jnp.zeros((z.rows, pad), jnp.bfloat16)
    lhs_ref[:, pad + 2 * z.pos :] = jnp.zeros((z.rows, pad), jnp.bfloat16)
    for source in range(z.wide):
        lhs_ref[:, pad + source * width : pad + (source + 1) * width] = field_ref[source]
    for tile in range(z.tiles):
        start = 2 * tile * LANES
        columns = slice(tile * LANES, (tile + 1) * LANES)
        fourth = jnp.dot(
            lhs_ref[:, start : start + 2 * z.window], fourth_ref[tile], preferred_element_type=jnp.float32
        )
        real_ref[:, columns] = (fourth * keep_ref[:, columns]).astype(jnp.bfloat16)
    split_sum(z, real_ref, send_ref, own_ref)


def call(kernel, operands, outs, scratch, flops, name, fetched=False, sent=()):
    source = pltpu.HBM if fetched else pltpu.VMEM
    spaces = [pltpu.HBM if i < len(sent) else pltpu.VMEM for i in range(len(outs))]
    scratch = [pltpu.VMEM(shape, dtype) for shape, dtype in scratch]
    if sent:
        scratch += [pltpu.VMEM(*outs[0])] + [pltpu.SemaphoreType.DMA((parts,)) for parts in sent]
    if fetched:
        scratch = [pltpu.VMEM(x.shape, x.dtype) for x in operands] + scratch
        scratch.append(pltpu.SemaphoreType.DMA((len(operands),)))
        operands = [pltpu.with_memory_space_constraint(x, pltpu.HBM) for x in operands]
    return pl.pallas_call(
        kernel,
        out_shape=[space(shape, dtype) for space, (shape, dtype) in zip(spaces, outs)],
        in_specs=[pl.BlockSpec(memory_space=source)] * len(operands),
        out_specs=[pl.BlockSpec(memory_space=space) for space in spaces],
        scratch_shapes=scratch,
        compiler_params=pltpu.CompilerParams(vmem_limit_bytes=VMEM_LIMIT),
        cost_estimate=pl.CostEstimate(flops=flops, bytes_accessed=1 << 20, transcendentals=0),
        name=name,
    )(*operands)


def freq_sum(z, send, own):
    total = own
    for shift in range(1, z.freq):
        pairs = [(source, (source + shift) % z.freq) for source in range(z.freq)]
        total = total + lax.ppermute(send[shift - 1], "freq", pairs).astype(jnp.float32)
    return total


def body(mesh, wave, filters, vel_bins, blend_levels, aperture):
    z = Sizes(mesh, wave.shape, filters.shape, aperture.shape)
    bf16, f32 = jnp.bfloat16, jnp.float32
    filters = jnp.transpose(filters, (0, 2, 3, 1, 4))
    vel_bins = jnp.transpose(vel_bins, (0, 2, 1, 3))
    blend_levels = jnp.transpose(blend_levels, (0, 2, 1, 3))
    width = 2 * z.rows
    chunks = ((z.wide, z.rows, width), bf16)
    split = z.pos // z.freq
    parts = [((z.freq - 1, z.rows, split), bf16), ((z.rows, split), f32)]
    small = [((8, LANES), f32), ((8, z.pos), f32)]
    dense = 2 * 2 * z.window * z.bins * z.pos * z.rows
    (first,) = call(
        functools.partial(first_kernel, z),
        (wave[:, 0], filters, vel_bins, blend_levels),
        [chunks],
        small
        + [
            ((2 * z.window, 2 * z.bins * LANES), bf16),
            ((z.tiles * z.rows, 2 * z.window), bf16),
        ],
        2 * dense,
        "first",
        fetched=True,
        sent=(z.tiles,),
    )
    moved = lax.all_to_all(first, "wide", 0, 0, tiled=True)
    second_band, third_band, shallow_keep = call(
        functools.partial(prepare_middle_kernel, z),
        (filters, vel_bins, blend_levels, aperture),
        [
            ((z.tiles, LANES, 2 * z.window), bf16),
            ((z.tiles, LANES, 2 * z.window), bf16),
            ((z.blocks, width), f32),
        ],
        small + [((z.bins, z.pos, LANES), f32)],
        dense,
        "prepare_middle",
        fetched=True,
    )
    padded = z.pos + 2 * z.halo * LANES
    third, shallow = call(
        functools.partial(middle_kernel, z),
        (moved, second_band, third_band, shallow_keep),
        [chunks, ((z.pos, width), bf16)],
        [((padded, width), bf16)] * 4,
        dense,
        "middle",
        sent=(z.tiles, 1),
    )
    returned = lax.all_to_all(third, "wide", 0, 0, tiled=True)
    fourth_band, deep_keep = call(
        functools.partial(prepare_last_kernel, z),
        (filters, vel_bins, blend_levels, aperture),
        [((z.tiles, 2 * z.window, LANES), bf16), ((z.rows, z.pos), f32)],
        small,
        dense,
        "prepare_last",
        fetched=True,
    )
    image_shallow = freq_sum(
        z,
        *call(
            functools.partial(turn_kernel, z),
            (shallow,),
            parts,
            [((z.rows, z.pos), bf16)],
            dense // 8,
            "turn",
            fetched=True,
        ),
    )
    returned, image_shallow, fourth_band, deep_keep = lax.optimization_barrier(
        (returned, image_shallow, fourth_band, deep_keep)
    )
    image_deep = freq_sum(
        z,
        *call(
            functools.partial(last_kernel, z),
            (returned, fourth_band, deep_keep),
            parts,
            [((z.rows, 2 * padded), bf16), ((z.rows, z.pos), bf16)],
            dense // 4,
            "last",
        ),
    )
    return image_shallow, image_deep


def solution(mesh):
    return jax.shard_map(
        functools.partial(body, mesh),
        mesh=mesh,
        in_specs=(P(None, "freq", "wide", None), P(None, None, "freq", None, None), P(), P(), P()),
        out_specs=(P("wide", "freq"), P("wide", "freq")),
        check_vma=False,
    )
```

time: 43.6 us -> 40 us (0.917)
  blocking collectives: 18.1 us -> 0 us
  starting transfers between devices: 3.69 us -> 12 us
  Pallas kernels: 7.2 us -> 14.5 us
  local copies, waits for them, and re-layouts: 2.51 us -> 0 us
  waiting for transfers between devices: 9.69 us -> 10.9 us
    all_to_all x1 -> x0, blocking collectives: 18.1 us -> none  [body(): moved = lax.all_to_all(first, 'wide', 0, 0, tiled=True)]
    all_to_all x0 -> x1, starting transfers between devices: none -> 8.32 us  [body(): moved = lax.all_to_all(first, 'wide', 0, 0, tiled=True)]
    pallas_call x3 -> x6, Pallas kernels: 7.2 us -> 14.5 us  [call(): pl.pallas_call(kernel, out_shape=[space(shape, dtype) for space, (shape,...]
    all_to_all x0 -> x1, waiting for transfers between devices: none -> 5 us  [body(): moved = lax.all_to_all(first, 'wide', 0, 0, tiled=True)]
    all_to_all x1, waiting for transfers between devices: 9.13 us -> 4.67 us  [body(): returned = lax.all_to_all(third, 'wide', 0, 0, tiled=True)]
    unnamed x9 -> x0, local copies, waits for them, and re-layouts: 2.51 us -> none
    ppermute x2, waiting for transfers between devices: 0.56 us -> 1.24 us  [freq_sum(): lax.ppermute(send[shift - 1], 'freq', pairs).astype(jnp.float32)]
  transfers between devices with their start and end apart: 3 -> 4, of which waited for: 2 -> 3; matrix products, arithmetic and copies ran while one was open for 2% -> 2% of each run, Pallas kernels for 3% -> 22%
where the time goes in v2:
time: 40 us; the launch traced here: 39.5 us
  Pallas kernels  14.5 us (36%)
  starting transfers between devices  12 us (30%)
  waiting for transfers between devices  10.9 us (27%)
  other arithmetic  1.34 us (3%)
  between operations  0.71 us (2%)
    pallas_call x6, Pallas kernels, call(): pl.pallas_call(kernel, out_shape=[space(shape, dtype) for space, (shape,...  14.5 us
    all_to_all x1, starting transfers between devices, body(): moved = lax.all_to_all(first, 'wide', 0, 0, tiled=True)  8.32 us
    all_to_all x1, waiting for transfers between devices, body(): moved = lax.all_to_all(first, 'wide', 0, 0, tiled=True)  5 us
    all_to_all x1, waiting for transfers between devices, body(): returned = lax.all_to_all(third, 'wide', 0, 0, tiled=True)  4.67 us
    all_to_all x1, starting transfers between devices, body(): returned = lax.all_to_all(third, 'wide', 0, 0, tiled=True)  3.56 us
    add x2, other arithmetic, freq_sum(): total + lax.ppermute(send[shift - 1], 'freq', pairs).astype(jnp.float32)  1.34 us
    ppermute x2, waiting for transfers between devices, freq_sum(): lax.ppermute(send[shift - 1], 'freq', pairs).astype(jnp.float32)  1.24 us
  transfers between devices with their start and end apart: 4, of which 3 were waited for; matrix products, arithmetic and copies ran while one was open for 2% of the time, Pallas kernels for 22%

profile of v2, /device:TPU:0, one launch (start us, length us, event | category | flops | bytes accessed | tf_op | source)
XLA Modules:
  0.0 39.5 jit_solution(4253259941313621476)
XLA Ops:
  0.6 3.7 %first.1 = bf16[16,64,128]{2,1,0:T(8,128)(2,1)} custom-call(bf16[2,64,1024]{2,1,0:T(8,128)(2,1)} %bitcast.8, bf16[2,1,3,2,81]{4,3,2,1,0:T(2,128)(2,1)} %bitcast.15, s32[2,3,2,1024]{3,2,1,0:T(2,128)} %bitcast.9, s32[2,3,2,1024]{3,2,1,0:T(2,128)} %bitcast.12), custom_call_target="tpu_custom_call" | custom-call | flops 603979776 | bytes 1048576 | tf_op jit(solution)/shard_map/first/pallas_call | solution.py:376
  4.3 8.3 %all-to-all-start = ((bf16[16,64,128]{2,1,0:T(8,128)(2,1)}), bf16[16,64,128]{2,1,0:T(8,128)(2,1)S(1)}, u32[]{:S(2)}, u32[]{:S(2)}) async-start(bf16[16,64,128]{2,1,0:T(8,128)(2,1)} %first.1), calls=%async_computation | async-start | bytes 524288 | tf_op jit(solution)/shard_map/all_to_all | solution.py:422
  12.6 4.9 %prepare_middle.1 = (bf16[8,128,768]{2,1,0:T(8,128)(2,1)S(1)}, bf16[8,128,768]{2,1,0:T(8,128)(2,1)S(1)}, f32[64,128]{1,0:T(8,128)S(1)}) custom-call(bf16[2,1,3,2,81]{4,3,2,1,0:T(2,128)(2,1)} %bitcast.16, s32[2,3,2,1024]{3,2,1,0:T(2,128)} %bitcast.10, s32[2,3,2,1024]{3,2,1,0:T(2,128)} %bitcast.13, s32[2,64,64]{2,1,0:T(8,128)} %aperture_hbm.3), custom_call_target="tpu_custom_call" | custom-call | flops 301989888 | bytes 1048576 | tf_op jit(solution)/shard_map/prepare_middle/pallas_call | solution.py:376
  17.5 5.0 %all-to-all-done.moved_ref = bf16[16,64,128]{2,1,0:T(8,128)(2,1)S(1)} async-done(((bf16[16,64,128]{2,1,0:T(8,128)(2,1)}), bf16[16,64,128]{2,1,0:T(8,128)(2,1)S(1)}, u32[]{:S(2)}, u32[]{:S(2)}) %all-to-all-start) | async-done | bytes 262176 | tf_op jit(solution)/shard_map/all_to_all | solution.py:422
  22.5 1.8 %middle.1 = (bf16[16,64,128]{2,1,0:T(8,128)(2,1)}, bf16[1024,128]{1,0:T(8,128)(2,1)}) custom-call(bf16[16,64,128]{2,1,0:T(8,128)(2,1)S(1)} %all-to-all-done.moved_ref, bf16[8,128,768]{2,1,0:T(8,128)(2,1)S(1)} %get-tuple-element.17.second_ref, bf16[8,128,768]{2,1,0:T(8,128)(2,1)S(1)} %get-tuple-element.18.third_ref, f32[64,128]{1,0:T(8,128)S(1)} %get-tuple-element.19.keep_ref), custom_call_target="tpu_custom_call" | custom-call | flops 301989888 | bytes 1048576 | tf_op jit(solution)/shard_map/middle/pallas_call | solution.py:376
  24.3 3.6 %all-to-all-start.1 = ((bf16[16,64,128]{2,1,0:T(8,128)(2,1)}), bf16[16,64,128]{2,1,0:T(8,128)(2,1)S(1)}, u32[]{:S(2)}, u32[]{:S(2)}) async-start(bf16[16,64,128]{2,1,0:T(8,128)(2,1)} %get-tuple-element.20), calls=%async_computation.1 | async-start | bytes 524288 | tf_op jit(solution)/shard_map/all_to_all | solution.py:446
  27.9 1.1 %turn.1 = (bf16[1,64,512]{2,1,0:T(8,128)(2,1)S(1)}, f32[64,512]{1,0:T(8,128)S(1)}) custom-call(bf16[1024,128]{1,0:T(8,128)(2,1)} %get-tuple-element.21.shallow_hbm), custom_call_target="tpu_custom_call" | custom-call | flops 37748736 | bytes 1048576 | tf_op jit(solution)/shard_map/turn/pallas_call | solution.py:376
  29.0 0.1 collective-permute-start
  29.1 2.7 %prepare_last.1 = (bf16[8,768,128]{2,1,0:T(8,128)(2,1)S(1)}, f32[64,1024]{1,0:T(8,128)S(1)}) custom-call(bf16[2,1,3,2,81]{4,3,2,1,0:T(2,128)(2,1)} %bitcast.17, s32[2,3,2,1024]{3,2,1,0:T(2,128)} %bitcast.11, s32[2,3,2,1024]{3,2,1,0:T(2,128)} %bitcast.14, s32[2,64,64]{2,1,0:T(8,128)} %aperture_hbm.3), custom_call_target="tpu_custom_call" | custom-call | flops 301989888 | bytes 1048576 | tf_op jit(solution)/shard_map/prepare_last/pallas_call | solution.py:376
  31.7 0.0 collective-permute-done
  31.7 0.7 %convert_add_fusion.1 = f32[64,512]{1,0:T(8,128)} fusion(f32[64,512]{1,0:T(8,128)S(1)} %get-tuple-element.22, bf16[64,512]{1,0:T(8,128)(2,1)S(1)} %collective-permute-done), kind=kLoop, calls=%fused_computation.1 | loop fusion | flops 65536 | bytes 327680 | tf_op jit(solution)/shard_map/add | solution.py:392
  32.4 4.7 %all-to-all-done.1.field_ref = bf16[16,64,128]{2,1,0:T(8,128)(2,1)S(1)} async-done(((bf16[16,64,128]{2,1,0:T(8,128)(2,1)}), bf16[16,64,128]{2,1,0:T(8,128)(2,1)S(1)}, u32[]{:S(2)}, u32[]{:S(2)}) %all-to-all-start.1) | async-done | bytes 262176 | tf_op jit(solution)/shard_map/all_to_all | solution.py:446
  37.1 0.4 %last.1 = (bf16[1,64,512]{2,1,0:T(8,128)(2,1)S(1)}, f32[64,512]{1,0:T(8,128)S(1)}) custom-call(bf16[16,64,128]{2,1,0:T(8,128)(2,1)S(1)} %all-to-all-done.1.field_ref, bf16[8,768,128]{2,1,0:T(8,128)(2,1)S(1)} %get-tuple-element.28.fourth_ref, f32[64,1024]{1,0:T(8,128)S(1)} %get-tuple-element.29.keep_ref), custom_call_target="tpu_custom_call" | custom-call | flops 75497472 | bytes 1048576 | tf_op jit(solution)/shard_map/last/pallas_call | solution.py:376
  37.5 0.1 collective-permute-start.1
  37.6 1.2 %collective-permute-done.1 = bf16[64,512]{1,0:T(8,128)(2,1)S(1)} collective-permute-done((bf16[64,512]{1,0:T(8,128)(2,1)S(1)}, bf16[64,512]{1,0:T(8,128)(2,1)S(1)}, u32[]{:S(2)}, u32[]{:S(2)}) %collective-permute-start.1) | collective-permute-done | bytes 65568 | tf_op jit(solution)/shard_map/ppermute | solution.py:392
  38.9 0.7 %convert_add_fusion = f32[64,512]{1,0:T(8,128)} fusion(f32[64,512]{1,0:T(8,128)S(1)} %get-tuple-element.30, bf16[64,512]{1,0:T(8,128)(2,1)S(1)} %collective-permute-done.1), kind=kLoop, calls=%fused_computation | loop fusion | flops 65536 | bytes 327680 | tf_op jit(solution)/shard_map/add | solution.py:392
Async XLA Ops:
  4.3 18.2 %all-to-all-start = ((bf16[16,64,128]{2,1,0:T(8,128)(2,1)}), bf16[16,64,128]{2,1,0:T(8,128)(2,1)S(1)}, u32[]{:S(2)}, u32[]{:S(2)}) async-start(bf16[16,64,128]{2,1,0:T(8,128)(2,1)} %first.1), calls=%async_computation | async-start | bytes 524288 | tf_op jit(solution)/shard_map/all_to_all | solution.py:422
  24.3 12.8 %all-to-all-start.1 = ((bf16[16,64,128]{2,1,0:T(8,128)(2,1)}), bf16[16,64,128]{2,1,0:T(8,128)(2,1)S(1)}, u32[]{:S(2)}, u32[]{:S(2)}) async-start(bf16[16,64,128]{2,1,0:T(8,128)(2,1)} %get-tuple-element.20), calls=%async_computation.1 | async-start | bytes 524288 | tf_op jit(solution)/shard_map/all_to_all | solution.py:446
  29.0 2.7 %collective-permute-start = (bf16[64,512]{1,0:T(8,128)(2,1)S(1)}, bf16[64,512]{1,0:T(8,128)(2,1)S(1)}, u32[]{:S(2)}, u32[]{:S(2)}) collective-permute-start(bf16[64,512]{1,0:T(8,128)(2,1)S(1)} %bitcast.6), channel_id=1, source_target_pairs={{0,1},{1,0},{2,3},{3,2},{4,5},{5,4},{6,7},{7,6},{8,9},{9,8},{10,11... | collective-permute-start | bytes 196616 | tf_op jit(solution)/shard_map/ppermute | solution.py:392
  37.5 1.3 %collective-permute-start.1 = (bf16[64,512]{1,0:T(8,128)(2,1)S(1)}, bf16[64,512]{1,0:T(8,128)(2,1)S(1)}, u32[]{:S(2)}, u32[]{:S(2)}) collective-permute-start(bf16[64,512]{1,0:T(8,128)(2,1)S(1)} %bitcast.7), channel_id=1, source_target_pairs={{0,1},{1,0},{2,3},{3,2},{4,5},{5,4},{6,7},{7,6},{8,9},{9,8},{10,11... | collective-permute-start | bytes 196616 | tf_op jit(solution)/shard_map/ppermute | solution.py:392

commit v3 on v2

--- a/solution.py
+++ b/solution.py
@@ -107,18 +107,38 @@
     copies = fetch(
         [(filt_hbm, filt_ref), (bins_hbm, bins_ref), (levels_hbm, levels_ref), (wave_hbm, wave_ref)], sems
     )
+    group_rows = LANES // 2 // z.side
+    window_rows = z.window // z.side
+    lane = lax.broadcasted_iota(jnp.int32, (z.side, LANES), 1)
+    part, point = chunk_order(z, lane)
+    out_y = point // z.side - (z.half - z.halo * z.tile_rows)
+    b = lax.broadcasted_iota(jnp.int32, (z.side, LANES), 0) - point % z.side + z.half
+    b_valid = (b >= 0) & (b < z.taps)
+    base = b - out_y * z.taps
+    is_real = part == 0
+    indices = []
+    for y in range(window_rows - group_rows):
+        valid = b_valid & (out_y <= y) & (out_y > y - z.taps)
+        indices.append(jnp.where(valid, base + y * z.taps, LANES - 1))
+    empty = jnp.zeros((group_rows * z.side, LANES), jnp.bfloat16)
+    for k in range(z.bins):
+        for half in range(2):
+            top, columns = half * z.window, 2 * k * LANES
+            band_ref[top + z.window - group_rows * z.side : top + z.window, columns : columns + LANES] = empty
+            band_ref[top : top + group_rows * z.side, columns + LANES : columns + 2 * LANES] = empty
     copies[0].wait()
     fill_taps(z, filt_ref, 0, taps_ref)
-    lane = lax.broadcasted_iota(jnp.int32, (z.window, LANES), 1)
-    row = lax.broadcasted_iota(jnp.int32, (z.window, LANES), 0)
-    for v in range(2):
-        part, point = chunk_order(z, lane + v * LANES)
-        index = tap_index(z, row // z.side, row % z.side, point // z.side, point % z.side)
-        for k in range(z.bins):
+    for k in range(z.bins):
+        columns = 2 * k * LANES
+        for y, index in enumerate(indices):
             real, imag = spread(taps_ref, k, index), spread(taps_ref, z.bins + k, index)
-            columns = slice((2 * k + v) * LANES, (2 * k + v + 1) * LANES)
-            band_ref[: z.window, columns] = jnp.where(part == 0, real, imag).astype(jnp.bfloat16)
-            band_ref[z.window :, columns] = jnp.where(part == 0, -imag, real).astype(jnp.bfloat16)
+            blocks = (jnp.where(is_real, real, imag), jnp.where(is_real, -imag, real))
+            for half in range(2):
+                block = blocks[half].astype(jnp.bfloat16)
+                top = half * z.window + y * z.side
+                band_ref[top : top + z.side, columns : columns + LANES] = block
+                top += group_rows * z.side
+                band_ref[top : top + z.side, columns + LANES : columns + 2 * LANES] = block
     copies[1].wait()
     copies[2].wait()
     fill_table(z, bins_ref, levels_ref, 0, 0, table_ref)
@@ -346,21 +366,22 @@
     split_sum(z, real_ref, send_ref, own_ref)
 
 
-def last_kernel(z, field_ref, fourth_ref, keep_ref, send_ref, own_ref, lhs_ref, real_ref):
+def last_kernel(z, shifts, field_ref, fourth_ref, keep_ref, out_ref, lhs_ref):
     pad = 2 * z.halo * LANES
     width = 2 * z.rows
     lhs_ref[:, :pad] = jnp.zeros((z.rows, pad), jnp.bfloat16)
     lhs_ref[:, pad + 2 * z.pos :] = jnp.zeros((z.rows, pad), jnp.bfloat16)
     for source in range(z.wide):
         lhs_ref[:, pad + source * width : pad + (source + 1) * width] = field_ref[source]
-    for tile in range(z.tiles):
-        start = 2 * tile * LANES
-        columns = slice(tile * LANES, (tile + 1) * LANES)
-        fourth = jnp.dot(
-            lhs_ref[:, start : start + 2 * z.window], fourth_ref[tile], preferred_element_type=jnp.float32
-        )
-        real_ref[:, columns] = (fourth * keep_ref[:, columns]).astype(jnp.bfloat16)
-    split_sum(z, real_ref, send_ref, own_ref)
+    me = lax.axis_index("freq")
+    tiles = z.tiles // z.freq
+    for i, shift in enumerate(shifts):
+        for j in range(tiles):
+            tile = lax.rem(me + shift, z.freq) * tiles + j
+            window = pl.ds(pl.multiple_of(2 * tile * LANES, 2 * LANES), 2 * z.window)
+            columns = pl.ds(pl.multiple_of(tile * LANES, LANES), LANES)
+            fourth = jnp.dot(lhs_ref[:, window], fourth_ref[tile], preferred_element_type=jnp.float32)
+            out_ref[i, :, j * LANES : (j + 1) * LANES] = (fourth * keep_ref[:, columns]).astype(out_ref.dtype)
 
 
 def call(kernel, operands, outs, scratch, flops, name, fetched=False, sent=()):
@@ -468,17 +489,17 @@
     returned, image_shallow, fourth_band, deep_keep = lax.optimization_barrier(
         (returned, image_shallow, fourth_band, deep_keep)
     )
-    image_deep = freq_sum(
-        z,
-        *call(
-            functools.partial(last_kernel, z),
+    deep = []
+    for shifts, part in ((range(1, z.freq), parts[0]), (range(1), ((1, z.rows, split), bf16))):
+        deep += call(
+            functools.partial(last_kernel, z, shifts),
             (returned, fourth_band, deep_keep),
-            parts,
-            [((z.rows, 2 * padded), bf16), ((z.rows, z.pos), bf16)],
-            dense // 4,
-            "last",
-        ),
-    )
+            [part],
+            [((z.rows, 2 * padded), bf16)],
+            dense // 8,
+            "last_own" if len(deep) else "last_send",
+        )
+    image_deep = freq_sum(z, deep[0], deep[1][0].astype(f32))
     return image_shallow, image_deep
 
 

time: 40 us -> 39 us (0.975)
  Pallas kernels: 14.5 us -> 13.8 us
    pallas_call x6 -> x7, Pallas kernels: 14.5 us -> 13.8 us  [call(): pl.pallas_call(kernel, out_shape=[space(shape, dtype) for space, (shape,...]
  transfers between devices with their start and end apart: 4 -> 4, of which waited for: 3 -> 3; matrix products, arithmetic and copies ran while one was open for 2% -> 2% of each run, Pallas kernels for 22% -> 23%
where the time goes in v3:
time: 39 us; the launch traced here: 38.5 us
  Pallas kernels  13.8 us (35%)
  starting transfers between devices  12 us (31%)
  waiting for transfers between devices  10.6 us (27%)
  other arithmetic  1.34 us (3%)
  between operations  0.72 us (2%)
    pallas_call x7, Pallas kernels, call(): pl.pallas_call(kernel, out_shape=[space(shape, dtype) for space, (shape,...  13.8 us
    all_to_all x1, starting transfers between devices, body(): moved = lax.all_to_all(first, 'wide', 0, 0, tiled=True)  8.33 us
    all_to_all x1, waiting for transfers between devices, body(): moved = lax.all_to_all(first, 'wide', 0, 0, tiled=True)  5 us
    all_to_all x1, waiting for transfers between devices, body(): returned = lax.all_to_all(third, 'wide', 0, 0, tiled=True)  4.67 us
    all_to_all x1, starting transfers between devices, body(): returned = lax.all_to_all(third, 'wide', 0, 0, tiled=True)  3.56 us
    add x2, other arithmetic, freq_sum(): total + lax.ppermute(send[shift - 1], 'freq', pairs).astype(jnp.float32)  1.34 us
    ppermute x2, waiting for transfers between devices, freq_sum(): lax.ppermute(send[shift - 1], 'freq', pairs).astype(jnp.float32)  0.95 us
  transfers between devices with their start and end apart: 4, of which 3 were waited for; matrix products, arithmetic and copies ran while one was open for 2% of the time, Pallas kernels for 23%

profile of v3, /device:TPU:0, one launch (start us, length us, event | category | flops | bytes accessed | tf_op | source)
XLA Modules:
  0.0 38.5 jit_solution(13002057831790474236)
XLA Ops:
  0.6 2.8 %first.1 = bf16[16,64,128]{2,1,0:T(8,128)(2,1)} custom-call(bf16[2,64,1024]{2,1,0:T(8,128)(2,1)} %bitcast.11, bf16[2,1,3,2,81]{4,3,2,1,0:T(2,128)(2,1)} %bitcast.18, s32[2,3,2,1024]{3,2,1,0:T(2,128)} %bitcast.12, s32[2,3,2,1024]{3,2,1,0:T(2,128)} %bitcast.15), custom_call_target="tpu_custom_call" | custom-call | flops 603979776 | bytes 1048576 | tf_op jit(solution)/shard_map/first/pallas_call | solution.py:397
  3.5 8.3 %all-to-all-start = ((bf16[16,64,128]{2,1,0:T(8,128)(2,1)}), bf16[16,64,128]{2,1,0:T(8,128)(2,1)S(1)}, u32[]{:S(2)}, u32[]{:S(2)}) async-start(bf16[16,64,128]{2,1,0:T(8,128)(2,1)} %first.1), calls=%async_computation | async-start | bytes 524288 | tf_op jit(solution)/shard_map/all_to_all | solution.py:443
  11.8 4.9 %prepare_middle.1 = (bf16[8,128,768]{2,1,0:T(8,128)(2,1)S(1)}, bf16[8,128,768]{2,1,0:T(8,128)(2,1)S(1)}, f32[64,128]{1,0:T(8,128)S(1)}) custom-call(bf16[2,1,3,2,81]{4,3,2,1,0:T(2,128)(2,1)} %bitcast.19, s32[2,3,2,1024]{3,2,1,0:T(2,128)} %bitcast.13, s32[2,3,2,1024]{3,2,1,0:T(2,128)} %bitcast.16, s32[2,64,64]{2,1,0:T(8,128)} %aperture_hbm.3), custom_call_target="tpu_custom_call" | custom-call | flops 301989888 | bytes 1048576 | tf_op jit(solution)/shard_map/prepare_middle/pallas_call | solution.py:397
  16.7 5.0 %all-to-all-done.moved_ref = bf16[16,64,128]{2,1,0:T(8,128)(2,1)S(1)} async-done(((bf16[16,64,128]{2,1,0:T(8,128)(2,1)}), bf16[16,64,128]{2,1,0:T(8,128)(2,1)S(1)}, u32[]{:S(2)}, u32[]{:S(2)}) %all-to-all-start) | async-done | bytes 262176 | tf_op jit(solution)/shard_map/all_to_all | solution.py:443
  21.7 1.8 %middle.1 = (bf16[16,64,128]{2,1,0:T(8,128)(2,1)}, bf16[1024,128]{1,0:T(8,128)(2,1)}) custom-call(bf16[16,64,128]{2,1,0:T(8,128)(2,1)S(1)} %all-to-all-done.moved_ref, bf16[8,128,768]{2,1,0:T(8,128)(2,1)S(1)} %get-tuple-element.15.second_ref, bf16[8,128,768]{2,1,0:T(8,128)(2,1)S(1)} %get-tuple-element.16.third_ref, f32[64,128]{1,0:T(8,128)S(1)} %get-tuple-element.17.keep_ref), custom_call_target="tpu_custom_call" | custom-call | flops 301989888 | bytes 1048576 | tf_op jit(solution)/shard_map/middle/pallas_call | solution.py:397
  23.5 3.6 %all-to-all-start.1 = ((bf16[16,64,128]{2,1,0:T(8,128)(2,1)}), bf16[16,64,128]{2,1,0:T(8,128)(2,1)S(1)}, u32[]{:S(2)}, u32[]{:S(2)}) async-start(bf16[16,64,128]{2,1,0:T(8,128)(2,1)} %get-tuple-element.18), calls=%async_computation.1 | async-start | bytes 524288 | tf_op jit(solution)/shard_map/all_to_all | solution.py:467
  27.0 1.1 %turn.1 = (bf16[1,64,512]{2,1,0:T(8,128)(2,1)S(1)}, f32[64,512]{1,0:T(8,128)S(1)}) custom-call(bf16[1024,128]{1,0:T(8,128)(2,1)} %get-tuple-element.19.shallow_hbm), custom_call_target="tpu_custom_call" | custom-call | flops 37748736 | bytes 1048576 | tf_op jit(solution)/shard_map/turn/pallas_call | solution.py:397
  28.1 0.1 collective-permute-start
  28.2 2.7 %prepare_last.1 = (bf16[8,768,128]{2,1,0:T(8,128)(2,1)S(1)}, f32[64,1024]{1,0:T(8,128)S(1)}) custom-call(bf16[2,1,3,2,81]{4,3,2,1,0:T(2,128)(2,1)} %bitcast.20, s32[2,3,2,1024]{3,2,1,0:T(2,128)} %bitcast.14, s32[2,3,2,1024]{3,2,1,0:T(2,128)} %bitcast.17, s32[2,64,64]{2,1,0:T(8,128)} %aperture_hbm.3), custom_call_target="tpu_custom_call" | custom-call | flops 301989888 | bytes 1048576 | tf_op jit(solution)/shard_map/prepare_last/pallas_call | solution.py:397
  30.9 0.0 collective-permute-done
  30.9 0.7 %convert_add_fusion.1 = f32[64,512]{1,0:T(8,128)} fusion(f32[64,512]{1,0:T(8,128)S(1)} %get-tuple-element.20, bf16[64,512]{1,0:T(8,128)(2,1)S(1)} %collective-permute-done), kind=kLoop, calls=%fused_computation.1 | loop fusion | flops 65536 | bytes 327680 | tf_op jit(solution)/shard_map/add | solution.py:413
  31.6 4.7 %all-to-all-done.1.field_ref = bf16[16,64,128]{2,1,0:T(8,128)(2,1)S(1)} async-done(((bf16[16,64,128]{2,1,0:T(8,128)(2,1)}), bf16[16,64,128]{2,1,0:T(8,128)(2,1)S(1)}, u32[]{:S(2)}, u32[]{:S(2)}) %all-to-all-start.1) | async-done | bytes 262176 | tf_op jit(solution)/shard_map/all_to_all | solution.py:467
  36.2 0.3 last_send.1
  36.5 0.1 collective-permute-start.1
  36.6 0.3 last_own.1
  36.9 0.9 %collective-permute-done.1 = bf16[64,512]{1,0:T(8,128)(2,1)S(1)} collective-permute-done((bf16[64,512]{1,0:T(8,128)(2,1)S(1)}, bf16[64,512]{1,0:T(8,128)(2,1)S(1)}, u32[]{:S(2)}, u32[]{:S(2)}) %collective-permute-start.1) | collective-permute-done | bytes 65568 | tf_op jit(solution)/shard_map/ppermute | solution.py:413
  37.9 0.7 %convert_add_fusion = f32[64,512]{1,0:T(8,128)} fusion(bf16[64,512]{1,0:T(8,128)(2,1)S(1)} %collective-permute-done.1, bf16[1,64,512]{2,1,0:T(8,128)(2,1)S(1)} %last_own.1), kind=kLoop, calls=%fused_computation | loop fusion | flops 98304 | bytes 262144 | tf_op jit(solution)/shard_map/add | solution.py:413
Async XLA Ops:
  3.5 18.2 %all-to-all-start = ((bf16[16,64,128]{2,1,0:T(8,128)(2,1)}), bf16[16,64,128]{2,1,0:T(8,128)(2,1)S(1)}, u32[]{:S(2)}, u32[]{:S(2)}) async-start(bf16[16,64,128]{2,1,0:T(8,128)(2,1)} %first.1), calls=%async_computation | async-start | bytes 524288 | tf_op jit(solution)/shard_map/all_to_all | solution.py:443
  23.5 12.8 %all-to-all-start.1 = ((bf16[16,64,128]{2,1,0:T(8,128)(2,1)}), bf16[16,64,128]{2,1,0:T(8,128)(2,1)S(1)}, u32[]{:S(2)}, u32[]{:S(2)}) async-start(bf16[16,64,128]{2,1,0:T(8,128)(2,1)} %get-tuple-element.18), calls=%async_computation.1 | async-start | bytes 524288 | tf_op jit(solution)/shard_map/all_to_all | solution.py:467
  28.1 2.8 %collective-permute-start = (bf16[64,512]{1,0:T(8,128)(2,1)S(1)}, bf16[64,512]{1,0:T(8,128)(2,1)S(1)}, u32[]{:S(2)}, u32[]{:S(2)}) collective-permute-start(bf16[64,512]{1,0:T(8,128)(2,1)S(1)} %bitcast.10), channel_id=1, source_target_pairs={{0,1},{1,0},{2,3},{3,2},{4,5},{5,4},{6,7},{7,6},{8,9},{9,8},{10,11... | collective-permute-start | bytes 196616 | tf_op jit(solution)/shard_map/ppermute | solution.py:413
  36.5 1.3 %collective-permute-start.1 = (bf16[64,512]{1,0:T(8,128)(2,1)S(1)}, bf16[64,512]{1,0:T(8,128)(2,1)S(1)}, u32[]{:S(2)}, u32[]{:S(2)}) collective-permute-start(bf16[64,512]{1,0:T(8,128)(2,1)S(1)} %bitcast.9), channel_id=1, source_target_pairs={{0,1},{1,0},{2,3},{3,2},{4,5},{5,4},{6,7},{7,6},{8,9},{9,8},{10,11... | collective-permute-start | bytes 196616 | tf_op jit(solution)/shard_map/ppermute | solution.py:413

commit v4 on v3

--- a/solution.py
+++ b/solution.py
@@ -29,6 +29,16 @@
         self.window = (1 + 2 * self.halo) * LANES
         self.blocks = aperture_shape[-1]
         self.blk = self.pos // self.blocks
+        self.chunks = LANES // self.rows
+        start = self.wide // 2 + self.wide // 8
+        self.start = start // self.chunks * self.chunks
+
+    def place(self, index):
+        return (index - self.start) % self.wide
+
+    def exchange(self, chunks):
+        order = [(self.start + i) % self.wide for i in range(self.wide)]
+        return lax.all_to_all(chunks, "wide", 0, 0, axis_index_groups=[order], tiled=True)
 
 
 def fill_taps(z, filt_ref, step, rows_ref):
@@ -76,8 +86,7 @@
 
 
 def sent(z, out_ref, out_hbm, sems, tile):
-    chunks = LANES // z.rows
-    place = pl.ds(tile * chunks, chunks)
+    place = pl.ds(z.place(tile * z.chunks), z.chunks)
     return pltpu.make_async_copy(out_ref.at[place], out_hbm.at[place], sems.at[tile])
 
 
@@ -173,9 +182,8 @@
         for k in range(z.bins):
             total = total + products[k][tile * z.rows : (tile + 1) * z.rows] * weights[k : k + 1]
         total = total.astype(jnp.bfloat16)
-        chunks = LANES // z.rows
-        for c in range(chunks):
-            out_ref[tile * chunks + c] = total[:, 2 * z.rows * c : 2 * z.rows * (c + 1)]
+        for c in range(z.chunks):
+            out_ref[z.place(tile * z.chunks + c)] = total[:, 2 * z.rows * c : 2 * z.rows * (c + 1)]
         send_out(z, out_ref, out_hbm, out_sems, tile)
     for tile in range(z.tiles):
         sent(z, out_ref, out_hbm, out_sems, tile).wait()
@@ -317,9 +325,12 @@
     for ref in (straight_ref, turned_ref, straight2_ref, turned2_ref):
         ref[:pad, :] = jnp.zeros((pad, width), jnp.bfloat16)
         ref[pad + z.pos :, :] = jnp.zeros((pad, width), jnp.bfloat16)
-    field = moved_ref[...].reshape(z.pos, width)
-    straight_ref[pad : pad + z.pos, :] = field
-    turned_ref[pad : pad + z.pos, :] = turned(z, field)
+    for tile in range(z.tiles):
+        place = slice(pad + tile * LANES, pad + (tile + 1) * LANES)
+        chunk = z.place(tile * z.chunks)
+        field = moved_ref[chunk : chunk + z.chunks].reshape(LANES, width)
+        straight_ref[place, :] = field
+        turned_ref[place, :] = turned(z, field)
     per_tile = LANES // z.blk
     for tile in range(z.tiles):
         place = slice(pad + tile * LANES, pad + (tile + 1) * LANES)
@@ -333,10 +344,10 @@
         straight2_ref.at[pl.ds(pad, z.pos)], shallow_hbm, shallow_sem.at[0]
     )
     shallow_copy.start()
-    chunks = LANES // z.rows
-    for tile in range(z.tiles):
+    for tile in range(z.tiles):
+        chunk = z.place(tile * z.chunks)
         third = over_sources(z, third_ref, straight2_ref, turned2_ref, tile).astype(jnp.bfloat16)
-        out_ref[tile * chunks : (tile + 1) * chunks] = third.reshape(chunks, z.rows, width)
+        out_ref[chunk : chunk + z.chunks] = third.reshape(z.chunks, z.rows, width)
         send_out(z, out_ref, out_hbm, out_sems, tile)
     for tile in range(z.tiles):
         sent(z, out_ref, out_hbm, out_sems, tile).wait()
@@ -372,7 +383,7 @@
     lhs_ref[:, :pad] = jnp.zeros((z.rows, pad), jnp.bfloat16)
     lhs_ref[:, pad + 2 * z.pos :] = jnp.zeros((z.rows, pad), jnp.bfloat16)
     for source in range(z.wide):
-        lhs_ref[:, pad + source * width : pad + (source + 1) * width] = field_ref[source]
+        lhs_ref[:, pad + source * width : pad + (source + 1) * width] = field_ref[z.place(source)]
     me = lax.axis_index("freq")
     tiles = z.tiles // z.freq
     for i, shift in enumerate(shifts):
@@ -440,7 +451,7 @@
         fetched=True,
         sent=(z.tiles,),
     )
-    moved = lax.all_to_all(first, "wide", 0, 0, tiled=True)
+    moved = z.exchange(first)
     second_band, third_band, shallow_keep = call(
         functools.partial(prepare_middle_kernel, z),
         (filters, vel_bins, blend_levels, aperture),
@@ -464,7 +475,7 @@
         "middle",
         sent=(z.tiles, 1),
     )
-    returned = lax.all_to_all(third, "wide", 0, 0, tiled=True)
+    returned = z.exchange(third)
     fourth_band, deep_keep = call(
         functools.partial(prepare_last_kernel, z),
         (filters, vel_bins, blend_levels, aperture),

time: 39 us -> 34.9 us (0.89)
  waiting for transfers between devices: 10.6 us -> 3.76 us
  starting transfers between devices: 12 us -> 14.8 us
    all_to_all x2, waiting for transfers between devices: 9.67 us -> 2.81 us  [exchange(): lax.all_to_all(chunks, 'wide', 0, 0, axis_index_groups=[order], tiled=True)]
    all_to_all x2, starting transfers between devices: 11.9 us -> 14.7 us  [exchange(): lax.all_to_all(chunks, 'wide', 0, 0, axis_index_groups=[order], tiled=True)]
  transfers between devices with their start and end apart: 4 -> 4, of which waited for: 3 -> 3; matrix products, arithmetic and copies ran while one was open for 2% -> 2% of each run, Pallas kernels for 23% -> 26%
where the time goes in v4:
time: 34.9 us; the launch traced here: 34.5 us
  starting transfers between devices  14.8 us (42%)
  Pallas kernels  13.8 us (40%)
  waiting for transfers between devices  3.76 us (11%)
  other arithmetic  1.34 us (4%)
  between operations  0.7 us (2%)
    all_to_all x2, starting transfers between devices, exchange(): lax.all_to_all(chunks, 'wide', 0, 0, axis_index_groups=[order], tiled=True)  14.7 us
    pallas_call x7, Pallas kernels, call(): pl.pallas_call(kernel, out_shape=[space(shape, dtype) for space, (shape,...  13.8 us
    all_to_all x2, waiting for transfers between devices, exchange(): lax.all_to_all(chunks, 'wide', 0, 0, axis_index_groups=[order], tiled=True)  2.81 us
    add x2, other arithmetic, freq_sum(): total + lax.ppermute(send[shift - 1], 'freq', pairs).astype(jnp.float32)  1.34 us
    ppermute x2, waiting for transfers between devices, freq_sum(): lax.ppermute(send[shift - 1], 'freq', pairs).astype(jnp.float32)  0.95 us
  transfers between devices with their start and end apart: 4, of which 3 were waited for; matrix products, arithmetic and copies ran while one was open for 2% of the time, Pallas kernels for 26%

profile of v4, /device:TPU:0, one launch (start us, length us, event | category | flops | bytes accessed | tf_op | source)
XLA Modules:
  0.0 34.5 jit_solution(10025223268867179050)
XLA Ops:
  0.6 2.8 %first.1 = bf16[16,64,128]{2,1,0:T(8,128)(2,1)} custom-call(bf16[2,64,1024]{2,1,0:T(8,128)(2,1)} %bitcast.11, bf16[2,1,3,2,81]{4,3,2,1,0:T(2,128)(2,1)} %bitcast.18, s32[2,3,2,1024]{3,2,1,0:T(2,128)} %bitcast.12, s32[2,3,2,1024]{3,2,1,0:T(2,128)} %bitcast.15), custom_call_target="tpu_custom_call" | custom-call | flops 603979776 | bytes 1048576 | tf_op jit(solution)/shard_map/first/pallas_call | solution.py:408
  3.5 8.8 %all-to-all-start = ((bf16[16,64,128]{2,1,0:T(8,128)(2,1)}), bf16[16,64,128]{2,1,0:T(8,128)(2,1)S(1)}, u32[]{:S(2)}, u32[]{:S(2)}) async-start(bf16[16,64,128]{2,1,0:T(8,128)(2,1)} %first.1), calls=%async_computation | async-start | bytes 524288 | tf_op jit(solution)/shard_map/all_to_all | solution.py:41
  12.3 4.9 %prepare_middle.1 = (bf16[8,128,768]{2,1,0:T(8,128)(2,1)S(1)}, bf16[8,128,768]{2,1,0:T(8,128)(2,1)S(1)}, f32[64,128]{1,0:T(8,128)S(1)}) custom-call(bf16[2,1,3,2,81]{4,3,2,1,0:T(2,128)(2,1)} %bitcast.19, s32[2,3,2,1024]{3,2,1,0:T(2,128)} %bitcast.13, s32[2,3,2,1024]{3,2,1,0:T(2,128)} %bitcast.16, s32[2,64,64]{2,1,0:T(8,128)} %aperture_hbm.3), custom_call_target="tpu_custom_call" | custom-call | flops 301989888 | bytes 1048576 | tf_op jit(solution)/shard_map/prepare_middle/pallas_call | solution.py:408
  17.1 2.0 %all-to-all-done.moved_ref = bf16[16,64,128]{2,1,0:T(8,128)(2,1)S(1)} async-done(((bf16[16,64,128]{2,1,0:T(8,128)(2,1)}), bf16[16,64,128]{2,1,0:T(8,128)(2,1)S(1)}, u32[]{:S(2)}, u32[]{:S(2)}) %all-to-all-start) | async-done | bytes 262176 | tf_op jit(solution)/shard_map/all_to_all | solution.py:41
  19.2 1.8 %middle.1 = (bf16[16,64,128]{2,1,0:T(8,128)(2,1)}, bf16[1024,128]{1,0:T(8,128)(2,1)}) custom-call(bf16[16,64,128]{2,1,0:T(8,128)(2,1)S(1)} %all-to-all-done.moved_ref, bf16[8,128,768]{2,1,0:T(8,128)(2,1)S(1)} %get-tuple-element.15.second_ref, bf16[8,128,768]{2,1,0:T(8,128)(2,1)S(1)} %get-tuple-element.16.third_ref, f32[64,128]{1,0:T(8,128)S(1)} %get-tuple-element.17.keep_ref), custom_call_target="tpu_custom_call" | custom-call | flops 301989888 | bytes 1048576 | tf_op jit(solution)/shard_map/middle/pallas_call | solution.py:408
  21.0 5.9 %all-to-all-start.1 = ((bf16[16,64,128]{2,1,0:T(8,128)(2,1)}), bf16[16,64,128]{2,1,0:T(8,128)(2,1)S(1)}, u32[]{:S(2)}, u32[]{:S(2)}) async-start(bf16[16,64,128]{2,1,0:T(8,128)(2,1)} %get-tuple-element.18), calls=%async_computation.1 | async-start | bytes 524288 | tf_op jit(solution)/shard_map/all_to_all | solution.py:41
  26.8 1.1 %turn.1 = (bf16[1,64,512]{2,1,0:T(8,128)(2,1)S(1)}, f32[64,512]{1,0:T(8,128)S(1)}) custom-call(bf16[1024,128]{1,0:T(8,128)(2,1)} %get-tuple-element.19.shallow_hbm), custom_call_target="tpu_custom_call" | custom-call | flops 37748736 | bytes 1048576 | tf_op jit(solution)/shard_map/turn/pallas_call | solution.py:408
  28.0 0.1 collective-permute-start
  28.0 2.7 %prepare_last.1 = (bf16[8,768,128]{2,1,0:T(8,128)(2,1)S(1)}, f32[64,1024]{1,0:T(8,128)S(1)}) custom-call(bf16[2,1,3,2,81]{4,3,2,1,0:T(2,128)(2,1)} %bitcast.20, s32[2,3,2,1024]{3,2,1,0:T(2,128)} %bitcast.14, s32[2,3,2,1024]{3,2,1,0:T(2,128)} %bitcast.17, s32[2,64,64]{2,1,0:T(8,128)} %aperture_hbm.3), custom_call_target="tpu_custom_call" | custom-call | flops 301989888 | bytes 1048576 | tf_op jit(solution)/shard_map/prepare_last/pallas_call | solution.py:408
  30.7 0.0 collective-permute-done
  30.7 0.7 %convert_add_fusion.1 = f32[64,512]{1,0:T(8,128)} fusion(f32[64,512]{1,0:T(8,128)S(1)} %get-tuple-element.20, bf16[64,512]{1,0:T(8,128)(2,1)S(1)} %collective-permute-done), kind=kLoop, calls=%fused_computation.1 | loop fusion | flops 65536 | bytes 327680 | tf_op jit(solution)/shard_map/add | solution.py:424
  31.4 0.8 %all-to-all-done.1.field_ref = bf16[16,64,128]{2,1,0:T(8,128)(2,1)S(1)} async-done(((bf16[16,64,128]{2,1,0:T(8,128)(2,1)}), bf16[16,64,128]{2,1,0:T(8,128)(2,1)S(1)}, u32[]{:S(2)}, u32[]{:S(2)}) %all-to-all-start.1) | async-done | bytes 262176 | tf_op jit(solution)/shard_map/all_to_all | solution.py:41
  32.2 0.3 last_send.1
  32.5 0.1 collective-permute-start.1
  32.6 0.3 last_own.1
  32.9 0.9 %collective-permute-done.1 = bf16[64,512]{1,0:T(8,128)(2,1)S(1)} collective-permute-done((bf16[64,512]{1,0:T(8,128)(2,1)S(1)}, bf16[64,512]{1,0:T(8,128)(2,1)S(1)}, u32[]{:S(2)}, u32[]{:S(2)}) %collective-permute-start.1) | collective-permute-done | bytes 65568 | tf_op jit(solution)/shard_map/ppermute | solution.py:424
  33.8 0.7 %convert_add_fusion = f32[64,512]{1,0:T(8,128)} fusion(bf16[64,512]{1,0:T(8,128)(2,1)S(1)} %collective-permute-done.1, bf16[1,64,512]{2,1,0:T(8,128)(2,1)S(1)} %last_own.1), kind=kLoop, calls=%fused_computation | loop fusion | flops 98304 | bytes 262144 | tf_op jit(solution)/shard_map/add | solution.py:424
Async XLA Ops:
  3.5 15.7 %all-to-all-start = ((bf16[16,64,128]{2,1,0:T(8,128)(2,1)}), bf16[16,64,128]{2,1,0:T(8,128)(2,1)S(1)}, u32[]{:S(2)}, u32[]{:S(2)}) async-start(bf16[16,64,128]{2,1,0:T(8,128)(2,1)} %first.1), calls=%async_computation | async-start | bytes 524288 | tf_op jit(solution)/shard_map/all_to_all | solution.py:41
  21.0 11.2 %all-to-all-start.1 = ((bf16[16,64,128]{2,1,0:T(8,128)(2,1)}), bf16[16,64,128]{2,1,0:T(8,128)(2,1)S(1)}, u32[]{:S(2)}, u32[]{:S(2)}) async-start(bf16[16,64,128]{2,1,0:T(8,128)(2,1)} %get-tuple-element.18), calls=%async_computation.1 | async-start | bytes 524288 | tf_op jit(solution)/shard_map/all_to_all | solution.py:41
  28.0 2.7 %collective-permute-start = (bf16[64,512]{1,0:T(8,128)(2,1)S(1)}, bf16[64,512]{1,0:T(8,128)(2,1)S(1)}, u32[]{:S(2)}, u32[]{:S(2)}) collective-permute-start(bf16[64,512]{1,0:T(8,128)(2,1)S(1)} %bitcast.10), channel_id=1, source_target_pairs={{0,1},{1,0},{2,3},{3,2},{4,5},{5,4},{6,7},{7,6},{8,9},{9,8},{10,11... | collective-permute-start | bytes 196616 | tf_op jit(solution)/shard_map/ppermute | solution.py:424
  32.5 1.3 %collective-permute-start.1 = (bf16[64,512]{1,0:T(8,128)(2,1)S(1)}, bf16[64,512]{1,0:T(8,128)(2,1)S(1)}, u32[]{:S(2)}, u32[]{:S(2)}) collective-permute-start(bf16[64,512]{1,0:T(8,128)(2,1)S(1)} %bitcast.9), channel_id=1, source_target_pairs={{0,1},{1,0},{2,3},{3,2},{4,5},{5,4},{6,7},{7,6},{8,9},{9,8},{10,11... | collective-permute-start | bytes 196616 | tf_op jit(solution)/shard_map/ppermute | solution.py:424

commit v5 on v4

--- a/solution.py
+++ b/solution.py
@@ -109,6 +109,7 @@
     table_ref,
     band_ref,
     lhs_ref,
+    acc_ref,
     out_ref,
     out_sems,
     sems,
@@ -165,26 +166,29 @@
                 lhs_ref[tile * z.rows : (tile + 1) * z.rows, place : place + LANES] = piece
     lane = lax.broadcasted_iota(jnp.int32, (8, LANES), 1)
     points = [chunk_order(z, lane + v * LANES)[1] for v in range(2)]
-    products = [
-        jnp.dot(
+    columns = []
+    for tile in range(z.tiles):
+        weights = table_ref[:, tile * LANES : (tile + 1) * LANES]
+        picked = [jnp.take_along_axis(weights, p, axis=1, mode="promise_in_bounds") for p in points]
+        columns.append(jnp.concatenate(picked, axis=1))
+    for k in range(z.bins):
+        product = jnp.dot(
             lhs_ref[...],
             band_ref[:, 2 * k * LANES : 2 * (k + 1) * LANES],
             preferred_element_type=jnp.float32,
         )
-        for k in range(z.bins)
-    ]
-    for tile in range(z.tiles):
-        weights = table_ref[:, tile * LANES : (tile + 1) * LANES]
-        weights = jnp.concatenate(
-            [jnp.take_along_axis(weights, p, axis=1, mode="promise_in_bounds") for p in points], axis=1
-        )
-        total = 0.0
-        for k in range(z.bins):
-            total = total + products[k][tile * z.rows : (tile + 1) * z.rows] * weights[k : k + 1]
-        total = total.astype(jnp.bfloat16)
-        for c in range(z.chunks):
-            out_ref[z.place(tile * z.chunks + c)] = total[:, 2 * z.rows * c : 2 * z.rows * (c + 1)]
-        send_out(z, out_ref, out_hbm, out_sems, tile)
+        for tile in range(z.tiles):
+            rows = slice(tile * z.rows, (tile + 1) * z.rows)
+            part = product[rows] * columns[tile][k : k + 1]
+            if k:
+                part = part + acc_ref[rows, :]
+            if k < z.bins - 1:
+                acc_ref[rows, :] = part
+            else:
+                total = part.astype(jnp.bfloat16)
+                for c in range(z.chunks):
+                    out_ref[z.place(tile * z.chunks + c)] = total[:, 2 * z.rows * c : 2 * z.rows * (c + 1)]
+                send_out(z, out_ref, out_hbm, out_sems, tile)
     for tile in range(z.tiles):
         sent(z, out_ref, out_hbm, out_sems, tile).wait()
 
@@ -281,6 +285,10 @@
                 for k in range(z.bins):
                     total = total + taps[k] * table_ref[k : k + 1, tile * LANES : (tile + 1) * LANES]
                 total = total if part == 0 else -total
+                if tile < z.halo:
+                    total = jnp.where(block * z.rows >= (z.halo - tile) * LANES, total, 0.0)
+                if tile >= z.tiles - z.halo:
+                    total = jnp.where(block * z.rows < (z.tiles + z.halo - tile) * LANES, total, 0.0)
                 fourth_ref[tile, pl.ds(place, z.rows), :] = total.astype(jnp.bfloat16)
 
     offset = lax.axis_index("wide") * z.rows
@@ -296,12 +304,14 @@
     return jnp.concatenate([-block[:, z.rows :], block[:, : z.rows]], axis=1)
 
 
-def over_sources(z, band_ref, straight_ref, turned_ref, tile):
-    start = tile * LANES
-    rhs = jnp.concatenate(
-        [straight_ref[start : start + z.window, :], turned_ref[start : start + z.window, :]], axis=0
-    )
-    return jnp.dot(band_ref[tile], rhs, preferred_element_type=jnp.float32)
+def over_sources(z, band_ref, straight, turn, tile):
+    low, high = max(tile - z.halo, 0), min(tile + z.halo, z.tiles - 1)
+    reach = range(low, high + 1)
+    rhs = jnp.concatenate([straight(j) for j in reach] + [turn(j) for j in reach], axis=0)
+    width = len(reach) * LANES
+    starts = [part * z.window + (low - tile + z.halo) * LANES for part in range(2)]
+    band = jnp.concatenate([band_ref[tile, :, start : start + width] for start in starts], axis=1)
+    return jnp.dot(band, rhs, preferred_element_type=jnp.float32)
 
 
 def middle_kernel(
@@ -312,7 +322,6 @@
     keep_ref,
     out_hbm,
     shallow_hbm,
-    straight_ref,
     turned_ref,
     straight2_ref,
     turned2_ref,
@@ -320,33 +329,29 @@
     out_sems,
     shallow_sem,
 ):
-    pad = z.halo * LANES
     width = 2 * z.rows
-    for ref in (straight_ref, turned_ref, straight2_ref, turned2_ref):
-        ref[:pad, :] = jnp.zeros((pad, width), jnp.bfloat16)
-        ref[pad + z.pos :, :] = jnp.zeros((pad, width), jnp.bfloat16)
-    for tile in range(z.tiles):
-        place = slice(pad + tile * LANES, pad + (tile + 1) * LANES)
+
+    def field(tile):
         chunk = z.place(tile * z.chunks)
-        field = moved_ref[chunk : chunk + z.chunks].reshape(LANES, width)
-        straight_ref[place, :] = field
-        turned_ref[place, :] = turned(z, field)
+        return moved_ref[chunk : chunk + z.chunks].reshape(LANES, width)
+
+    for tile in range(z.tiles):
+        turned_ref[tile] = turned(z, field(tile))
     per_tile = LANES // z.blk
     for tile in range(z.tiles):
-        place = slice(pad + tile * LANES, pad + (tile + 1) * LANES)
         mask = keep_ref[tile * per_tile : (tile + 1) * per_tile, :]
         mask = jnp.broadcast_to(mask[:, None, :], (per_tile, z.blk, width)).reshape(LANES, width)
-        shallow = over_sources(z, second_ref, straight_ref, turned_ref, tile) * mask
+        shallow = over_sources(z, second_ref, field, lambda j: turned_ref[j], tile) * mask
         shallow = shallow.astype(jnp.bfloat16)
-        straight2_ref[place, :] = shallow
-        turned2_ref[place, :] = turned(z, shallow)
-    shallow_copy = pltpu.make_async_copy(
-        straight2_ref.at[pl.ds(pad, z.pos)], shallow_hbm, shallow_sem.at[0]
-    )
+        straight2_ref[tile * LANES : (tile + 1) * LANES, :] = shallow
+        turned2_ref[tile] = turned(z, shallow)
+    shallow_copy = pltpu.make_async_copy(straight2_ref, shallow_hbm, shallow_sem.at[0])
     shallow_copy.start()
     for tile in range(z.tiles):
         chunk = z.place(tile * z.chunks)
-        third = over_sources(z, third_ref, straight2_ref, turned2_ref, tile).astype(jnp.bfloat16)
+        third = over_sources(
+            z, third_ref, lambda j: straight2_ref[j * LANES : (j + 1) * LANES, :], lambda j: turned2_ref[j], tile
+        ).astype(jnp.bfloat16)
         out_ref[chunk : chunk + z.chunks] = third.reshape(z.chunks, z.rows, width)
         send_out(z, out_ref, out_hbm, out_sems, tile)
     for tile in range(z.tiles):
@@ -377,21 +382,18 @@
     split_sum(z, real_ref, send_ref, own_ref)
 
 
-def last_kernel(z, shifts, field_ref, fourth_ref, keep_ref, out_ref, lhs_ref):
-    pad = 2 * z.halo * LANES
-    width = 2 * z.rows
-    lhs_ref[:, :pad] = jnp.zeros((z.rows, pad), jnp.bfloat16)
-    lhs_ref[:, pad + 2 * z.pos :] = jnp.zeros((z.rows, pad), jnp.bfloat16)
-    for source in range(z.wide):
-        lhs_ref[:, pad + source * width : pad + (source + 1) * width] = field_ref[z.place(source)]
+def last_kernel(z, shifts, field_ref, fourth_ref, keep_ref, out_ref):
     me = lax.axis_index("freq")
     tiles = z.tiles // z.freq
     for i, shift in enumerate(shifts):
         for j in range(tiles):
             tile = lax.rem(me + shift, z.freq) * tiles + j
-            window = pl.ds(pl.multiple_of(2 * tile * LANES, 2 * LANES), 2 * z.window)
+            first = (tile - z.halo) * z.chunks - z.start + 2 * z.wide
+            pieces = [field_ref[lax.rem(first + c, z.wide)] for c in range((1 + 2 * z.halo) * z.chunks)]
             columns = pl.ds(pl.multiple_of(tile * LANES, LANES), LANES)
-            fourth = jnp.dot(lhs_ref[:, window], fourth_ref[tile], preferred_element_type=jnp.float32)
+            fourth = jnp.dot(
+                jnp.concatenate(pieces, axis=1), fourth_ref[tile], preferred_element_type=jnp.float32
+            )
             out_ref[i, :, j * LANES : (j + 1) * LANES] = (fourth * keep_ref[:, columns]).astype(out_ref.dtype)
 
 
@@ -445,6 +447,7 @@
         + [
             ((2 * z.window, 2 * z.bins * LANES), bf16),
             ((z.tiles * z.rows, 2 * z.window), bf16),
+            ((z.tiles * z.rows, 2 * LANES), f32),
         ],
         2 * dense,
         "first",
@@ -465,12 +468,11 @@
         "prepare_middle",
         fetched=True,
     )
-    padded = z.pos + 2 * z.halo * LANES
     third, shallow = call(
         functools.partial(middle_kernel, z),
         (moved, second_band, third_band, shallow_keep),
         [chunks, ((z.pos, width), bf16)],
-        [((padded, width), bf16)] * 4,
+        [((z.tiles, LANES, width), bf16), ((z.pos, width), bf16), ((z.tiles, LANES, width), bf16)],
         dense,
         "middle",
         sent=(z.tiles, 1),
@@ -506,7 +508,7 @@
             functools.partial(last_kernel, z, shifts),
             (returned, fourth_band, deep_keep),
             [part],
-            [((z.rows, 2 * padded), bf16)],
+            [],
             dense // 8,
             "last_own" if len(deep) else "last_send",
         )

time: 34.9 us -> 34.8 us (level)
  no operation moved by 1% of the time
where the time goes in v5:
time: 34.8 us; the launch traced here: 34.3 us
  starting transfers between devices  14.8 us (43%)
  Pallas kernels  13.7 us (39%)
  waiting for transfers between devices  3.76 us (11%)
  other arithmetic  1.34 us (4%)
  between operations  0.7 us (2%)
    all_to_all x2, starting transfers between devices, exchange(): lax.all_to_all(chunks, 'wide', 0, 0, axis_index_groups=[order], tiled=True)  14.7 us
    pallas_call x7, Pallas kernels, call(): pl.pallas_call(kernel, out_shape=[space(shape, dtype) for space, (shape,...  13.7 us
    all_to_all x2, waiting for transfers between devices, exchange(): lax.all_to_all(chunks, 'wide', 0, 0, axis_index_groups=[order], tiled=True)  2.8 us
    add x2, other arithmetic, freq_sum(): total + lax.ppermute(send[shift - 1], 'freq', pairs).astype(jnp.float32)  1.34 us
    ppermute x2, waiting for transfers between devices, freq_sum(): lax.ppermute(send[shift - 1], 'freq', pairs).astype(jnp.float32)  0.96 us
  transfers between devices with their start and end apart: 4, of which 3 were waited for; matrix products, arithmetic and copies ran while one was open for 2% of the time, Pallas kernels for 26%

profile of v5, /device:TPU:0, one launch (start us, length us, event | category | flops | bytes accessed | tf_op | source)
XLA Modules:
  0.0 34.3 jit_solution(13045813277595243721)
XLA Ops:
  0.6 2.8 %first.1 = bf16[16,64,128]{2,1,0:T(8,128)(2,1)} custom-call(bf16[2,64,1024]{2,1,0:T(8,128)(2,1)} %bitcast.11, bf16[2,1,3,2,81]{4,3,2,1,0:T(2,128)(2,1)} %bitcast.18, s32[2,3,2,1024]{3,2,1,0:T(2,128)} %bitcast.12, s32[2,3,2,1024]{3,2,1,0:T(2,128)} %bitcast.15), custom_call_target="tpu_custom_call" | custom-call | flops 603979776 | bytes 1048576 | tf_op jit(solution)/shard_map/first/pallas_call | solution.py:410
  3.5 8.8 %all-to-all-start = ((bf16[16,64,128]{2,1,0:T(8,128)(2,1)}), bf16[16,64,128]{2,1,0:T(8,128)(2,1)S(1)}, u32[]{:S(2)}, u32[]{:S(2)}) async-start(bf16[16,64,128]{2,1,0:T(8,128)(2,1)} %first.1), calls=%async_computation | async-start | bytes 524288 | tf_op jit(solution)/shard_map/all_to_all | solution.py:41
  12.3 4.9 %prepare_middle.1 = (bf16[8,128,768]{2,1,0:T(8,128)(2,1)S(1)}, bf16[8,128,768]{2,1,0:T(8,128)(2,1)S(1)}, f32[64,128]{1,0:T(8,128)S(1)}) custom-call(bf16[2,1,3,2,81]{4,3,2,1,0:T(2,128)(2,1)} %bitcast.19, s32[2,3,2,1024]{3,2,1,0:T(2,128)} %bitcast.13, s32[2,3,2,1024]{3,2,1,0:T(2,128)} %bitcast.16, s32[2,64,64]{2,1,0:T(8,128)} %aperture_hbm.3), custom_call_target="tpu_custom_call" | custom-call | flops 301989888 | bytes 1048576 | tf_op jit(solution)/shard_map/prepare_middle/pallas_call | solution.py:410
  17.1 2.0 %all-to-all-done.moved_ref = bf16[16,64,128]{2,1,0:T(8,128)(2,1)S(1)} async-done(((bf16[16,64,128]{2,1,0:T(8,128)(2,1)}), bf16[16,64,128]{2,1,0:T(8,128)(2,1)S(1)}, u32[]{:S(2)}, u32[]{:S(2)}) %all-to-all-start) | async-done | bytes 262176 | tf_op jit(solution)/shard_map/all_to_all | solution.py:41
  19.2 1.7 %middle.1 = (bf16[16,64,128]{2,1,0:T(8,128)(2,1)}, bf16[1024,128]{1,0:T(8,128)(2,1)}) custom-call(bf16[16,64,128]{2,1,0:T(8,128)(2,1)S(1)} %all-to-all-done.moved_ref, bf16[8,128,768]{2,1,0:T(8,128)(2,1)S(1)} %get-tuple-element.15.second_ref, bf16[8,128,768]{2,1,0:T(8,128)(2,1)S(1)} %get-tuple-element.16.third_ref, f32[64,128]{1,0:T(8,128)S(1)} %get-tuple-element.17.keep_ref), custom_call_target="tpu_custom_call" | custom-call | flops 301989888 | bytes 1048576 | tf_op jit(solution)/shard_map/middle/pallas_call | solution.py:410
  20.9 5.9 %all-to-all-start.1 = ((bf16[16,64,128]{2,1,0:T(8,128)(2,1)}), bf16[16,64,128]{2,1,0:T(8,128)(2,1)S(1)}, u32[]{:S(2)}, u32[]{:S(2)}) async-start(bf16[16,64,128]{2,1,0:T(8,128)(2,1)} %get-tuple-element.18), calls=%async_computation.1 | async-start | bytes 524288 | tf_op jit(solution)/shard_map/all_to_all | solution.py:41
  26.8 1.1 %turn.1 = (bf16[1,64,512]{2,1,0:T(8,128)(2,1)S(1)}, f32[64,512]{1,0:T(8,128)S(1)}) custom-call(bf16[1024,128]{1,0:T(8,128)(2,1)} %get-tuple-element.19.shallow_hbm), custom_call_target="tpu_custom_call" | custom-call | flops 37748736 | bytes 1048576 | tf_op jit(solution)/shard_map/turn/pallas_call | solution.py:410
  27.9 0.1 collective-permute-start
  28.0 2.7 %prepare_last.1 = (bf16[8,768,128]{2,1,0:T(8,128)(2,1)S(1)}, f32[64,1024]{1,0:T(8,128)S(1)}) custom-call(bf16[2,1,3,2,81]{4,3,2,1,0:T(2,128)(2,1)} %bitcast.20, s32[2,3,2,1024]{3,2,1,0:T(2,128)} %bitcast.14, s32[2,3,2,1024]{3,2,1,0:T(2,128)} %bitcast.17, s32[2,64,64]{2,1,0:T(8,128)} %aperture_hbm.3), custom_call_target="tpu_custom_call" | custom-call | flops 301989888 | bytes 1048576 | tf_op jit(solution)/shard_map/prepare_last/pallas_call | solution.py:410
  30.6 0.0 collective-permute-done
  30.6 0.7 %convert_add_fusion.1 = f32[64,512]{1,0:T(8,128)} fusion(f32[64,512]{1,0:T(8,128)S(1)} %get-tuple-element.20, bf16[64,512]{1,0:T(8,128)(2,1)S(1)} %collective-permute-done), kind=kLoop, calls=%fused_computation.1 | loop fusion | flops 65536 | bytes 327680 | tf_op jit(solution)/shard_map/add | solution.py:426
  31.3 0.8 %all-to-all-done.1.field_ref = bf16[16,64,128]{2,1,0:T(8,128)(2,1)S(1)} async-done(((bf16[16,64,128]{2,1,0:T(8,128)(2,1)}), bf16[16,64,128]{2,1,0:T(8,128)(2,1)S(1)}, u32[]{:S(2)}, u32[]{:S(2)}) %all-to-all-start.1) | async-done | bytes 262176 | tf_op jit(solution)/shard_map/all_to_all | solution.py:41
  32.1 0.3 last_send.1
  32.4 0.1 collective-permute-start.1
  32.4 0.3 last_own.1
  32.7 1.0 %collective-permute-done.1 = bf16[64,512]{1,0:T(8,128)(2,1)S(1)} collective-permute-done((bf16[64,512]{1,0:T(8,128)(2,1)S(1)}, bf16[64,512]{1,0:T(8,128)(2,1)S(1)}, u32[]{:S(2)}, u32[]{:S(2)}) %collective-permute-start.1) | collective-permute-done | bytes 65568 | tf_op jit(solution)/shard_map/ppermute | solution.py:426
  33.7 0.7 %convert_add_fusion = f32[64,512]{1,0:T(8,128)} fusion(bf16[64,512]{1,0:T(8,128)(2,1)S(1)} %collective-permute-done.1, bf16[1,64,512]{2,1,0:T(8,128)(2,1)S(1)} %last_own.1), kind=kLoop, calls=%fused_computation | loop fusion | flops 98304 | bytes 262144 | tf_op jit(solution)/shard_map/add | solution.py:426
Async XLA Ops:
  3.5 15.7 %all-to-all-start = ((bf16[16,64,128]{2,1,0:T(8,128)(2,1)}), bf16[16,64,128]{2,1,0:T(8,128)(2,1)S(1)}, u32[]{:S(2)}, u32[]{:S(2)}) async-start(bf16[16,64,128]{2,1,0:T(8,128)(2,1)} %first.1), calls=%async_computation | async-start | bytes 524288 | tf_op jit(solution)/shard_map/all_to_all | solution.py:41
  20.9 11.2 %all-to-all-start.1 = ((bf16[16,64,128]{2,1,0:T(8,128)(2,1)}), bf16[16,64,128]{2,1,0:T(8,128)(2,1)S(1)}, u32[]{:S(2)}, u32[]{:S(2)}) async-start(bf16[16,64,128]{2,1,0:T(8,128)(2,1)} %get-tuple-element.18), calls=%async_computation.1 | async-start | bytes 524288 | tf_op jit(solution)/shard_map/all_to_all | solution.py:41
  27.9 2.8 %collective-permute-start = (bf16[64,512]{1,0:T(8,128)(2,1)S(1)}, bf16[64,512]{1,0:T(8,128)(2,1)S(1)}, u32[]{:S(2)}, u32[]{:S(2)}) collective-permute-start(bf16[64,512]{1,0:T(8,128)(2,1)S(1)} %bitcast.10), channel_id=1, source_target_pairs={{0,1},{1,0},{2,3},{3,2},{4,5},{5,4},{6,7},{7,6},{8,9},{9,8},{10,11... | collective-permute-start | bytes 196616 | tf_op jit(solution)/shard_map/ppermute | solution.py:426
  32.4 1.3 %collective-permute-start.1 = (bf16[64,512]{1,0:T(8,128)(2,1)S(1)}, bf16[64,512]{1,0:T(8,128)(2,1)S(1)}, u32[]{:S(2)}, u32[]{:S(2)}) collective-permute-start(bf16[64,512]{1,0:T(8,128)(2,1)S(1)} %bitcast.9), channel_id=1, source_target_pairs={{0,1},{1,0},{2,3},{3,2},{4,5},{5,4},{6,7},{7,6},{8,9},{9,8},{10,11... | collective-permute-start | bytes 196616 | tf_op jit(solution)/shard_map/ppermute | solution.py:426

commit v6 on v5

--- a/solution.py
+++ b/solution.py
@@ -110,6 +110,7 @@
     band_ref,
     lhs_ref,
     acc_ref,
+    source_ref,
     out_ref,
     out_sems,
     sems,
@@ -119,17 +120,20 @@
     )
     group_rows = LANES // 2 // z.side
     window_rows = z.window // z.side
+    lift = z.half - z.halo * z.tile_rows
+    steps = window_rows - group_rows
+    half_lanes = LANES // 2
     lane = lax.broadcasted_iota(jnp.int32, (z.side, LANES), 1)
     part, point = chunk_order(z, lane)
-    out_y = point // z.side - (z.half - z.halo * z.tile_rows)
     b = lax.broadcasted_iota(jnp.int32, (z.side, LANES), 0) - point % z.side + z.half
-    b_valid = (b >= 0) & (b < z.taps)
-    base = b - out_y * z.taps
-    is_real = part == 0
-    indices = []
-    for y in range(window_rows - group_rows):
-        valid = b_valid & (out_y <= y) & (out_y > y - z.taps)
-        indices.append(jnp.where(valid, base + y * z.taps, LANES - 1))
+    index = (group_rows - 1 - point // z.side) * z.taps + b + part * half_lanes
+    index = jnp.where((b >= 0) & (b < z.taps), index, LANES - 1)
+    lane = lax.broadcasted_iota(jnp.int32, (16, LANES), 1)
+    row = lax.broadcasted_iota(jnp.int32, (16, LANES), 0)
+    is_low = lane < half_lanes
+    inside = jnp.where(is_low, lane, lane - half_lanes)
+    tap = (row - (group_rows - 1) + lift) * z.taps + inside
+    picked = jnp.where((inside < group_rows * z.taps) & (tap >= 0) & (tap < z.tap_count), tap, LANES - 1)
     empty = jnp.zeros((group_rows * z.side, LANES), jnp.bfloat16)
     for k in range(z.bins):
         for half in range(2):
@@ -140,11 +144,12 @@
     fill_taps(z, filt_ref, 0, taps_ref)
     for k in range(z.bins):
         columns = 2 * k * LANES
-        for y, index in enumerate(indices):
-            real, imag = spread(taps_ref, k, index), spread(taps_ref, z.bins + k, index)
-            blocks = (jnp.where(is_real, real, imag), jnp.where(is_real, -imag, real))
+        real, imag = spread(taps_ref, k, picked), spread(taps_ref, z.bins + k, picked)
+        source_ref[2 * k] = jnp.where(is_low, real, imag)
+        source_ref[2 * k + 1] = jnp.where(is_low, -imag, real)
+        for y in range(steps):
             for half in range(2):
-                block = blocks[half].astype(jnp.bfloat16)
+                block = spread(source_ref.at[2 * k + half], y, index).astype(jnp.bfloat16)
                 top = half * z.window + y * z.side
                 band_ref[top : top + z.side, columns : columns + LANES] = block
                 top += group_rows * z.side
@@ -448,6 +453,7 @@
             ((2 * z.window, 2 * z.bins * LANES), bf16),
             ((z.tiles * z.rows, 2 * z.window), bf16),
             ((z.tiles * z.rows, 2 * LANES), f32),
+            ((2 * z.bins, 16, LANES), f32),
         ],
         2 * dense,
         "first",

time: 34.8 us -> 34.8 us (level)
  no operation moved by 1% of the time
where the time goes in v6:
time: 34.8 us; the launch traced here: 34.3 us
  starting transfers between devices  14.8 us (43%)
  Pallas kernels  13.7 us (39%)
  waiting for transfers between devices  3.76 us (11%)
  other arithmetic  1.34 us (4%)
  between operations  0.7 us (2%)
    all_to_all x2, starting transfers between devices, exchange(): lax.all_to_all(chunks, 'wide', 0, 0, axis_index_groups=[order], tiled=True)  14.7 us
    pallas_call x7, Pallas kernels, call(): pl.pallas_call(kernel, out_shape=[space(shape, dtype) for space, (shape,...  13.7 us
    all_to_all x2, waiting for transfers between devices, exchange(): lax.all_to_all(chunks, 'wide', 0, 0, axis_index_groups=[order], tiled=True)  2.8 us
    add x2, other arithmetic, freq_sum(): total + lax.ppermute(send[shift - 1], 'freq', pairs).astype(jnp.float32)  1.34 us
    ppermute x2, waiting for transfers between devices, freq_sum(): lax.ppermute(send[shift - 1], 'freq', pairs).astype(jnp.float32)  0.96 us
  transfers between devices with their start and end apart: 4, of which 3 were waited for; matrix products, arithmetic and copies ran while one was open for 2% of the time, Pallas kernels for 26%

profile of v6, /device:TPU:0, one launch (start us, length us, event | category | flops | bytes accessed | tf_op | source)
XLA Modules:
  0.0 34.3 jit_solution(7198596169117526774)
XLA Ops:
  0.6 2.8 %first.1 = bf16[16,64,128]{2,1,0:T(8,128)(2,1)} custom-call(bf16[2,64,1024]{2,1,0:T(8,128)(2,1)} %bitcast.11, bf16[2,1,3,2,81]{4,3,2,1,0:T(2,128)(2,1)} %bitcast.18, s32[2,3,2,1024]{3,2,1,0:T(2,128)} %bitcast.12, s32[2,3,2,1024]{3,2,1,0:T(2,128)} %bitcast.15), custom_call_target="tpu_custom_call" | custom-call | flops 603979776 | bytes 1048576 | tf_op jit(solution)/shard_map/first/pallas_call | solution.py:415
  3.4 8.8 %all-to-all-start = ((bf16[16,64,128]{2,1,0:T(8,128)(2,1)}), bf16[16,64,128]{2,1,0:T(8,128)(2,1)S(1)}, u32[]{:S(2)}, u32[]{:S(2)}) async-start(bf16[16,64,128]{2,1,0:T(8,128)(2,1)} %first.1), calls=%async_computation | async-start | bytes 524288 | tf_op jit(solution)/shard_map/all_to_all | solution.py:41
  12.2 4.9 %prepare_middle.1 = (bf16[8,128,768]{2,1,0:T(8,128)(2,1)S(1)}, bf16[8,128,768]{2,1,0:T(8,128)(2,1)S(1)}, f32[64,128]{1,0:T(8,128)S(1)}) custom-call(bf16[2,1,3,2,81]{4,3,2,1,0:T(2,128)(2,1)} %bitcast.19, s32[2,3,2,1024]{3,2,1,0:T(2,128)} %bitcast.13, s32[2,3,2,1024]{3,2,1,0:T(2,128)} %bitcast.16, s32[2,64,64]{2,1,0:T(8,128)} %aperture_hbm.3), custom_call_target="tpu_custom_call" | custom-call | flops 301989888 | bytes 1048576 | tf_op jit(solution)/shard_map/prepare_middle/pallas_call | solution.py:415
  17.1 2.0 %all-to-all-done.moved_ref = bf16[16,64,128]{2,1,0:T(8,128)(2,1)S(1)} async-done(((bf16[16,64,128]{2,1,0:T(8,128)(2,1)}), bf16[16,64,128]{2,1,0:T(8,128)(2,1)S(1)}, u32[]{:S(2)}, u32[]{:S(2)}) %all-to-all-start) | async-done | bytes 262176 | tf_op jit(solution)/shard_map/all_to_all | solution.py:41
  19.1 1.7 %middle.1 = (bf16[16,64,128]{2,1,0:T(8,128)(2,1)}, bf16[1024,128]{1,0:T(8,128)(2,1)}) custom-call(bf16[16,64,128]{2,1,0:T(8,128)(2,1)S(1)} %all-to-all-done.moved_ref, bf16[8,128,768]{2,1,0:T(8,128)(2,1)S(1)} %get-tuple-element.15.second_ref, bf16[8,128,768]{2,1,0:T(8,128)(2,1)S(1)} %get-tuple-element.16.third_ref, f32[64,128]{1,0:T(8,128)S(1)} %get-tuple-element.17.keep_ref), custom_call_target="tpu_custom_call" | custom-call | flops 301989888 | bytes 1048576 | tf_op jit(solution)/shard_map/middle/pallas_call | solution.py:415
  20.8 5.9 %all-to-all-start.1 = ((bf16[16,64,128]{2,1,0:T(8,128)(2,1)}), bf16[16,64,128]{2,1,0:T(8,128)(2,1)S(1)}, u32[]{:S(2)}, u32[]{:S(2)}) async-start(bf16[16,64,128]{2,1,0:T(8,128)(2,1)} %get-tuple-element.18), calls=%async_computation.1 | async-start | bytes 524288 | tf_op jit(solution)/shard_map/all_to_all | solution.py:41
  26.7 1.1 %turn.1 = (bf16[1,64,512]{2,1,0:T(8,128)(2,1)S(1)}, f32[64,512]{1,0:T(8,128)S(1)}) custom-call(bf16[1024,128]{1,0:T(8,128)(2,1)} %get-tuple-element.19.shallow_hbm), custom_call_target="tpu_custom_call" | custom-call | flops 37748736 | bytes 1048576 | tf_op jit(solution)/shard_map/turn/pallas_call | solution.py:415
  27.8 0.1 collective-permute-start
  27.9 2.7 %prepare_last.1 = (bf16[8,768,128]{2,1,0:T(8,128)(2,1)S(1)}, f32[64,1024]{1,0:T(8,128)S(1)}) custom-call(bf16[2,1,3,2,81]{4,3,2,1,0:T(2,128)(2,1)} %bitcast.20, s32[2,3,2,1024]{3,2,1,0:T(2,128)} %bitcast.14, s32[2,3,2,1024]{3,2,1,0:T(2,128)} %bitcast.17, s32[2,64,64]{2,1,0:T(8,128)} %aperture_hbm.3), custom_call_target="tpu_custom_call" | custom-call | flops 301989888 | bytes 1048576 | tf_op jit(solution)/shard_map/prepare_last/pallas_call | solution.py:415
  30.6 0.0 collective-permute-done
  30.6 0.7 %convert_add_fusion.1 = f32[64,512]{1,0:T(8,128)} fusion(f32[64,512]{1,0:T(8,128)S(1)} %get-tuple-element.20, bf16[64,512]{1,0:T(8,128)(2,1)S(1)} %collective-permute-done), kind=kLoop, calls=%fused_computation.1 | loop fusion | flops 65536 | bytes 327680 | tf_op jit(solution)/shard_map/add | solution.py:431
  31.2 0.8 %all-to-all-done.1.field_ref = bf16[16,64,128]{2,1,0:T(8,128)(2,1)S(1)} async-done(((bf16[16,64,128]{2,1,0:T(8,128)(2,1)}), bf16[16,64,128]{2,1,0:T(8,128)(2,1)S(1)}, u32[]{:S(2)}, u32[]{:S(2)}) %all-to-all-start.1) | async-done | bytes 262176 | tf_op jit(solution)/shard_map/all_to_all | solution.py:41
  32.0 0.3 last_send.1
  32.3 0.1 collective-permute-start.1
  32.4 0.3 last_own.1
  32.7 1.0 %collective-permute-done.1 = bf16[64,512]{1,0:T(8,128)(2,1)S(1)} collective-permute-done((bf16[64,512]{1,0:T(8,128)(2,1)S(1)}, bf16[64,512]{1,0:T(8,128)(2,1)S(1)}, u32[]{:S(2)}, u32[]{:S(2)}) %collective-permute-start.1) | collective-permute-done | bytes 65568 | tf_op jit(solution)/shard_map/ppermute | solution.py:431
  33.6 0.7 %convert_add_fusion = f32[64,512]{1,0:T(8,128)} fusion(bf16[64,512]{1,0:T(8,128)(2,1)S(1)} %collective-permute-done.1, bf16[1,64,512]{2,1,0:T(8,128)(2,1)S(1)} %last_own.1), kind=kLoop, calls=%fused_computation | loop fusion | flops 98304 | bytes 262144 | tf_op jit(solution)/shard_map/add | solution.py:431
Async XLA Ops:
  3.4 15.7 %all-to-all-start = ((bf16[16,64,128]{2,1,0:T(8,128)(2,1)}), bf16[16,64,128]{2,1,0:T(8,128)(2,1)S(1)}, u32[]{:S(2)}, u32[]{:S(2)}) async-start(bf16[16,64,128]{2,1,0:T(8,128)(2,1)} %first.1), calls=%async_computation | async-start | bytes 524288 | tf_op jit(solution)/shard_map/all_to_all | solution.py:41
  20.8 11.2 %all-to-all-start.1 = ((bf16[16,64,128]{2,1,0:T(8,128)(2,1)}), bf16[16,64,128]{2,1,0:T(8,128)(2,1)S(1)}, u32[]{:S(2)}, u32[]{:S(2)}) async-start(bf16[16,64,128]{2,1,0:T(8,128)(2,1)} %get-tuple-element.18), calls=%async_computation.1 | async-start | bytes 524288 | tf_op jit(solution)/shard_map/all_to_all | solution.py:41
  27.8 2.8 %collective-permute-start = (bf16[64,512]{1,0:T(8,128)(2,1)S(1)}, bf16[64,512]{1,0:T(8,128)(2,1)S(1)}, u32[]{:S(2)}, u32[]{:S(2)}) collective-permute-start(bf16[64,512]{1,0:T(8,128)(2,1)S(1)} %bitcast.10), channel_id=1, source_target_pairs={{0,1},{1,0},{2,3},{3,2},{4,5},{5,4},{6,7},{7,6},{8,9},{9,8},{10,11... | collective-permute-start | bytes 196616 | tf_op jit(solution)/shard_map/ppermute | solution.py:431
  32.3 1.3 %collective-permute-start.1 = (bf16[64,512]{1,0:T(8,128)(2,1)S(1)}, bf16[64,512]{1,0:T(8,128)(2,1)S(1)}, u32[]{:S(2)}, u32[]{:S(2)}) collective-permute-start(bf16[64,512]{1,0:T(8,128)(2,1)S(1)} %bitcast.9), channel_id=1, source_target_pairs={{0,1},{1,0},{2,3},{3,2},{4,5},{5,4},{6,7},{7,6},{8,9},{9,8},{10,11... | collective-permute-start | bytes 196616 | tf_op jit(solution)/shard_map/ppermute | solution.py:431

commit v7 on v6

--- a/solution.py
+++ b/solution.py
@@ -30,15 +30,20 @@
         self.blocks = aperture_shape[-1]
         self.blk = self.pos // self.blocks
         self.chunks = LANES // self.rows
-        start = self.wide // 2 + self.wide // 8
-        self.start = start // self.chunks * self.chunks
-
-    def place(self, index):
-        return (index - self.start) % self.wide
-
-    def exchange(self, chunks):
-        order = [(self.start + i) % self.wide for i in range(self.wide)]
-        return lax.all_to_all(chunks, "wide", 0, 0, axis_index_groups=[order], tiled=True)
+        quarter = self.wide // 4
+        blocks = [list(range(i * quarter, (i + 1) * quarter)) for i in range(4)]
+        middle = quarter // 2
+        self.start = blocks[2][middle]
+        self.orders = (
+            blocks[2][middle:] + blocks[2][:middle] + blocks[1][::-1] + blocks[0] + blocks[3],
+            [(self.start + i) % self.wide for i in range(self.wide)],
+        )
+
+    def place(self, turn, index):
+        return self.orders[turn].index(index)
+
+    def exchange(self, turn, chunks):
+        return lax.all_to_all(chunks, "wide", 0, 0, axis_index_groups=[self.orders[turn]], tiled=True)
 
 
 def fill_taps(z, filt_ref, step, rows_ref):
@@ -85,13 +90,9 @@
     return copies
 
 
-def sent(z, out_ref, out_hbm, sems, tile):
-    place = pl.ds(z.place(tile * z.chunks), z.chunks)
+def sent(z, turn, out_ref, out_hbm, sems, tile):
+    place = pl.ds(min(z.place(turn, tile * z.chunks + c) for c in range(z.chunks)), z.chunks)
     return pltpu.make_async_copy(out_ref.at[place], out_hbm.at[place], sems.at[tile])
-
-
-def send_out(z, out_ref, out_hbm, sems, tile):
-    sent(z, out_ref, out_hbm, sems, tile).start()
 
 
 def first_kernel(
@@ -192,10 +193,10 @@
             else:
                 total = part.astype(jnp.bfloat16)
                 for c in range(z.chunks):
-                    out_ref[z.place(tile * z.chunks + c)] = total[:, 2 * z.rows * c : 2 * z.rows * (c + 1)]
-                send_out(z, out_ref, out_hbm, out_sems, tile)
-    for tile in range(z.tiles):
-        sent(z, out_ref, out_hbm, out_sems, tile).wait()
+                    out_ref[z.place(0, tile * z.chunks + c)] = total[:, 2 * z.rows * c : 2 * z.rows * (c + 1)]
+                sent(z, 0, out_ref, out_hbm, out_sems, tile).start()
+    for tile in range(z.tiles):
+        sent(z, 0, out_ref, out_hbm, out_sems, tile).wait()
 
 
 def prepare_middle_kernel(
@@ -337,8 +338,7 @@
     width = 2 * z.rows
 
     def field(tile):
-        chunk = z.place(tile * z.chunks)
-        return moved_ref[chunk : chunk + z.chunks].reshape(LANES, width)
+        return jnp.concatenate([moved_ref[z.place(0, tile * z.chunks + c)] for c in range(z.chunks)], axis=0)
 
     for tile in range(z.tiles):
         turned_ref[tile] = turned(z, field(tile))
@@ -353,14 +353,14 @@
     shallow_copy = pltpu.make_async_copy(straight2_ref, shallow_hbm, shallow_sem.at[0])
     shallow_copy.start()
     for tile in range(z.tiles):
-        chunk = z.place(tile * z.chunks)
+        chunk = z.place(1, tile * z.chunks)
         third = over_sources(
             z, third_ref, lambda j: straight2_ref[j * LANES : (j + 1) * LANES, :], lambda j: turned2_ref[j], tile
         ).astype(jnp.bfloat16)
         out_ref[chunk : chunk + z.chunks] = third.reshape(z.chunks, z.rows, width)
-        send_out(z, out_ref, out_hbm, out_sems, tile)
-    for tile in range(z.tiles):
-        sent(z, out_ref, out_hbm, out_sems, tile).wait()
+        sent(z, 1, out_ref, out_hbm, out_sems, tile).start()
+    for tile in range(z.tiles):
+        sent(z, 1, out_ref, out_hbm, out_sems, tile).wait()
     shallow_copy.wait()
 
 
@@ -460,7 +460,7 @@
         fetched=True,
         sent=(z.tiles,),
     )
-    moved = z.exchange(first)
+    moved = z.exchange(0, first)
     second_band, third_band, shallow_keep = call(
         functools.partial(prepare_middle_kernel, z),
         (filters, vel_bins, blend_levels, aperture),
@@ -483,7 +483,7 @@
         "middle",
         sent=(z.tiles, 1),
     )
-    returned = z.exchange(third)
+    returned = z.exchange(1, third)
     fourth_band, deep_keep = call(
         functools.partial(prepare_last_kernel, z),
         (filters, vel_bins, blend_levels, aperture),

time: 34.8 us -> 34.4 us (0.989)
  starting transfers between devices: 14.8 us -> 14.1 us
  waiting for transfers between devices: 3.76 us -> 4.11 us
    all_to_all x2, starting transfers between devices: 14.7 us -> 13.9 us  [exchange(): lax.all_to_all(chunks, 'wide', 0, 0, axis_index_groups=[self.orders[turn]...]
where the time goes in v7:
time: 34.4 us; the launch traced here: 33.9 us
  starting transfers between devices  14.1 us (41%)
  Pallas kernels  13.7 us (40%)
  waiting for transfers between devices  4.11 us (12%)
  other arithmetic  1.34 us (4%)
  between operations  0.7 us (2%)
    all_to_all x2, starting transfers between devices, exchange(): lax.all_to_all(chunks, 'wide', 0, 0, axis_index_groups=[self.orders[turn]...  13.9 us
    pallas_call x7, Pallas kernels, call(): pl.pallas_call(kernel, out_shape=[space(shape, dtype) for space, (shape,...  13.7 us
    all_to_all x2, waiting for transfers between devices, exchange(): lax.all_to_all(chunks, 'wide', 0, 0, axis_index_groups=[self.orders[turn]...  3.15 us
    add x2, other arithmetic, freq_sum(): total + lax.ppermute(send[shift - 1], 'freq', pairs).astype(jnp.float32)  1.34 us
    ppermute x2, waiting for transfers between devices, freq_sum(): lax.ppermute(send[shift - 1], 'freq', pairs).astype(jnp.float32)  0.96 us
  transfers between devices with their start and end apart: 4, of which 3 were waited for; matrix products, arithmetic and copies ran while one was open for 2% of the time, Pallas kernels for 26%

profile of v7, /device:TPU:0, one launch (start us, length us, event | category | flops | bytes accessed | tf_op | source)
XLA Modules:
  0.0 33.9 jit_solution(1445831543602782382)
XLA Ops:
  0.6 2.8 %first.1 = bf16[16,64,128]{2,1,0:T(8,128)(2,1)} custom-call(bf16[2,64,1024]{2,1,0:T(8,128)(2,1)} %bitcast.11, bf16[2,1,3,2,81]{4,3,2,1,0:T(2,128)(2,1)} %bitcast.18, s32[2,3,2,1024]{3,2,1,0:T(2,128)} %bitcast.12, s32[2,3,2,1024]{3,2,1,0:T(2,128)} %bitcast.15), custom_call_target="tpu_custom_call" | custom-call | flops 603979776 | bytes 1048576 | tf_op jit(solution)/shard_map/first/pallas_call | solution.py:415
  3.4 8.8 %all-to-all-start = ((bf16[16,64,128]{2,1,0:T(8,128)(2,1)}), bf16[16,64,128]{2,1,0:T(8,128)(2,1)S(1)}, u32[]{:S(2)}, u32[]{:S(2)}) async-start(bf16[16,64,128]{2,1,0:T(8,128)(2,1)} %first.1), calls=%async_computation | async-start | bytes 524288 | tf_op jit(solution)/shard_map/all_to_all | solution.py:46
  12.2 4.9 %prepare_middle.1 = (bf16[8,128,768]{2,1,0:T(8,128)(2,1)S(1)}, bf16[8,128,768]{2,1,0:T(8,128)(2,1)S(1)}, f32[64,128]{1,0:T(8,128)S(1)}) custom-call(bf16[2,1,3,2,81]{4,3,2,1,0:T(2,128)(2,1)} %bitcast.19, s32[2,3,2,1024]{3,2,1,0:T(2,128)} %bitcast.13, s32[2,3,2,1024]{3,2,1,0:T(2,128)} %bitcast.16, s32[2,64,64]{2,1,0:T(8,128)} %aperture_hbm.3), custom_call_target="tpu_custom_call" | custom-call | flops 301989888 | bytes 1048576 | tf_op jit(solution)/shard_map/prepare_middle/pallas_call | solution.py:415
  17.1 2.4 %all-to-all-done.moved_ref = bf16[16,64,128]{2,1,0:T(8,128)(2,1)S(1)} async-done(((bf16[16,64,128]{2,1,0:T(8,128)(2,1)}), bf16[16,64,128]{2,1,0:T(8,128)(2,1)S(1)}, u32[]{:S(2)}, u32[]{:S(2)}) %all-to-all-start) | async-done | bytes 262176 | tf_op jit(solution)/shard_map/all_to_all | solution.py:46
  19.4 1.7 %middle.1 = (bf16[16,64,128]{2,1,0:T(8,128)(2,1)}, bf16[1024,128]{1,0:T(8,128)(2,1)}) custom-call(bf16[16,64,128]{2,1,0:T(8,128)(2,1)S(1)} %all-to-all-done.moved_ref, bf16[8,128,768]{2,1,0:T(8,128)(2,1)S(1)} %get-tuple-element.15.second_ref, bf16[8,128,768]{2,1,0:T(8,128)(2,1)S(1)} %get-tuple-element.16.third_ref, f32[64,128]{1,0:T(8,128)S(1)} %get-tuple-element.17.keep_ref), custom_call_target="tpu_custom_call" | custom-call | flops 301989888 | bytes 1048576 | tf_op jit(solution)/shard_map/middle/pallas_call | solution.py:415
  21.1 5.1 %all-to-all-start.1 = ((bf16[16,64,128]{2,1,0:T(8,128)(2,1)}), bf16[16,64,128]{2,1,0:T(8,128)(2,1)S(1)}, u32[]{:S(2)}, u32[]{:S(2)}) async-start(bf16[16,64,128]{2,1,0:T(8,128)(2,1)} %get-tuple-element.18), calls=%async_computation.1 | async-start | bytes 524288 | tf_op jit(solution)/shard_map/all_to_all | solution.py:46
  26.3 1.1 %turn.1 = (bf16[1,64,512]{2,1,0:T(8,128)(2,1)S(1)}, f32[64,512]{1,0:T(8,128)S(1)}) custom-call(bf16[1024,128]{1,0:T(8,128)(2,1)} %get-tuple-element.19.shallow_hbm), custom_call_target="tpu_custom_call" | custom-call | flops 37748736 | bytes 1048576 | tf_op jit(solution)/shard_map/turn/pallas_call | solution.py:415
  27.4 0.1 collective-permute-start
  27.5 2.7 %prepare_last.1 = (bf16[8,768,128]{2,1,0:T(8,128)(2,1)S(1)}, f32[64,1024]{1,0:T(8,128)S(1)}) custom-call(bf16[2,1,3,2,81]{4,3,2,1,0:T(2,128)(2,1)} %bitcast.20, s32[2,3,2,1024]{3,2,1,0:T(2,128)} %bitcast.14, s32[2,3,2,1024]{3,2,1,0:T(2,128)} %bitcast.17, s32[2,64,64]{2,1,0:T(8,128)} %aperture_hbm.3), custom_call_target="tpu_custom_call" | custom-call | flops 301989888 | bytes 1048576 | tf_op jit(solution)/shard_map/prepare_last/pallas_call | solution.py:415
  30.1 0.0 collective-permute-done
  30.2 0.7 %convert_add_fusion.1 = f32[64,512]{1,0:T(8,128)} fusion(f32[64,512]{1,0:T(8,128)S(1)} %get-tuple-element.20, bf16[64,512]{1,0:T(8,128)(2,1)S(1)} %collective-permute-done), kind=kLoop, calls=%fused_computation.1 | loop fusion | flops 65536 | bytes 327680 | tf_op jit(solution)/shard_map/add | solution.py:431
  30.8 0.8 %all-to-all-done.1.field_ref = bf16[16,64,128]{2,1,0:T(8,128)(2,1)S(1)} async-done(((bf16[16,64,128]{2,1,0:T(8,128)(2,1)}), bf16[16,64,128]{2,1,0:T(8,128)(2,1)S(1)}, u32[]{:S(2)}, u32[]{:S(2)}) %all-to-all-start.1) | async-done | bytes 262176 | tf_op jit(solution)/shard_map/all_to_all | solution.py:46
  31.6 0.3 last_send.1
  31.9 0.1 collective-permute-start.1
  32.0 0.3 last_own.1
  32.2 1.0 %collective-permute-done.1 = bf16[64,512]{1,0:T(8,128)(2,1)S(1)} collective-permute-done((bf16[64,512]{1,0:T(8,128)(2,1)S(1)}, bf16[64,512]{1,0:T(8,128)(2,1)S(1)}, u32[]{:S(2)}, u32[]{:S(2)}) %collective-permute-start.1) | collective-permute-done | bytes 65568 | tf_op jit(solution)/shard_map/ppermute | solution.py:431
  33.2 0.7 %convert_add_fusion = f32[64,512]{1,0:T(8,128)} fusion(bf16[64,512]{1,0:T(8,128)(2,1)S(1)} %collective-permute-done.1, bf16[1,64,512]{2,1,0:T(8,128)(2,1)S(1)} %last_own.1), kind=kLoop, calls=%fused_computation | loop fusion | flops 98304 | bytes 262144 | tf_op jit(solution)/shard_map/add | solution.py:431
Async XLA Ops:
  3.4 16.0 %all-to-all-start = ((bf16[16,64,128]{2,1,0:T(8,128)(2,1)}), bf16[16,64,128]{2,1,0:T(8,128)(2,1)S(1)}, u32[]{:S(2)}, u32[]{:S(2)}) async-start(bf16[16,64,128]{2,1,0:T(8,128)(2,1)} %first.1), calls=%async_computation | async-start | bytes 524288 | tf_op jit(solution)/shard_map/all_to_all | solution.py:46
  21.1 10.5 %all-to-all-start.1 = ((bf16[16,64,128]{2,1,0:T(8,128)(2,1)}), bf16[16,64,128]{2,1,0:T(8,128)(2,1)S(1)}, u32[]{:S(2)}, u32[]{:S(2)}) async-start(bf16[16,64,128]{2,1,0:T(8,128)(2,1)} %get-tuple-element.18), calls=%async_computation.1 | async-start | bytes 524288 | tf_op jit(solution)/shard_map/all_to_all | solution.py:46
  27.4 2.8 %collective-permute-start = (bf16[64,512]{1,0:T(8,128)(2,1)S(1)}, bf16[64,512]{1,0:T(8,128)(2,1)S(1)}, u32[]{:S(2)}, u32[]{:S(2)}) collective-permute-start(bf16[64,512]{1,0:T(8,128)(2,1)S(1)} %bitcast.10), channel_id=1, source_target_pairs={{0,1},{1,0},{2,3},{3,2},{4,5},{5,4},{6,7},{7,6},{8,9},{9,8},{10,11... | collective-permute-start | bytes 196616 | tf_op jit(solution)/shard_map/ppermute | solution.py:431
  31.9 1.3 %collective-permute-start.1 = (bf16[64,512]{1,0:T(8,128)(2,1)S(1)}, bf16[64,512]{1,0:T(8,128)(2,1)S(1)}, u32[]{:S(2)}, u32[]{:S(2)}) collective-permute-start(bf16[64,512]{1,0:T(8,128)(2,1)S(1)} %bitcast.9), channel_id=1, source_target_pairs={{0,1},{1,0},{2,3},{3,2},{4,5},{5,4},{6,7},{7,6},{8,9},{9,8},{10,11... | collective-permute-start | bytes 196616 | tf_op jit(solution)/shard_map/ppermute | solution.py:431

commit v8 on v7

--- a/solution.py
+++ b/solution.py
@@ -157,7 +157,6 @@
                 band_ref[top : top + z.side, columns + LANES : columns + 2 * LANES] = block
     copies[1].wait()
     copies[2].wait()
-    fill_table(z, bins_ref, levels_ref, 0, 0, table_ref)
     copies[3].wait()
     spans = 1 + 2 * z.halo
     for part in range(2):
@@ -172,17 +171,19 @@
                 lhs_ref[tile * z.rows : (tile + 1) * z.rows, place : place + LANES] = piece
     lane = lax.broadcasted_iota(jnp.int32, (8, LANES), 1)
     points = [chunk_order(z, lane + v * LANES)[1] for v in range(2)]
-    columns = []
-    for tile in range(z.tiles):
-        weights = table_ref[:, tile * LANES : (tile + 1) * LANES]
-        picked = [jnp.take_along_axis(weights, p, axis=1, mode="promise_in_bounds") for p in points]
-        columns.append(jnp.concatenate(picked, axis=1))
     for k in range(z.bins):
         product = jnp.dot(
             lhs_ref[...],
             band_ref[:, 2 * k * LANES : 2 * (k + 1) * LANES],
             preferred_element_type=jnp.float32,
         )
+        if k == 0:
+            fill_table(z, bins_ref, levels_ref, 0, 0, table_ref)
+            columns = []
+            for tile in range(z.tiles):
+                weights = table_ref[:, tile * LANES : (tile + 1) * LANES]
+                picked = [jnp.take_along_axis(weights, p, axis=1, mode="promise_in_bounds") for p in points]
+                columns.append(jnp.concatenate(picked, axis=1))
         for tile in range(z.tiles):
             rows = slice(tile * z.rows, (tile + 1) * z.rows)
             part = product[rows] * columns[tile][k : k + 1]

time: 34.4 us -> 34.4 us (level)
  no operation moved by 1% of the time
where the time goes in v8:
time: 34.4 us; the launch traced here: 33.8 us
  starting transfers between devices  14.1 us (41%)
  Pallas kernels  13.6 us (40%)
  waiting for transfers between devices  4.11 us (12%)
  other arithmetic  1.34 us (4%)
  between operations  0.7 us (2%)
    all_to_all x2, starting transfers between devices, exchange(): lax.all_to_all(chunks, 'wide', 0, 0, axis_index_groups=[self.orders[turn]...  13.9 us
    pallas_call x7, Pallas kernels, call(): pl.pallas_call(kernel, out_shape=[space(shape, dtype) for space, (shape,...  13.6 us
    all_to_all x2, waiting for transfers between devices, exchange(): lax.all_to_all(chunks, 'wide', 0, 0, axis_index_groups=[self.orders[turn]...  3.15 us
    add x2, other arithmetic, freq_sum(): total + lax.ppermute(send[shift - 1], 'freq', pairs).astype(jnp.float32)  1.34 us
    ppermute x2, waiting for transfers between devices, freq_sum(): lax.ppermute(send[shift - 1], 'freq', pairs).astype(jnp.float32)  0.96 us
  transfers between devices with their start and end apart: 4, of which 3 were waited for; matrix products, arithmetic and copies ran while one was open for 2% of the time, Pallas kernels for 26%

profile of v8, /device:TPU:0, one launch (start us, length us, event | category | flops | bytes accessed | tf_op | source)
XLA Modules:
  0.0 33.8 jit_solution(5807013161491064305)
XLA Ops:
  0.6 2.8 %first.1 = bf16[16,64,128]{2,1,0:T(8,128)(2,1)} custom-call(bf16[2,64,1024]{2,1,0:T(8,128)(2,1)} %bitcast.11, bf16[2,1,3,2,81]{4,3,2,1,0:T(2,128)(2,1)} %bitcast.18, s32[2,3,2,1024]{3,2,1,0:T(2,128)} %bitcast.12, s32[2,3,2,1024]{3,2,1,0:T(2,128)} %bitcast.15), custom_call_target="tpu_custom_call" | custom-call | flops 603979776 | bytes 1048576 | tf_op jit(solution)/shard_map/first/pallas_call | solution.py:416
  3.4 8.8 %all-to-all-start = ((bf16[16,64,128]{2,1,0:T(8,128)(2,1)}), bf16[16,64,128]{2,1,0:T(8,128)(2,1)S(1)}, u32[]{:S(2)}, u32[]{:S(2)}) async-start(bf16[16,64,128]{2,1,0:T(8,128)(2,1)} %first.1), calls=%async_computation | async-start | bytes 524288 | tf_op jit(solution)/shard_map/all_to_all | solution.py:46
  12.2 4.9 %prepare_middle.1 = (bf16[8,128,768]{2,1,0:T(8,128)(2,1)S(1)}, bf16[8,128,768]{2,1,0:T(8,128)(2,1)S(1)}, f32[64,128]{1,0:T(8,128)S(1)}) custom-call(bf16[2,1,3,2,81]{4,3,2,1,0:T(2,128)(2,1)} %bitcast.19, s32[2,3,2,1024]{3,2,1,0:T(2,128)} %bitcast.13, s32[2,3,2,1024]{3,2,1,0:T(2,128)} %bitcast.16, s32[2,64,64]{2,1,0:T(8,128)} %aperture_hbm.3), custom_call_target="tpu_custom_call" | custom-call | flops 301989888 | bytes 1048576 | tf_op jit(solution)/shard_map/prepare_middle/pallas_call | solution.py:416
  17.1 2.4 %all-to-all-done.moved_ref = bf16[16,64,128]{2,1,0:T(8,128)(2,1)S(1)} async-done(((bf16[16,64,128]{2,1,0:T(8,128)(2,1)}), bf16[16,64,128]{2,1,0:T(8,128)(2,1)S(1)}, u32[]{:S(2)}, u32[]{:S(2)}) %all-to-all-start) | async-done | bytes 262176 | tf_op jit(solution)/shard_map/all_to_all | solution.py:46
  19.4 1.7 %middle.1 = (bf16[16,64,128]{2,1,0:T(8,128)(2,1)}, bf16[1024,128]{1,0:T(8,128)(2,1)}) custom-call(bf16[16,64,128]{2,1,0:T(8,128)(2,1)S(1)} %all-to-all-done.moved_ref, bf16[8,128,768]{2,1,0:T(8,128)(2,1)S(1)} %get-tuple-element.15.second_ref, bf16[8,128,768]{2,1,0:T(8,128)(2,1)S(1)} %get-tuple-element.16.third_ref, f32[64,128]{1,0:T(8,128)S(1)} %get-tuple-element.17.keep_ref), custom_call_target="tpu_custom_call" | custom-call | flops 301989888 | bytes 1048576 | tf_op jit(solution)/shard_map/middle/pallas_call | solution.py:416
  21.1 5.1 %all-to-all-start.1 = ((bf16[16,64,128]{2,1,0:T(8,128)(2,1)}), bf16[16,64,128]{2,1,0:T(8,128)(2,1)S(1)}, u32[]{:S(2)}, u32[]{:S(2)}) async-start(bf16[16,64,128]{2,1,0:T(8,128)(2,1)} %get-tuple-element.18), calls=%async_computation.1 | async-start | bytes 524288 | tf_op jit(solution)/shard_map/all_to_all | solution.py:46
  26.3 1.1 %turn.1 = (bf16[1,64,512]{2,1,0:T(8,128)(2,1)S(1)}, f32[64,512]{1,0:T(8,128)S(1)}) custom-call(bf16[1024,128]{1,0:T(8,128)(2,1)} %get-tuple-element.19.shallow_hbm), custom_call_target="tpu_custom_call" | custom-call | flops 37748736 | bytes 1048576 | tf_op jit(solution)/shard_map/turn/pallas_call | solution.py:416
  27.4 0.1 collective-permute-start
  27.4 2.7 %prepare_last.1 = (bf16[8,768,128]{2,1,0:T(8,128)(2,1)S(1)}, f32[64,1024]{1,0:T(8,128)S(1)}) custom-call(bf16[2,1,3,2,81]{4,3,2,1,0:T(2,128)(2,1)} %bitcast.20, s32[2,3,2,1024]{3,2,1,0:T(2,128)} %bitcast.14, s32[2,3,2,1024]{3,2,1,0:T(2,128)} %bitcast.17, s32[2,64,64]{2,1,0:T(8,128)} %aperture_hbm.3), custom_call_target="tpu_custom_call" | custom-call | flops 301989888 | bytes 1048576 | tf_op jit(solution)/shard_map/prepare_last/pallas_call | solution.py:416
  30.1 0.0 collective-permute-done
  30.1 0.7 %convert_add_fusion.1 = f32[64,512]{1,0:T(8,128)} fusion(f32[64,512]{1,0:T(8,128)S(1)} %get-tuple-element.20, bf16[64,512]{1,0:T(8,128)(2,1)S(1)} %collective-permute-done), kind=kLoop, calls=%fused_computation.1 | loop fusion | flops 65536 | bytes 327680 | tf_op jit(solution)/shard_map/add | solution.py:432
  30.8 0.8 %all-to-all-done.1.field_ref = bf16[16,64,128]{2,1,0:T(8,128)(2,1)S(1)} async-done(((bf16[16,64,128]{2,1,0:T(8,128)(2,1)}), bf16[16,64,128]{2,1,0:T(8,128)(2,1)S(1)}, u32[]{:S(2)}, u32[]{:S(2)}) %all-to-all-start.1) | async-done | bytes 262176 | tf_op jit(solution)/shard_map/all_to_all | solution.py:46
  31.6 0.3 last_send.1
  31.9 0.1 collective-permute-start.1
  31.9 0.3 last_own.1
  32.2 1.0 %collective-permute-done.1 = bf16[64,512]{1,0:T(8,128)(2,1)S(1)} collective-permute-done((bf16[64,512]{1,0:T(8,128)(2,1)S(1)}, bf16[64,512]{1,0:T(8,128)(2,1)S(1)}, u32[]{:S(2)}, u32[]{:S(2)}) %collective-permute-start.1) | collective-permute-done | bytes 65568 | tf_op jit(solution)/shard_map/ppermute | solution.py:432
  33.2 0.7 %convert_add_fusion = f32[64,512]{1,0:T(8,128)} fusion(bf16[64,512]{1,0:T(8,128)(2,1)S(1)} %collective-permute-done.1, bf16[1,64,512]{2,1,0:T(8,128)(2,1)S(1)} %last_own.1), kind=kLoop, calls=%fused_computation | loop fusion | flops 98304 | bytes 262144 | tf_op jit(solution)/shard_map/add | solution.py:432
Async XLA Ops:
  3.4 16.0 %all-to-all-start = ((bf16[16,64,128]{2,1,0:T(8,128)(2,1)}), bf16[16,64,128]{2,1,0:T(8,128)(2,1)S(1)}, u32[]{:S(2)}, u32[]{:S(2)}) async-start(bf16[16,64,128]{2,1,0:T(8,128)(2,1)} %first.1), calls=%async_computation | async-start | bytes 524288 | tf_op jit(solution)/shard_map/all_to_all | solution.py:46
  21.1 10.5 %all-to-all-start.1 = ((bf16[16,64,128]{2,1,0:T(8,128)(2,1)}), bf16[16,64,128]{2,1,0:T(8,128)(2,1)S(1)}, u32[]{:S(2)}, u32[]{:S(2)}) async-start(bf16[16,64,128]{2,1,0:T(8,128)(2,1)} %get-tuple-element.18), calls=%async_computation.1 | async-start | bytes 524288 | tf_op jit(solution)/shard_map/all_to_all | solution.py:46
  27.4 2.8 %collective-permute-start = (bf16[64,512]{1,0:T(8,128)(2,1)S(1)}, bf16[64,512]{1,0:T(8,128)(2,1)S(1)}, u32[]{:S(2)}, u32[]{:S(2)}) collective-permute-start(bf16[64,512]{1,0:T(8,128)(2,1)S(1)} %bitcast.10), channel_id=1, source_target_pairs={{0,1},{1,0},{2,3},{3,2},{4,5},{5,4},{6,7},{7,6},{8,9},{9,8},{10,11... | collective-permute-start | bytes 196616 | tf_op jit(solution)/shard_map/ppermute | solution.py:432
  31.9 1.3 %collective-permute-start.1 = (bf16[64,512]{1,0:T(8,128)(2,1)S(1)}, bf16[64,512]{1,0:T(8,128)(2,1)S(1)}, u32[]{:S(2)}, u32[]{:S(2)}) collective-permute-start(bf16[64,512]{1,0:T(8,128)(2,1)S(1)} %bitcast.9), channel_id=1, source_target_pairs={{0,1},{1,0},{2,3},{3,2},{4,5},{5,4},{6,7},{7,6},{8,9},{9,8},{10,11... | collective-permute-start | bytes 196616 | tf_op jit(solution)/shard_map/ppermute | solution.py:432

commit v9 on v8

--- a/solution.py
+++ b/solution.py
@@ -171,12 +171,9 @@
                 lhs_ref[tile * z.rows : (tile + 1) * z.rows, place : place + LANES] = piece
     lane = lax.broadcasted_iota(jnp.int32, (8, LANES), 1)
     points = [chunk_order(z, lane + v * LANES)[1] for v in range(2)]
+    whole = jnp.dot(lhs_ref[...], band_ref[...], preferred_element_type=jnp.float32)
     for k in range(z.bins):
-        product = jnp.dot(
-            lhs_ref[...],
-            band_ref[:, 2 * k * LANES : 2 * (k + 1) * LANES],
-            preferred_element_type=jnp.float32,
-        )
+        product = whole[:, 2 * k * LANES : 2 * (k + 1) * LANES]
         if k == 0:
             fill_table(z, bins_ref, levels_ref, 0, 0, table_ref)
             columns = []

time: 34.4 us -> 34.4 us (level)
  no operation moved by 1% of the time
where the time goes in v9:
time: 34.4 us; the launch traced here: 33.8 us
  starting transfers between devices  14.1 us (41%)
  Pallas kernels  13.6 us (40%)
  waiting for transfers between devices  4.11 us (12%)
  other arithmetic  1.34 us (4%)
  between operations  0.7 us (2%)
    all_to_all x2, starting transfers between devices, exchange(): lax.all_to_all(chunks, 'wide', 0, 0, axis_index_groups=[self.orders[turn]...  13.9 us
    pallas_call x7, Pallas kernels, call(): pl.pallas_call(kernel, out_shape=[space(shape, dtype) for space, (shape,...  13.6 us
    all_to_all x2, waiting for transfers between devices, exchange(): lax.all_to_all(chunks, 'wide', 0, 0, axis_index_groups=[self.orders[turn]...  3.15 us
    add x2, other arithmetic, freq_sum(): total + lax.ppermute(send[shift - 1], 'freq', pairs).astype(jnp.float32)  1.34 us
    ppermute x2, waiting for transfers between devices, freq_sum(): lax.ppermute(send[shift - 1], 'freq', pairs).astype(jnp.float32)  0.96 us
  transfers between devices with their start and end apart: 4, of which 3 were waited for; matrix products, arithmetic and copies ran while one was open for 2% of the time, Pallas kernels for 26%

profile of v9, /device:TPU:0, one launch (start us, length us, event | category | flops | bytes accessed | tf_op | source)
XLA Modules:
  0.0 33.8 jit_solution(12347185991503153712)
XLA Ops:
  0.6 2.8 %first.1 = bf16[16,64,128]{2,1,0:T(8,128)(2,1)} custom-call(bf16[2,64,1024]{2,1,0:T(8,128)(2,1)} %bitcast.11, bf16[2,1,3,2,81]{4,3,2,1,0:T(2,128)(2,1)} %bitcast.18, s32[2,3,2,1024]{3,2,1,0:T(2,128)} %bitcast.12, s32[2,3,2,1024]{3,2,1,0:T(2,128)} %bitcast.15), custom_call_target="tpu_custom_call" | custom-call | flops 603979776 | bytes 1048576 | tf_op jit(solution)/shard_map/first/pallas_call | solution.py:413
  3.4 8.8 %all-to-all-start = ((bf16[16,64,128]{2,1,0:T(8,128)(2,1)}), bf16[16,64,128]{2,1,0:T(8,128)(2,1)S(1)}, u32[]{:S(2)}, u32[]{:S(2)}) async-start(bf16[16,64,128]{2,1,0:T(8,128)(2,1)} %first.1), calls=%async_computation | async-start | bytes 524288 | tf_op jit(solution)/shard_map/all_to_all | solution.py:46
  12.2 4.9 %prepare_middle.1 = (bf16[8,128,768]{2,1,0:T(8,128)(2,1)S(1)}, bf16[8,128,768]{2,1,0:T(8,128)(2,1)S(1)}, f32[64,128]{1,0:T(8,128)S(1)}) custom-call(bf16[2,1,3,2,81]{4,3,2,1,0:T(2,128)(2,1)} %bitcast.19, s32[2,3,2,1024]{3,2,1,0:T(2,128)} %bitcast.13, s32[2,3,2,1024]{3,2,1,0:T(2,128)} %bitcast.16, s32[2,64,64]{2,1,0:T(8,128)} %aperture_hbm.3), custom_call_target="tpu_custom_call" | custom-call | flops 301989888 | bytes 1048576 | tf_op jit(solution)/shard_map/prepare_middle/pallas_call | solution.py:413
  17.1 2.4 %all-to-all-done.moved_ref = bf16[16,64,128]{2,1,0:T(8,128)(2,1)S(1)} async-done(((bf16[16,64,128]{2,1,0:T(8,128)(2,1)}), bf16[16,64,128]{2,1,0:T(8,128)(2,1)S(1)}, u32[]{:S(2)}, u32[]{:S(2)}) %all-to-all-start) | async-done | bytes 262176 | tf_op jit(solution)/shard_map/all_to_all | solution.py:46
  19.4 1.7 %middle.1 = (bf16[16,64,128]{2,1,0:T(8,128)(2,1)}, bf16[1024,128]{1,0:T(8,128)(2,1)}) custom-call(bf16[16,64,128]{2,1,0:T(8,128)(2,1)S(1)} %all-to-all-done.moved_ref, bf16[8,128,768]{2,1,0:T(8,128)(2,1)S(1)} %get-tuple-element.15.second_ref, bf16[8,128,768]{2,1,0:T(8,128)(2,1)S(1)} %get-tuple-element.16.third_ref, f32[64,128]{1,0:T(8,128)S(1)} %get-tuple-element.17.keep_ref), custom_call_target="tpu_custom_call" | custom-call | flops 301989888 | bytes 1048576 | tf_op jit(solution)/shard_map/middle/pallas_call | solution.py:413
  21.1 5.1 %all-to-all-start.1 = ((bf16[16,64,128]{2,1,0:T(8,128)(2,1)}), bf16[16,64,128]{2,1,0:T(8,128)(2,1)S(1)}, u32[]{:S(2)}, u32[]{:S(2)}) async-start(bf16[16,64,128]{2,1,0:T(8,128)(2,1)} %get-tuple-element.18), calls=%async_computation.1 | async-start | bytes 524288 | tf_op jit(solution)/shard_map/all_to_all | solution.py:46
  26.3 1.1 %turn.1 = (bf16[1,64,512]{2,1,0:T(8,128)(2,1)S(1)}, f32[64,512]{1,0:T(8,128)S(1)}) custom-call(bf16[1024,128]{1,0:T(8,128)(2,1)} %get-tuple-element.19.shallow_hbm), custom_call_target="tpu_custom_call" | custom-call | flops 37748736 | bytes 1048576 | tf_op jit(solution)/shard_map/turn/pallas_call | solution.py:413
  27.4 0.1 collective-permute-start
  27.4 2.7 %prepare_last.1 = (bf16[8,768,128]{2,1,0:T(8,128)(2,1)S(1)}, f32[64,1024]{1,0:T(8,128)S(1)}) custom-call(bf16[2,1,3,2,81]{4,3,2,1,0:T(2,128)(2,1)} %bitcast.20, s32[2,3,2,1024]{3,2,1,0:T(2,128)} %bitcast.14, s32[2,3,2,1024]{3,2,1,0:T(2,128)} %bitcast.17, s32[2,64,64]{2,1,0:T(8,128)} %aperture_hbm.3), custom_call_target="tpu_custom_call" | custom-call | flops 301989888 | bytes 1048576 | tf_op jit(solution)/shard_map/prepare_last/pallas_call | solution.py:413
  30.1 0.0 collective-permute-done
  30.1 0.7 %convert_add_fusion.1 = f32[64,512]{1,0:T(8,128)} fusion(f32[64,512]{1,0:T(8,128)S(1)} %get-tuple-element.20, bf16[64,512]{1,0:T(8,128)(2,1)S(1)} %collective-permute-done), kind=kLoop, calls=%fused_computation.1 | loop fusion | flops 65536 | bytes 327680 | tf_op jit(solution)/shard_map/add | solution.py:429
  30.8 0.8 %all-to-all-done.1.field_ref = bf16[16,64,128]{2,1,0:T(8,128)(2,1)S(1)} async-done(((bf16[16,64,128]{2,1,0:T(8,128)(2,1)}), bf16[16,64,128]{2,1,0:T(8,128)(2,1)S(1)}, u32[]{:S(2)}, u32[]{:S(2)}) %all-to-all-start.1) | async-done | bytes 262176 | tf_op jit(solution)/shard_map/all_to_all | solution.py:46
  31.6 0.3 last_send.1
  31.9 0.1 collective-permute-start.1
  31.9 0.3 last_own.1
  32.2 1.0 %collective-permute-done.1 = bf16[64,512]{1,0:T(8,128)(2,1)S(1)} collective-permute-done((bf16[64,512]{1,0:T(8,128)(2,1)S(1)}, bf16[64,512]{1,0:T(8,128)(2,1)S(1)}, u32[]{:S(2)}, u32[]{:S(2)}) %collective-permute-start.1) | collective-permute-done | bytes 65568 | tf_op jit(solution)/shard_map/ppermute | solution.py:429
  33.2 0.7 %convert_add_fusion = f32[64,512]{1,0:T(8,128)} fusion(bf16[64,512]{1,0:T(8,128)(2,1)S(1)} %collective-permute-done.1, bf16[1,64,512]{2,1,0:T(8,128)(2,1)S(1)} %last_own.1), kind=kLoop, calls=%fused_computation | loop fusion | flops 98304 | bytes 262144 | tf_op jit(solution)/shard_map/add | solution.py:429
Async XLA Ops:
  3.4 16.0 %all-to-all-start = ((bf16[16,64,128]{2,1,0:T(8,128)(2,1)}), bf16[16,64,128]{2,1,0:T(8,128)(2,1)S(1)}, u32[]{:S(2)}, u32[]{:S(2)}) async-start(bf16[16,64,128]{2,1,0:T(8,128)(2,1)} %first.1), calls=%async_computation | async-start | bytes 524288 | tf_op jit(solution)/shard_map/all_to_all | solution.py:46
  21.1 10.5 %all-to-all-start.1 = ((bf16[16,64,128]{2,1,0:T(8,128)(2,1)}), bf16[16,64,128]{2,1,0:T(8,128)(2,1)S(1)}, u32[]{:S(2)}, u32[]{:S(2)}) async-start(bf16[16,64,128]{2,1,0:T(8,128)(2,1)} %get-tuple-element.18), calls=%async_computation.1 | async-start | bytes 524288 | tf_op jit(solution)/shard_map/all_to_all | solution.py:46
  27.4 2.8 %collective-permute-start = (bf16[64,512]{1,0:T(8,128)(2,1)S(1)}, bf16[64,512]{1,0:T(8,128)(2,1)S(1)}, u32[]{:S(2)}, u32[]{:S(2)}) collective-permute-start(bf16[64,512]{1,0:T(8,128)(2,1)S(1)} %bitcast.10), channel_id=1, source_target_pairs={{0,1},{1,0},{2,3},{3,2},{4,5},{5,4},{6,7},{7,6},{8,9},{9,8},{10,11... | collective-permute-start | bytes 196616 | tf_op jit(solution)/shard_map/ppermute | solution.py:429
  31.9 1.3 %collective-permute-start.1 = (bf16[64,512]{1,0:T(8,128)(2,1)S(1)}, bf16[64,512]{1,0:T(8,128)(2,1)S(1)}, u32[]{:S(2)}, u32[]{:S(2)}) collective-permute-start(bf16[64,512]{1,0:T(8,128)(2,1)S(1)} %bitcast.9), channel_id=1, source_target_pairs={{0,1},{1,0},{2,3},{3,2},{4,5},{5,4},{6,7},{7,6},{8,9},{9,8},{10,11... | collective-permute-start | bytes 196616 | tf_op jit(solution)/shard_map/ppermute | solution.py:429

commit v10 on v7

--- a/solution.py
+++ b/solution.py
@@ -340,10 +340,12 @@
     def field(tile):
         return jnp.concatenate([moved_ref[z.place(0, tile * z.chunks + c)] for c in range(z.chunks)], axis=0)
 
-    for tile in range(z.tiles):
+    for tile in range(z.halo):
         turned_ref[tile] = turned(z, field(tile))
     per_tile = LANES // z.blk
     for tile in range(z.tiles):
+        if tile + z.halo < z.tiles:
+            turned_ref[tile + z.halo] = turned(z, field(tile + z.halo))
         mask = keep_ref[tile * per_tile : (tile + 1) * per_tile, :]
         mask = jnp.broadcast_to(mask[:, None, :], (per_tile, z.blk, width)).reshape(LANES, width)
         shallow = over_sources(z, second_ref, field, lambda j: turned_ref[j], tile) * mask

time: 34.4 us -> 34.4 us (level)
  no operation moved by 1% of the time
where the time goes in v10:
time: 34.4 us; the launch traced here: 33.9 us
  starting transfers between devices  14.1 us (41%)
  Pallas kernels  13.7 us (40%)
  waiting for transfers between devices  4.11 us (12%)
  other arithmetic  1.34 us (4%)
  between operations  0.7 us (2%)
    all_to_all x2, starting transfers between devices, exchange(): lax.all_to_all(chunks, 'wide', 0, 0, axis_index_groups=[self.orders[turn]...  13.9 us
    pallas_call x7, Pallas kernels, call(): pl.pallas_call(kernel, out_shape=[space(shape, dtype) for space, (shape,...  13.7 us
    all_to_all x2, waiting for transfers between devices, exchange(): lax.all_to_all(chunks, 'wide', 0, 0, axis_index_groups=[self.orders[turn]...  3.15 us
    add x2, other arithmetic, freq_sum(): total + lax.ppermute(send[shift - 1], 'freq', pairs).astype(jnp.float32)  1.34 us
    ppermute x2, waiting for transfers between devices, freq_sum(): lax.ppermute(send[shift - 1], 'freq', pairs).astype(jnp.float32)  0.96 us
  transfers between devices with their start and end apart: 4, of which 3 were waited for; matrix products, arithmetic and copies ran while one was open for 2% of the time, Pallas kernels for 26%

profile of v10, /device:TPU:0, one launch (start us, length us, event | category | flops | bytes accessed | tf_op | source)
XLA Modules:
  0.0 33.9 jit_solution(1445831543602782382)
XLA Ops:
  0.6 2.8 %first.1 = bf16[16,64,128]{2,1,0:T(8,128)(2,1)} custom-call(bf16[2,64,1024]{2,1,0:T(8,128)(2,1)} %bitcast.11, bf16[2,1,3,2,81]{4,3,2,1,0:T(2,128)(2,1)} %bitcast.18, s32[2,3,2,1024]{3,2,1,0:T(2,128)} %bitcast.12, s32[2,3,2,1024]{3,2,1,0:T(2,128)} %bitcast.15), custom_call_target="tpu_custom_call" | custom-call | flops 603979776 | bytes 1048576 | tf_op jit(solution)/shard_map/first/pallas_call | solution.py:417
  3.4 8.8 %all-to-all-start = ((bf16[16,64,128]{2,1,0:T(8,128)(2,1)}), bf16[16,64,128]{2,1,0:T(8,128)(2,1)S(1)}, u32[]{:S(2)}, u32[]{:S(2)}) async-start(bf16[16,64,128]{2,1,0:T(8,128)(2,1)} %first.1), calls=%async_computation | async-start | bytes 524288 | tf_op jit(solution)/shard_map/all_to_all | solution.py:46
  12.2 4.9 %prepare_middle.1 = (bf16[8,128,768]{2,1,0:T(8,128)(2,1)S(1)}, bf16[8,128,768]{2,1,0:T(8,128)(2,1)S(1)}, f32[64,128]{1,0:T(8,128)S(1)}) custom-call(bf16[2,1,3,2,81]{4,3,2,1,0:T(2,128)(2,1)} %bitcast.19, s32[2,3,2,1024]{3,2,1,0:T(2,128)} %bitcast.13, s32[2,3,2,1024]{3,2,1,0:T(2,128)} %bitcast.16, s32[2,64,64]{2,1,0:T(8,128)} %aperture_hbm.3), custom_call_target="tpu_custom_call" | custom-call | flops 301989888 | bytes 1048576 | tf_op jit(solution)/shard_map/prepare_middle/pallas_call | solution.py:417
  17.1 2.4 %all-to-all-done.moved_ref = bf16[16,64,128]{2,1,0:T(8,128)(2,1)S(1)} async-done(((bf16[16,64,128]{2,1,0:T(8,128)(2,1)}), bf16[16,64,128]{2,1,0:T(8,128)(2,1)S(1)}, u32[]{:S(2)}, u32[]{:S(2)}) %all-to-all-start) | async-done | bytes 262176 | tf_op jit(solution)/shard_map/all_to_all | solution.py:46
  19.4 1.7 %middle.1 = (bf16[16,64,128]{2,1,0:T(8,128)(2,1)}, bf16[1024,128]{1,0:T(8,128)(2,1)}) custom-call(bf16[16,64,128]{2,1,0:T(8,128)(2,1)S(1)} %all-to-all-done.moved_ref, bf16[8,128,768]{2,1,0:T(8,128)(2,1)S(1)} %get-tuple-element.15.second_ref, bf16[8,128,768]{2,1,0:T(8,128)(2,1)S(1)} %get-tuple-element.16.third_ref, f32[64,128]{1,0:T(8,128)S(1)} %get-tuple-element.17.keep_ref), custom_call_target="tpu_custom_call" | custom-call | flops 301989888 | bytes 1048576 | tf_op jit(solution)/shard_map/middle/pallas_call | solution.py:417
  21.1 5.1 %all-to-all-start.1 = ((bf16[16,64,128]{2,1,0:T(8,128)(2,1)}), bf16[16,64,128]{2,1,0:T(8,128)(2,1)S(1)}, u32[]{:S(2)}, u32[]{:S(2)}) async-start(bf16[16,64,128]{2,1,0:T(8,128)(2,1)} %get-tuple-element.18), calls=%async_computation.1 | async-start | bytes 524288 | tf_op jit(solution)/shard_map/all_to_all | solution.py:46
  26.3 1.1 %turn.1 = (bf16[1,64,512]{2,1,0:T(8,128)(2,1)S(1)}, f32[64,512]{1,0:T(8,128)S(1)}) custom-call(bf16[1024,128]{1,0:T(8,128)(2,1)} %get-tuple-element.19.shallow_hbm), custom_call_target="tpu_custom_call" | custom-call | flops 37748736 | bytes 1048576 | tf_op jit(solution)/shard_map/turn/pallas_call | solution.py:417
  27.4 0.1 collective-permute-start
  27.5 2.7 %prepare_last.1 = (bf16[8,768,128]{2,1,0:T(8,128)(2,1)S(1)}, f32[64,1024]{1,0:T(8,128)S(1)}) custom-call(bf16[2,1,3,2,81]{4,3,2,1,0:T(2,128)(2,1)} %bitcast.20, s32[2,3,2,1024]{3,2,1,0:T(2,128)} %bitcast.14, s32[2,3,2,1024]{3,2,1,0:T(2,128)} %bitcast.17, s32[2,64,64]{2,1,0:T(8,128)} %aperture_hbm.3), custom_call_target="tpu_custom_call" | custom-call | flops 301989888 | bytes 1048576 | tf_op jit(solution)/shard_map/prepare_last/pallas_call | solution.py:417
  30.1 0.0 collective-permute-done
  30.2 0.7 %convert_add_fusion.1 = f32[64,512]{1,0:T(8,128)} fusion(f32[64,512]{1,0:T(8,128)S(1)} %get-tuple-element.20, bf16[64,512]{1,0:T(8,128)(2,1)S(1)} %collective-permute-done), kind=kLoop, calls=%fused_computation.1 | loop fusion | flops 65536 | bytes 327680 | tf_op jit(solution)/shard_map/add | solution.py:433
  30.8 0.8 %all-to-all-done.1.field_ref = bf16[16,64,128]{2,1,0:T(8,128)(2,1)S(1)} async-done(((bf16[16,64,128]{2,1,0:T(8,128)(2,1)}), bf16[16,64,128]{2,1,0:T(8,128)(2,1)S(1)}, u32[]{:S(2)}, u32[]{:S(2)}) %all-to-all-start.1) | async-done | bytes 262176 | tf_op jit(solution)/shard_map/all_to_all | solution.py:46
  31.6 0.3 last_send.1
  31.9 0.1 collective-permute-start.1
  32.0 0.3 last_own.1
  32.2 1.0 %collective-permute-done.1 = bf16[64,512]{1,0:T(8,128)(2,1)S(1)} collective-permute-done((bf16[64,512]{1,0:T(8,128)(2,1)S(1)}, bf16[64,512]{1,0:T(8,128)(2,1)S(1)}, u32[]{:S(2)}, u32[]{:S(2)}) %collective-permute-start.1) | collective-permute-done | bytes 65568 | tf_op jit(solution)/shard_map/ppermute | solution.py:433
  33.2 0.7 %convert_add_fusion = f32[64,512]{1,0:T(8,128)} fusion(bf16[64,512]{1,0:T(8,128)(2,1)S(1)} %collective-permute-done.1, bf16[1,64,512]{2,1,0:T(8,128)(2,1)S(1)} %last_own.1), kind=kLoop, calls=%fused_computation | loop fusion | flops 98304 | bytes 262144 | tf_op jit(solution)/shard_map/add | solution.py:433
Async XLA Ops:
  3.4 16.0 %all-to-all-start = ((bf16[16,64,128]{2,1,0:T(8,128)(2,1)}), bf16[16,64,128]{2,1,0:T(8,128)(2,1)S(1)}, u32[]{:S(2)}, u32[]{:S(2)}) async-start(bf16[16,64,128]{2,1,0:T(8,128)(2,1)} %first.1), calls=%async_computation | async-start | bytes 524288 | tf_op jit(solution)/shard_map/all_to_all | solution.py:46
  21.1 10.5 %all-to-all-start.1 = ((bf16[16,64,128]{2,1,0:T(8,128)(2,1)}), bf16[16,64,128]{2,1,0:T(8,128)(2,1)S(1)}, u32[]{:S(2)}, u32[]{:S(2)}) async-start(bf16[16,64,128]{2,1,0:T(8,128)(2,1)} %get-tuple-element.18), calls=%async_computation.1 | async-start | bytes 524288 | tf_op jit(solution)/shard_map/all_to_all | solution.py:46
  27.4 2.8 %collective-permute-start = (bf16[64,512]{1,0:T(8,128)(2,1)S(1)}, bf16[64,512]{1,0:T(8,128)(2,1)S(1)}, u32[]{:S(2)}, u32[]{:S(2)}) collective-permute-start(bf16[64,512]{1,0:T(8,128)(2,1)S(1)} %bitcast.10), channel_id=1, source_target_pairs={{0,1},{1,0},{2,3},{3,2},{4,5},{5,4},{6,7},{7,6},{8,9},{9,8},{10,11... | collective-permute-start | bytes 196616 | tf_op jit(solution)/shard_map/ppermute | solution.py:433
  31.9 1.3 %collective-permute-start.1 = (bf16[64,512]{1,0:T(8,128)(2,1)S(1)}, bf16[64,512]{1,0:T(8,128)(2,1)S(1)}, u32[]{:S(2)}, u32[]{:S(2)}) collective-permute-start(bf16[64,512]{1,0:T(8,128)(2,1)S(1)} %bitcast.9), channel_id=1, source_target_pairs={{0,1},{1,0},{2,3},{3,2},{4,5},{5,4},{6,7},{7,6},{8,9},{9,8},{10,11... | collective-permute-start | bytes 196616 | tf_op jit(solution)/shard_map/ppermute | solution.py:433
